TPU v7x, 128 devices: a whole 4x4x4 slice. The times are simulated.
128 devices in a mesh: ctx: 32 (over y, x, core), head: 4 (over z).
Axes of the slice: x: 4, y: 4, z: 4, core: 2. Of those that a mesh axis runs over, the one named last changes fastest.
Arguments:
- query_rows: bfloat16 [16384, 8192], P('ctx', 'head'), may hold values from -6 to 6
- key_rows: bfloat16 [16384, 8192], P('ctx', 'head'), may hold values from -6 to 6
- value_rows: bfloat16 [16384, 8192], P('ctx', 'head'), may hold values from -6 to 6
- out_grad: bfloat16 [16384, 8192], P('ctx', 'head'), may hold values from -6 to 6
- norm_gain: float32 [8192], P('head'), may hold values from 0.5 to 1.5
Outputs:
- query_grad: bfloat16 [16384, 8192], P('ctx', 'head')
- key_grad: bfloat16 [16384, 8192], P('ctx', 'head')
- value_grad: bfloat16 [16384, 8192], P('ctx', 'head')
All inputs are finite; a program needn't handle non-finite values.
Results may differ from a plain program's by a relative error of at most 0.0059.
Values sent between devices are 32-bit elements; how exact they have to be, the bound alone decides.
No kernel may reach another device: no remote copies, remote signals or barrier semaphores. Data moves between devices by JAX's collectives and lax.ppermute only.
A program may use at most 192 MiB of HBM per device.

v0:
```python
import jax
import jax.numpy as jnp
from jax import lax
from jax.sharding import PartitionSpec as P

DH = 128


epsilon = 1e-06


def entering(part, axis, combine, identity, reverse):
    count = lax.axis_size(axis)
    place = lax.axis_index(axis)
    ahead = count - 1 - place if reverse else place
    gathered = lax.all_gather(part, axis)
    state = jnp.zeros_like(part) + jnp.asarray(identity, part.dtype)

    def one(hop, state):
        source = count - 1 - hop if reverse else hop
        return combine(state, lax.dynamic_index_in_dim(gathered, source, 0, False))

    return lax.fori_loop(0, ahead, one, state)


def causal_mask(count):
    places = lax.broadcasted_iota(jnp.int32, (count, count), 0)
    others = lax.broadcasted_iota(jnp.int32, (count, count), 1)
    return others <= places


def add_states(earlier, later):
    return earlier + later


def local(query_rows, key_rows, value_rows, out_grad, norm_gain):
    length, width = query_rows.shape
    groups = width // DH
    query_data = query_rows.reshape(length, groups, DH)
    key_data = key_rows.reshape(length, groups, DH)
    value_data = value_rows.reshape(length, groups, DH)
    causal = causal_mask(length)[None]
    local_state = jnp.einsum(
        "thi,thj->hij", key_data, value_data, preferred_element_type=jnp.float32
    )
    zero_state = jnp.zeros_like(local_state)
    prefix = entering(local_state, "ctx", add_states, zero_state, False)
    prefix_half = prefix.astype(jnp.bfloat16)
    scores = jnp.einsum("thi,shi->hts", query_data, key_data, preferred_element_type=jnp.float32)
    score_half = jnp.where(causal, scores, 0.0).astype(jnp.bfloat16)
    output = jnp.einsum("hts,shj->thj", score_half, value_data, preferred_element_type=jnp.float32)
    output = output + jnp.einsum(
        "thi,hij->thj", query_data, prefix_half, preferred_element_type=jnp.float32
    )
    gain_data = norm_gain.reshape(groups, DH)
    scaled = out_grad.reshape(length, groups, DH).astype(jnp.float32) * gain_data
    squares = jnp.sum(output * output, axis=(1, 2))
    products = jnp.sum(scaled * output, axis=(1, 2))
    squares, products = lax.psum((squares, products), "head")
    width_all = width * lax.axis_size("head")
    radius = jnp.sqrt(squares / width_all + epsilon)
    coeff = products / (width_all * radius * radius)
    grad_out = ((scaled - output * coeff[:, None, None]) / radius[:, None, None]).astype(
        jnp.bfloat16
    )
    local_grad = jnp.einsum(
        "thi,thj->hij", query_data, grad_out, preferred_element_type=jnp.float32
    )
    later = entering(local_grad, "ctx", add_states, zero_state, True)
    later_half = later.astype(jnp.bfloat16)
    mixing = jnp.einsum("thj,shj->hts", grad_out, value_data, preferred_element_type=jnp.float32)
    mixing = jnp.where(causal, mixing, 0.0).astype(jnp.bfloat16)
    query_grad = jnp.einsum("hts,shi->thi", mixing, key_data, preferred_element_type=jnp.float32)
    query_grad = query_grad + jnp.einsum(
        "thj,hij->thi", grad_out, prefix_half, preferred_element_type=jnp.float32
    )
    key_grad = jnp.einsum("hts,thi->shi", mixing, query_data, preferred_element_type=jnp.float32)
    key_grad = key_grad + jnp.einsum(
        "shj,hij->shi", value_data, later_half, preferred_element_type=jnp.float32
    )
    value_grad = jnp.einsum(
        "hts,thj->shj", score_half, grad_out, preferred_element_type=jnp.float32
    )
    value_grad = value_grad + jnp.einsum(
        "shi,hij->shj", key_data, later_half, preferred_element_type=jnp.float32
    )
    return (
        query_grad.reshape(length, width).astype(jnp.bfloat16),
        key_grad.reshape(length, width).astype(jnp.bfloat16),
        value_grad.reshape(length, width).astype(jnp.bfloat16),
    )


def solution(mesh):
    in_specs = (P("ctx", "head"), P("ctx", "head"), P("ctx", "head"), P("ctx", "head"), P("head"))
    out_specs = (P("ctx", "head"), P("ctx", "head"), P("ctx", "head"))
    return jax.shard_map(local, mesh=mesh, in_specs=in_specs, out_specs=out_specs, check_vma=False)
```

profile of v0, /device:TPU:1, one launch (start us, length us, event | category | flops | bytes accessed | tf_op | source)
XLA Modules:
  0.0 392.3 jit_solution(5105326178334288420)
XLA Ops:
  7.2 0.0 all-gather.5.cloned.1.call-start
  7.2 3.7 copy.57
  10.9 4.3 %copy.33 = bf16[512,16,128]{0,2,1:T(8,128)(2,1)} copy(bf16[512,16,128]{2,1,0:T(8,128)(2,1)} %bitcast.109) | data formatting | bytes 4194304 | tf_op jit(solution)/shard_map/reshape | solution.py:40
  15.2 3.9 fusion.7
  19.1 0.0 all-gather.5.cloned.1.call-update
  19.1 0.0 all-gather.7.cloned.1.call-start
  19.2 4.2 %copy.29 = f32[512,2048]{0,1:T(8,128)} copy(bf16[512,2048]{1,0:T(8,128)(2,1)} %param.12) | data formatting | bytes 6291456 | tf_op jit(solution)/shard_map/convert_element_type | solution.py:56
  23.4 0.1 iota_compare_fusion
  23.5 4.1 %select_convert_fusion.1 = bf16[16,512,512]{2,1,0:T(8,128)(2,1)S(1)} fusion(pred[512,512]{1,0:T(8,128)(4,1)S(1)} %iota_compare_fusion, bf16[512,2048]{1,0:T(8,128)(2,1)} %param.10, bf16[512,2048]{1,0:T(8,128)(2,1)S(1)} %copy-done), kind=kOutput, calls=%fused_computation.3 | convolution fusion | flops 1082130432 | bytes 12845056 | tf_op jit(solution)/shard_map/thi,shi->hts/dot_general | solution.py:49
  27.6 3.2 copy-done.1
  30.8 4.8 %fusion.2 = f32[16,512,128]{1,2,0:T(8,128)} fusion(bf16[16,512,512]{2,1,0:T(8,128)(2,1)S(1)} %select_convert_fusion.1, bf16[512,2048]{1,0:T(8,128)(2,1)S(1)} %copy-done.6), kind=kOutput, calls=%fused_computation.13 | convolution fusion | flops 1073741824 | bytes 14680064 | tf_op jit(solution)/shard_map/hts,shj->thj/dot_general | solution.py:51
  35.7 100.9 %all-gather.5.cloned.1.call-done = f32[512,128,128]{2,1,0:T(8,128)} async-done(((f32[16,128,128]{2,1,0:T(8,128)}), f32[512,128,128]{2,1,0:T(8,128)}) %all-gather.5.cloned.1.call-update) | async-done | bytes 33554448 | tf_op jit(solution)/shard_map/all_gather | solution.py:16
  136.6 0.1 broadcast_in_dim.26.clone
  136.7 1.5 while.22
  136.7 1.5 bitcast_add_fusion.7
  138.2 5.5 %multiply_reduce_fusion.1 = (f32[512]{0:T(512)S(1)}, f32[512]{0:T(512)S(1)}, f32[512,16,128]{0,2,1:T(8,128)}) fusion(f32[512,2048]{0,1:T(8,128)} %copy.29, f32[16,128]{1,0:T(8,128)S(1)} %bitcast.116, f32[16,128,128]{2,1,0:T(8,128)S(1)} %get-tuple-element.82, f32[16,512,128]{1,2,0:T(8,128)} %fusion.2, bf16[512,2048]{1,0:T(8,128)(2,1)S(1)} %copy-done), kind=kOutput, calls=%fused_computation.12 | convolution fusion | flops 274988032 | bytes 15740928 | tf_op jit(solution)/shard_map/thi,hij->thj/dot_general | solution.py:52
  143.8 9.0 %all-reduce = (f32[512]{0:T(512)S(1)}, f32[512]{0:T(512)S(1)}) all-reduce(f32[512]{0:T(512)S(1)} %get-tuple-element.95, f32[512]{0:T(512)S(1)} %get-tuple-element.94), channel_id=1, replica_groups=mesh['ctx'=32,'head'=4] {'head'}, use_global_device_ids=true, to_apply=%region_5.6 | all-reduce | flops 1024 | bytes 8192 | tf_op jit(solution)/shard_map/psum | solution.py:59
  152.7 3.9 divide_convert_fusion
  156.6 1.3 copy-done.2
  157.9 1.7 fusion.18
  159.7 2.6 copy.43
  162.3 4.9 %select_convert_fusion = bf16[16,512,512]{2,1,0:T(8,128)(2,1)S(1)} fusion(bf16[512,16,128]{0,2,1:T(8,128)(2,1)} %copy-done.2, pred[512,512]{1,0:T(8,128)(4,1)S(1)} %iota_compare_fusion, bf16[512,2048]{1,0:T(8,128)(2,1)} %param.11), kind=kOutput, calls=%fused_computation.2 | convolution fusion | flops 1082130432 | bytes 12845056 | tf_op jit(solution)/shard_map/thj,shj->hts/dot_general | solution.py:71
  167.2 4.9 %fusion.34 = f32[16,512,128]{1,2,0:T(8,128)} fusion(bf16[16,512,512]{2,1,0:T(8,128)(2,1)S(1)} %select_convert_fusion, bf16[512,16,128]{0,2,1:T(8,128)(2,1)S(1)} %copy-done.7), kind=kOutput, calls=%fused_computation.46 | convolution fusion | flops 1073741824 | bytes 14680064 | tf_op jit(solution)/shard_map/hts,shi->thi/dot_general | solution.py:73
  172.1 4.3 %fusion.1 = bf16[512,16,128]{0,2,1:T(8,128)(2,1)} fusion(f32[16,512,128]{1,2,0:T(8,128)} %fusion.34, bf16[512,16,128]{0,2,1:T(8,128)(2,1)S(1)} %copy-done.3, f32[16,128,128]{2,1,0:T(8,128)S(1)} %get-tuple-element.82), kind=kOutput, calls=%fused_computation.7 | convolution fusion | flops 270794752 | bytes 9437184 | tf_op jit(solution)/shard_map/thj,hij->thi/dot_general | solution.py:74
  176.3 3.9 copy.47
  180.2 7.3 %fusion.35 = f32[16,128,512]{2,1,0:T(8,128)} fusion(bf16[512,16,128]{0,2,1:T(8,128)(2,1)} %copy-done.2, bf16[16,512,512]{2,1,0:T(8,128)(2,1)} %copy-done.1), kind=kOutput, calls=%fused_computation.47 | convolution fusion | flops 1073741824 | bytes 14680064 | tf_op jit(solution)/shard_map/hts,thj->shj/dot_general | solution.py:81
  187.6 130.7 %all-gather.7.cloned.1.call-done = f32[512,128,128]{2,1,0:T(8,128)} async-done(((f32[16,128,128]{2,1,0:T(8,128)}), f32[512,128,128]{2,1,0:T(8,128)}) %all-gather.7.cloned.1.call-update) | async-done | bytes 33554448 | tf_op jit(solution)/shard_map/all_gather | solution.py:16
  318.2 0.1 broadcast_in_dim.26
  318.3 45.4 %while.23 = (s32[]{:T(128)}, f32[16,128,128]{2,1,0:T(8,128)S(1)}, s32[]{:T(128)}, f32[32,16,128,128]{3,2,1,0:T(8,128)}, s32[]{:T(128)}, /*index=5*/s32[]{:T(128)}, s32[]{:T(128)}, s32[]{:T(128)}) while((s32[]{:T(128)}, f32[16,128,128]{2,1,0:T(8,128)S(1)}, s32[]{:T(128)}, f32[32,16,128,128]{3,2,1,0:T(8,128)}, s32[]{:T(128)}, ...), condition=%wide.region_7.8_spmd, body=%wide.region_6.7_spmd.sunk | while | flops 262150 | bytes 3145871 | solution.py:23
  318.4 1.5 bitcast_add_fusion.8
  319.9 1.5 bitcast_add_fusion.8
  321.4 1.5 bitcast_add_fusion.8
  322.9 1.5 bitcast_add_fusion.8
  324.4 1.5 bitcast_add_fusion.8
  325.9 1.5 bitcast_add_fusion.8
  327.4 1.5 bitcast_add_fusion.8
  328.9 1.5 bitcast_add_fusion.8
  330.4 1.5 bitcast_add_fusion.8
  332.0 1.5 bitcast_add_fusion.8
  333.5 1.5 bitcast_add_fusion.8
  335.0 1.5 bitcast_add_fusion.8
  336.5 1.5 bitcast_add_fusion.8
  338.0 1.5 bitcast_add_fusion.8
  339.5 1.5 bitcast_add_fusion.8
  341.0 1.5 bitcast_add_fusion.8
  342.5 1.5 bitcast_add_fusion.8
  344.1 1.5 bitcast_add_fusion.8
  345.6 1.5 bitcast_add_fusion.8
  347.1 1.5 bitcast_add_fusion.8
  348.6 1.5 bitcast_add_fusion.8
  350.1 1.5 bitcast_add_fusion.8
  351.6 1.5 bitcast_add_fusion.8
  353.1 1.5 bitcast_add_fusion.8
  354.6 1.5 bitcast_add_fusion.8
  356.1 1.5 bitcast_add_fusion.8
  357.7 1.5 bitcast_add_fusion.8
  359.2 1.5 bitcast_add_fusion.8
  360.7 1.5 bitcast_add_fusion.8
  362.2 1.5 bitcast_add_fusion.8
  363.7 4.4 %fusion.4 = f32[16,128,512]{2,1,0:T(8,128)} fusion(f32[16,128,128]{2,1,0:T(8,128)S(1)} %get-tuple-element.83, bf16[512,2048]{1,0:T(8,128)(2,1)} %param.11), kind=kOutput, calls=%fused_computation.15 | convolution fusion | flops 268697600 | bytes 7340032 | tf_op jit(solution)/shard_map/shj,hij->shi/dot_general | solution.py:78
  368.1 2.2 add_convert_fusion
  370.3 3.9 copy.49
  374.2 7.3 %fusion = bf16[512,16,128]{0,2,1:T(8,128)(2,1)} fusion(f32[16,128,512]{2,1,0:T(8,128)} %fusion.4, bf16[16,512,512]{2,1,0:T(8,128)(2,1)} %copy-done.4, bf16[512,2048]{1,0:T(8,128)(2,1)S(1)} %copy-done), kind=kOutput, calls=%fused_computation.5 | convolution fusion | flops 1075838976 | bytes 16777216 | tf_op jit(solution)/shard_map/hts,thi->shi/dot_general | solution.py:77
  381.6 3.9 copy.48
  (20 shorter events, 0.1 us)
Async XLA Ops:
  7.2 16.3 %copy-start = (bf16[512,2048]{1,0:T(8,128)(2,1)S(1)}, bf16[512,2048]{1,0:T(8,128)(2,1)}, u32[]{:S(2)}) copy-start(bf16[512,2048]{1,0:T(8,128)(2,1)} %param.9) | copy-start | bytes 6291460
  7.2 129.4 %all-gather.5.cloned.1.call-start = ((), (), s32[]{:S(2)}) async-start(), calls=%async_computation | async-start | bytes 34603008 | tf_op jit(solution)/shard_map/all_gather | solution.py:16
  19.1 299.1 %all-gather.7.cloned.1.call-start = ((), (), s32[]{:S(2)}) async-start(), calls=%async_computation.1 | async-start | bytes 34603008 | tf_op jit(solution)/shard_map/all_gather | solution.py:16
  23.5 7.4 %copy-start.6 = (bf16[512,2048]{1,0:T(8,128)(2,1)S(1)}, bf16[512,2048]{1,0:T(8,128)(2,1)}, u32[]{:S(2)}) copy-start(bf16[512,2048]{1,0:T(8,128)(2,1)} %param.11) | copy-start | bytes 6291460
  27.6 3.2 copy-start.1
  136.7 1.5 copy-start.9
  156.6 1.3 copy-start.2
  162.3 4.9 %copy-start.7 = (bf16[512,16,128]{0,2,1:T(8,128)(2,1)S(1)}, bf16[512,16,128]{0,2,1:T(8,128)(2,1)}, u32[]{:S(2)}) copy-start(bf16[512,16,128]{0,2,1:T(8,128)(2,1)} %copy.33) | copy-start | bytes 6291460
  167.1 4.9 %copy-start.4 = (bf16[16,512,512]{2,1,0:T(8,128)(2,1)}, bf16[16,512,512]{2,1,0:T(8,128)(2,1)S(1)}, u32[]{:S(2)}) copy-start(bf16[16,512,512]{2,1,0:T(8,128)(2,1)S(1)} %select_convert_fusion) | copy-start | bytes 25165828
  167.2 4.9 %copy-start.3 = (bf16[512,16,128]{0,2,1:T(8,128)(2,1)S(1)}, bf16[512,16,128]{0,2,1:T(8,128)(2,1)}, u32[]{:S(2)}) copy-start(bf16[512,16,128]{0,2,1:T(8,128)(2,1)} %copy-done.2) | copy-start | bytes 6291460
  363.7 4.4 %copy-start.5 = (f32[16,128,512]{2,1,0:T(8,128)S(1)}, f32[16,128,512]{2,1,0:T(8,128)}, u32[]{:S(2)}) copy-start(f32[16,128,512]{2,1,0:T(8,128)} %fusion.35) | copy-start | bytes 12582916
  363.7 4.4 %copy-start.8 = (bf16[512,2048]{1,0:T(8,128)(2,1)S(1)}, bf16[512,2048]{1,0:T(8,128)(2,1)}, u32[]{:S(2)}) copy-start(bf16[512,2048]{1,0:T(8,128)(2,1)} %param.10) | copy-start | bytes 6291460
Sparse Core Ops, SparseCore 0:
  19.2 117.3 all-gather.4
  162.4 155.8 all-gather.6
where the time goes:
time: 394 us; the launch traced here: 392 us
  waiting for transfers between devices  232 us (59%)
  matrix products  55.4 us (14%)
  other arithmetic  50.1 us (13%)
  local copies, waits for them, and re-layouts  31.2 us (8%)
  between operations  14.2 us (4%)
  blocking collectives  8.96 us (2%)
    all_gather x2, waiting for transfers between devices, entering(): gathered = lax.all_gather(part, axis)  232 us
    add x31, other arithmetic, add_states(): return earlier + later  46.2 us
    unnamed x24, local copies, waits for them, and re-layouts  20 us
    psum x1, blocking collectives, local(): squares, products = lax.psum((squares, products), 'head')  8.96 us
  transfers between devices with their start and end apart: 2, of which 2 were waited for; matrix products, arithmetic and copies ran while one was open for 10% of the time, Pallas kernels for 0%

commit v1 on v0

v1 whole, which is shorter than its diff:
```python
import functools

import jax
import jax.numpy as jnp
from jax import lax
from jax.experimental import pallas as pl
from jax.experimental.pallas import tpu as pltpu
from jax.sharding import PartitionSpec as P

DH = 128
BLOCK = 512
HALF = 256
HEADS_LOCAL = 16
WIDTH = HEADS_LOCAL * DH
WIDTH_ALL = 8192
PAIRS = HEADS_LOCAL // 2
SIDE = PAIRS // 2
ROWS = HEADS_LOCAL * DH // 2
CHIPS = 16
SLICE = ROWS // CHIPS
LIMIT = 24 * 1024 * 1024

epsilon = 1e-06

F32 = jnp.float32
BF16 = jnp.bfloat16


def dot(a, b):
    return lax.dot_general(a, b, (((1,), (0,)), ((), ())), preferred_element_type=F32)


def dot_nt(a, b):
    return lax.dot_general(a, b, (((1,), (1,)), ((), ())), preferred_element_type=F32)


def dot_tn(a, b):
    return lax.dot_general(a, b, (((0,), (0,)), ((), ())), preferred_element_type=F32)


def columns(step, core):
    return (0, jnp.bitwise_xor(core[0], step // SIDE) * SIDE + step % SIDE)


def token_spec():
    return pl.BlockSpec((BLOCK, 2 * DH), columns)


def state_spec():
    return pl.BlockSpec((1, 2 * DH, DH), lambda step, core: (step // SIDE, step % SIDE, 0))


def half_spec(which):
    def place(step, core):
        if which == 0:
            return (jnp.minimum(step, SIDE - 1), 0)
        return (jnp.maximum(step - SIDE, 0), 0)

    return pl.BlockSpec((2 * DH, DH), place)


def call(body, in_specs, out_specs, out_shape, flops, bytes_accessed, scratch=()):
    return pl.pallas_call(
        body,
        grid_spec=pltpu.PrefetchScalarGridSpec(
            num_scalar_prefetch=1,
            grid=(PAIRS,),
            in_specs=in_specs,
            out_specs=out_specs,
            scratch_shapes=list(scratch),
        ),
        out_shape=out_shape,
        compiler_params=pltpu.CompilerParams(
            vmem_limit_bytes=LIMIT, dimension_semantics=("arbitrary",)
        ),
        cost_estimate=pl.CostEstimate(
            flops=flops, bytes_accessed=bytes_accessed, transcendentals=0
        ),
    )


def shape(dims, kind):
    return jax.ShapeDtypeStruct(dims, kind)


MIB = 1024 * 1024
STATES = shape((2, ROWS, DH), F32)
TOKENS_F32 = shape((BLOCK, WIDTH), F32)
TOKENS_BF16 = shape((BLOCK, WIDTH), BF16)


def store_states(out, a, b):
    both = dot_tn(a, b)
    out[0, :DH, :] = both[:DH, :DH]
    out[0, DH:, :] = both[DH:, DH:]


def local_state_body(core, k, v, out):
    store_states(out, k[...], v[...])


def lower(array):
    rows = lax.broadcasted_iota(jnp.int32, array.shape, 0) + (array.shape[1] - array.shape[0])
    cols = lax.broadcasted_iota(jnp.int32, array.shape, 1)
    return jnp.where(cols <= rows, array, 0.0).astype(BF16)


def upper(array):
    rows = lax.broadcasted_iota(jnp.int32, array.shape, 0)
    cols = lax.broadcasted_iota(jnp.int32, array.shape, 1)
    return jnp.where(cols >= rows, array, 0.0).astype(BF16)


def intra_body(core, q, k, v, out):
    for h in range(2):
        cols = slice(h * DH, (h + 1) * DH)
        keys, values = k[:, cols], v[:, cols]
        top = lower(dot_nt(q[:HALF, cols], keys[:HALF]))
        out[:HALF, cols] = dot(top, values[:HALF])
        bottom = lower(dot_nt(q[HALF:, cols], keys))
        out[HALF:, cols] = dot(bottom, values)


def gather_state(core, base_own, base_other, side_own, side_other, weight):
    step = pl.program_id(0)
    own = base_own[...] + weight * side_own[...]
    other = base_other[...] + weight * side_other[...]
    return jnp.where(step < SIDE, own, other).astype(BF16)


def output_body(
    core, q, intra, out_grad, gain, base_own, base_other, side_own, side_other,
    output, prefix_half, stats, square_acc, product_acc,
):
    step = pl.program_id(0)

    @pl.when(step == 0)
    def _():
        square_acc[...] = jnp.zeros_like(square_acc)
        product_acc[...] = jnp.zeros_like(product_acc)

    weight = core[0].astype(F32)
    prefix = gather_state(core, base_own, base_other, side_own, side_other, weight)
    prefix_half[0] = prefix
    for h in range(2):
        cols = slice(h * DH, (h + 1) * DH)
        value = intra[:, cols] + dot(q[:, cols], prefix[cols, :])
        output[:, cols] = value
        scaled = out_grad[:, cols].astype(F32) * gain[:, cols]
        square_acc[...] += value * value
        product_acc[...] += scaled * value

    @pl.when(step == PAIRS - 1)
    def _():
        stats[0:1, :] = jnp.sum(square_acc[...].T, axis=0, keepdims=True)
        stats[1:2, :] = jnp.sum(product_acc[...].T, axis=0, keepdims=True)


def grad_body(core, q, output, out_grad, gain, s0, s1, s2, s3, grad_out, states, inverse, coeff):
    @pl.when(pl.program_id(0) == 0)
    def _():
        total = (s0[...] + s1[...]) + (s2[...] + s3[...])
        radius = jnp.sqrt(total[0:1, :] / WIDTH_ALL + epsilon)
        scale = total[1:2, :] / (WIDTH_ALL * radius * radius)
        inverse[...] = jnp.broadcast_to(1.0 / radius, (DH, BLOCK)).T
        coeff[...] = jnp.broadcast_to(scale, (DH, BLOCK)).T

    for h in range(2):
        cols = slice(h * DH, (h + 1) * DH)
        scaled = out_grad[:, cols].astype(F32) * gain[:, cols]
        grad = (scaled - output[:, cols] * coeff[...]) * inverse[...]
        grad_out[:, cols] = grad.astype(BF16)
    store_states(states, q[...], grad_out[...])


def middle_body(core, q, k, v, g, prefix_half, query_grad, key_part, value_part):
    for h in range(2):
        cols = slice(h * DH, (h + 1) * DH)
        queries, keys, values, grads = q[:, cols], k[:, cols], v[:, cols], g[:, cols]
        prefix = prefix_half[0, cols, :]
        for rows, seen in ((slice(0, HALF), slice(0, HALF)), (slice(HALF, BLOCK), slice(0, BLOCK))):
            mixing = lower(dot_nt(grads[rows], values[seen]))
            total = dot(mixing, keys[seen]) + dot_nt(grads[rows], prefix)
            query_grad[rows, cols] = total.astype(BF16)
        for rows, seen in ((slice(0, HALF), slice(0, BLOCK)), (slice(HALF, BLOCK), slice(HALF, BLOCK))):
            mixing = upper(dot_nt(values[rows], grads[seen]))
            key_part[rows, cols] = dot(mixing, queries[seen])
            scores = upper(dot_nt(keys[rows], queries[seen]))
            value_part[rows, cols] = dot(scores, grads[seen])


def last_body(
    core, k, v, key_part, value_part, base_own, base_other, side_own, side_other,
    key_grad, value_grad,
):
    weight = 1.0 - core[0].astype(F32)
    later = gather_state(core, base_own, base_other, side_own, side_other, weight)
    for h in range(2):
        cols = slice(h * DH, (h + 1) * DH)
        key_grad[:, cols] = (key_part[:, cols] + dot_nt(v[:, cols], later[cols, :])).astype(BF16)
        value_grad[:, cols] = (value_part[:, cols] + dot(k[:, cols], later[cols, :])).astype(BF16)


def scan_body(reverse, parts, out):
    state = jnp.zeros((SLICE, DH), F32)
    order = range(CHIPS - 1, -1, -1) if reverse else range(CHIPS)
    for place in order:
        out[place] = state
        state = state + parts[place]


def chip_scan(parts, reverse):
    return pl.pallas_call(
        functools.partial(scan_body, reverse),
        out_shape=shape((CHIPS, SLICE, DH), F32),
        compiler_params=pltpu.CompilerParams(vmem_limit_bytes=LIMIT),
        cost_estimate=pl.CostEstimate(flops=MIB, bytes_accessed=MIB, transcendentals=0),
    )(parts)


PARTNERS = [(i, i ^ 1) for i in range(2 * CHIPS)]
SAME_CORE = [[core + 2 * chip for chip in range(CHIPS)] for core in range(2)]


def exchange(parts):
    return lax.all_to_all(parts, "ctx", 0, 0, axis_index_groups=SAME_CORE, tiled=True)


def swap(part):
    return lax.ppermute(part, "ctx", PARTNERS)


def entering(states, reverse):
    own, other = states[0], states[1]
    side_own = swap(other)
    side_other = swap(own)
    chip = (own + side_own).reshape(CHIPS, SLICE, DH)
    base_own = exchange(chip_scan(exchange(chip), reverse)).reshape(ROWS, DH)
    base_other = swap(base_own)
    return base_own, base_other, side_own, side_other


def local(query_rows, key_rows, value_rows, out_grad, norm_gain):
    core = (lax.axis_index("ctx") % 2).astype(jnp.int32).reshape(1)
    gain = norm_gain.reshape(1, WIDTH)
    token, state = token_spec(), state_spec()
    halves = [half_spec(0), half_spec(1), half_spec(0), half_spec(1)]
    gain_spec = pl.BlockSpec((1, 2 * DH), columns)
    stats_spec = pl.BlockSpec((2, BLOCK), lambda step, core: (0, 0))
    lanes = pltpu.VMEM((BLOCK, DH), F32)
    stats_shape = shape((2, BLOCK), F32)

    states = call(
        local_state_body, [token, token], state, STATES, 2 * BLOCK * WIDTH * DH * 2, 5 * MIB
    )(core, key_rows, value_rows)
    bases = entering(states, False)
    intra = call(
        intra_body, [token] * 3, token, TOKENS_F32, 6 * BLOCK * BLOCK * WIDTH, 10 * MIB
    )(core, query_rows, key_rows, value_rows)
    output, prefix_half, stats = call(
        output_body,
        [token, token, token, gain_spec] + halves,
        [token, state, stats_spec],
        [TOKENS_F32, shape((2, ROWS, DH), BF16), stats_shape],
        2 * BLOCK * WIDTH * DH,
        14 * MIB,
        (lanes, lanes),
    )(core, query_rows, intra, out_grad, gain, *bases)
    others = [
        lax.ppermute(stats, "head", [(i, (i + hop) % 4) for i in range(4)]) for hop in (1, 2, 3)
    ]
    grad_out, grad_states = call(
        grad_body,
        [token, token, token, gain_spec] + [stats_spec] * 4,
        [token, state],
        [TOKENS_BF16, STATES],
        4 * BLOCK * WIDTH * DH,
        11 * MIB,
        (lanes, lanes),
    )(core, query_rows, output, out_grad, gain, stats, *others)
    laters = entering(grad_states, True)
    query_grad, key_part, value_part = call(
        middle_body,
        [token] * 4 + [state],
        [token] * 3,
        [TOKENS_BF16, TOKENS_F32, TOKENS_F32],
        10 * BLOCK * BLOCK * WIDTH,
        18 * MIB,
    )(core, query_rows, key_rows, value_rows, grad_out, prefix_half)
    key_grad, value_grad = call(
        last_body,
        [token] * 4 + halves,
        [token, token],
        [TOKENS_BF16, TOKENS_BF16],
        4 * BLOCK * WIDTH * DH,
        18 * MIB,
    )(core, key_rows, value_rows, key_part, value_part, *laters)
    return query_grad, key_grad, value_grad


def solution(mesh):
    in_specs = (P("ctx", "head"), P("ctx", "head"), P("ctx", "head"), P("ctx", "head"), P("head"))
    out_specs = (P("ctx", "head"), P("ctx", "head"), P("ctx", "head"))
    return jax.shard_map(local, mesh=mesh, in_specs=in_specs, out_specs=out_specs, check_vma=False)
```

time: 394 us -> 141 us (0.36)
  waiting for transfers between devices: 232 us -> 22.6 us
  matrix products: 55.4 us -> 0 us
  other arithmetic: 50.1 us -> 0.11 us
  Pallas kernels: 0 us -> 46.8 us
  starting transfers between devices: 0.08 us -> 23.4 us
  blocking collectives: 8.96 us -> 30.7 us
  local copies, waits for them, and re-layouts: 31.2 us -> 15.7 us
  between operations: 14.2 us -> 0.8 us
    all_gather x2 -> x0, waiting for transfers between devices: 232 us -> none  [entering(): gathered = lax.all_gather(part, axis)]
    dot_general x12 -> x0, matrix products: 55.4 us -> none  [the longest x1 7.34 us: local(): jnp.einsum('hts,thj->shj', score_half, grad_out, preferred_element_type=j...]
    pallas_call x0 -> x8, Pallas kernels: none -> 46.8 us  [the longest x1 17.4 us: local(): call(middle_body, [token] * 4 + [state], [token] * 3, [TOKENS_BF16, TOKEN...]
    add x31 -> x2, other arithmetic: 46.2 us -> 0.11 us  [entering(): chip = (own + side_own).reshape(CHIPS, SLICE, DH)]
    all_to_all x0 -> x2, blocking collectives: none -> 30.7 us  [exchange(): lax.all_to_all(parts, 'ctx', 0, 0, axis_index_groups=SAME_CORE, tiled=True)]
    ppermute x0 -> x9, starting transfers between devices: none -> 16.3 us  [the longest x6 11.8 us: swap(): return lax.ppermute(part, 'ctx', PARTNERS)]
    all_to_all x0 -> x2, waiting for transfers between devices: none -> 16.2 us  [exchange(): lax.all_to_all(parts, 'ctx', 0, 0, axis_index_groups=SAME_CORE, tiled=True)]
    psum x1 -> x0, blocking collectives: 8.96 us -> none  [local(): squares, products = lax.psum((squares, products), 'head')]
  transfers between devices with their start and end apart: 2 -> 11, of which waited for: 2 -> 6; matrix products, arithmetic and copies ran while one was open for 10% -> 0% of each run, Pallas kernels for 0% -> 19%
where the time goes in v1:
time: 141 us; the launch traced here: 140 us
  Pallas kernels  46.8 us (33%)
  blocking collectives  30.7 us (22%)
  starting transfers between devices  23.4 us (17%)
  waiting for transfers between devices  22.6 us (16%)
  local copies, waits for them, and re-layouts  15.7 us (11%)
    all_to_all x2, blocking collectives, exchange(): lax.all_to_all(parts, 'ctx', 0, 0, axis_index_groups=SAME_CORE, tiled=True)  30.7 us
    pallas_call x1, Pallas kernels, local(): call(middle_body, [token] * 4 + [state], [token] * 3, [TOKENS_BF16, TOKEN...  17.4 us
    all_to_all x2, waiting for transfers between devices, exchange(): lax.all_to_all(parts, 'ctx', 0, 0, axis_index_groups=SAME_CORE, tiled=True)  16.2 us
    unnamed x30, local copies, waits for them, and re-layouts  13.8 us
    ppermute x6, starting transfers between devices, swap(): return lax.ppermute(part, 'ctx', PARTNERS)  11.8 us
    pallas_call x1, Pallas kernels, local(): call(intra_body, [token] * 3, token, TOKENS_F32, 6 * BLOCK * BLOCK * WIDT...  8.81 us
    all_to_all x2, starting transfers between devices, exchange(): lax.all_to_all(parts, 'ctx', 0, 0, axis_index_groups=SAME_CORE, tiled=True)  7.15 us
    pallas_call x1, Pallas kernels, local(): call(last_body, [token] * 4 + halves, [token, token], [TOKENS_BF16, TOKEN...  7.01 us
  transfers between devices with their start and end apart: 11, of which 6 were waited for; matrix products, arithmetic and copies ran while one was open for 0% of the time, Pallas kernels for 19%

profile of v1, /device:TPU:1, one launch (start us, length us, event | category | flops | bytes accessed | tf_op | source)
XLA Modules:
  0.0 140.1 jit_solution(8901936544968202013)
XLA Ops:
  0.6 0.0 copy-start.2
  0.7 1.6 %copy-done.2 = bf16[512,2048]{1,0:T(8,128)(2,1)S(1)} copy-done((bf16[512,2048]{1,0:T(8,128)(2,1)S(1)}, bf16[512,2048]{1,0:T(8,128)(2,1)}, u32[]{:S(2)}) %copy-start.2) | copy-done | bytes 2097176
  2.2 0.0 copy-start.5
  2.2 1.6 %copy-done.5 = bf16[512,2048]{1,0:T(8,128)(2,1)S(1)} copy-done((bf16[512,2048]{1,0:T(8,128)(2,1)S(1)}, bf16[512,2048]{1,0:T(8,128)(2,1)}, u32[]{:S(2)}) %copy-start.5) | copy-done | bytes 2097176
  3.8 3.0 %shard_map.77 = f32[2,1024,128]{2,1,0:T(8,128)S(1)} custom-call(s32[1]{0:T(128)} %bitcast.core, bf16[512,2048]{1,0:T(8,128)(2,1)S(1)} %copy-done.2, bf16[512,2048]{1,0:T(8,128)(2,1)S(1)} %copy-done.5), custom_call_target="tpu_custom_call" | custom-call | flops 536870912 | bytes 5242880 | tf_op jit(solution)/shard_map/pallas_call | solution.py:253
  6.8 0.9 slice_bitcast_fusion.1
  7.7 0.0 copy-start.1
  7.7 1.4 %collective-permute-start = (f32[1024,128]{1,0:T(8,128)S(1)}, f32[1024,128]{1,0:T(8,128)S(1)}, u32[]{:S(2)}, u32[]{:S(2)}) collective-permute-start(f32[1024,128]{1,0:T(8,128)S(1)} %get-tuple-element.26), channel_id=1, source_target_pairs={{0,4},{4,0},{8,12},{12,8},{16,20},{20,16},{24,28},{28,24},{32,36},... | collective-permute-start | bytes 1572872 | tf_op jit(solution)/shard_map/ppermute | solution.py:230
  9.1 1.5 %collective-permute-done.side_own = f32[1024,128]{1,0:T(8,128)S(1)} collective-permute-done((f32[1024,128]{1,0:T(8,128)S(1)}, f32[1024,128]{1,0:T(8,128)S(1)}, u32[]{:S(2)}, u32[]{:S(2)}) %collective-permute-start) | collective-permute-done | bytes 524320 | tf_op jit(solution)/shard_map/ppermute | solution.py:230
  10.7 0.1 fusion.1
  10.7 17.4 %all_to_all.20.parts = f32[16,64,128]{2,1,0:T(8,128)S(1)} all-to-all(f32[16,64,128]{2,1,0:T(8,128)S(1)} %bitcast.24), channel_id=1, replica_groups={{0,8,16,24,32,40,48,56,64,72,80,88,96,104,112,120},{4,12,20,28,36,44,52..., dimensions={0} | all-to-all | bytes 1048576 | tf_op jit(solution)/shard_map/all_to_all | solution.py:226
  28.1 0.0 copy-start.8
  28.1 0.8 copy-done.8
  28.9 3.6 %all-to-all-start.1 = ((f32[16,64,128]{2,1,0:T(8,128)}), f32[16,64,128]{2,1,0:T(8,128)S(1)}, u32[]{:S(2)}, u32[]{:S(2)}) async-start(f32[16,64,128]{2,1,0:T(8,128)} %copy-done.8), calls=%async_computation.1 | async-start | bytes 1048576 | tf_op jit(solution)/shard_map/all_to_all | solution.py:226
  32.5 1.9 %collective-permute-start.2 = (f32[1024,128]{1,0:T(8,128)}, f32[1024,128]{1,0:T(8,128)}, u32[]{:S(2)}, u32[]{:S(2)}) collective-permute-start(f32[1024,128]{1,0:T(8,128)} %get-tuple-element.25), channel_id=1, source_target_pairs={{0,4},{4,0},{8,12},{12,8},{16,20},{20,16},{24,28},{28,24},{32,36},... | collective-permute-start | bytes 1572872 | tf_op jit(solution)/shard_map/ppermute | solution.py:230
  34.4 8.1 %all-to-all-done.1 = f32[16,64,128]{2,1,0:T(8,128)S(1)} async-done(((f32[16,64,128]{2,1,0:T(8,128)}), f32[16,64,128]{2,1,0:T(8,128)S(1)}, u32[]{:S(2)}, u32[]{:S(2)}) %all-to-all-start.1) | async-done | bytes 524320 | tf_op jit(solution)/shard_map/all_to_all | solution.py:226
  42.5 0.0 copy-start
  42.5 2.5 %collective-permute-start.1 = (f32[1024,128]{1,0:T(8,128)S(1)}, f32[1024,128]{1,0:T(8,128)S(1)}, u32[]{:S(2)}, u32[]{:S(2)}) collective-permute-start(f32[1024,128]{1,0:T(8,128)S(1)} %bitcast.20), channel_id=1, source_target_pairs={{0,4},{4,0},{8,12},{12,8},{16,20},{20,16},{24,28},{28,24},{32,36},... | collective-permute-start | bytes 1572872 | tf_op jit(solution)/shard_map/ppermute | solution.py:230
  45.0 0.0 copy-done.1
  45.0 0.0 copy-start.3
  45.0 1.6 %copy-done.3 = bf16[512,2048]{1,0:T(8,128)(2,1)S(1)} copy-done((bf16[512,2048]{1,0:T(8,128)(2,1)S(1)}, bf16[512,2048]{1,0:T(8,128)(2,1)}, u32[]{:S(2)}) %copy-start.3) | copy-done | bytes 2097176
  46.6 0.0 copy-start.6
  46.6 1.6 %copy-done.6 = bf16[512,2048]{1,0:T(8,128)(2,1)S(1)} copy-done((bf16[512,2048]{1,0:T(8,128)(2,1)S(1)}, bf16[512,2048]{1,0:T(8,128)(2,1)}, u32[]{:S(2)}) %copy-start.6) | copy-done | bytes 2097176
  48.2 0.0 copy-start.10
  48.2 8.8 %shard_map.76.intra = f32[512,2048]{1,0:T(8,128)S(1)} custom-call(s32[1]{0:T(128)} %bitcast.core, bf16[512,2048]{1,0:T(8,128)(2,1)S(1)} %copy-done.1, bf16[512,2048]{1,0:T(8,128)(2,1)S(1)} %copy-done.3, bf16[512,2048]{1,0:T(8,128)(2,1)S(1)} %copy-done.6), custom_call_target="tpu_custom_call" | custom-call | flops 3221225472 | bytes 10485760 | tf_op jit(solution)/shard_map/pallas_call | solution.py:257
  57.0 0.0 collective-permute-done.2.side_other
  57.0 0.0 collective-permute-done.1.base_other
  57.0 0.0 copy-done
  57.0 0.0 copy-done.10
  57.0 5.9 %shard_map.79 = (f32[512,2048]{1,0:T(8,128)S(1)}, bf16[2,1024,128]{2,1,0:T(8,128)(2,1)S(1)}, f32[2,512]{1,0:T(2,128)S(1)}) custom-call(s32[1]{0:T(128)} %bitcast.core, bf16[512,2048]{1,0:T(8,128)(2,1)S(1)} %copy-done.1, f32[512,2048]{1,0:T(8,128)S(1)} %shard_map.76.intra, bf16[512,2048]{1,0:T(8,128)(2,1)S(1)} %copy-done, f32[1,2048]{1,0:T(1,128)S(1)} %bitcast.22, ...), custom_call_target="tpu_custom_call" | custom-call | flops 268435456 | bytes 14680064 | tf_op jit(solution)/shard_map/pallas_call | solution.py:260
  62.9 0.0 copy-start.13
  63.0 3.8 %collective-permute-start.5 = (f32[2,512]{1,0:T(2,128)S(1)}, f32[2,512]{1,0:T(2,128)S(1)}, u32[]{:S(2)}, u32[]{:S(2)}) collective-permute-start(f32[2,512]{1,0:T(2,128)S(1)} %get-tuple-element.14.s0), channel_id=1, source_target_pairs={{0,3},{1,0},{2,1},{3,2},{4,7},{5,4},{6,5},{7,6},{8,11},{9,8},{10,9... | collective-permute-start | bytes 12296 | tf_op jit(solution)/shard_map/ppermute | solution.py:270
  66.8 0.0 collective-permute-start.4
  66.8 0.7 collective-permute-start.3
  67.5 0.1 collective-permute-done.5.s3
  67.5 3.2 %collective-permute-done.4.s2 = f32[2,512]{1,0:T(2,128)S(1)} collective-permute-done((f32[2,512]{1,0:T(2,128)S(1)}, f32[2,512]{1,0:T(2,128)S(1)}, u32[]{:S(2)}, u32[]{:S(2)}) %collective-permute-start.4) | collective-permute-done | bytes 4128 | tf_op jit(solution)/shard_map/ppermute | solution.py:270
  70.7 0.0 collective-permute-done.3.s1
  70.7 4.7 %shard_map.80 = (bf16[512,2048]{1,0:T(8,128)(2,1)S(1)}, f32[2,1024,128]{2,1,0:T(8,128)S(1)}) custom-call(s32[1]{0:T(128)} %bitcast.core, bf16[512,2048]{1,0:T(8,128)(2,1)S(1)} %copy-done.1, f32[512,2048]{1,0:T(8,128)S(1)} %get-tuple-element.13.output, bf16[512,2048]{1,0:T(8,128)(2,1)S(1)} %copy-done, f32[1,2048]{1,0:T(1,128)S(1)} %bitcast.23, ...), custom_call_target="tpu_custom_call" | custom-call | flops 536870912 | bytes 11534336 | tf_op jit(solution)/shard_map/pallas_call | solution.py:272
  75.4 0.0 copy-done.13
  75.4 0.0 copy-start.11
  75.4 1.0 slice_bitcast_fusion.3
  76.5 1.6 %collective-permute-start.6 = (f32[1024,128]{1,0:T(8,128)S(1)}, f32[1024,128]{1,0:T(8,128)S(1)}, u32[]{:S(2)}, u32[]{:S(2)}) collective-permute-start(f32[1024,128]{1,0:T(8,128)S(1)} %get-tuple-element.24), channel_id=1, source_target_pairs={{0,4},{4,0},{8,12},{12,8},{16,20},{20,16},{24,28},{28,24},{32,36},... | collective-permute-start | bytes 1572872 | tf_op jit(solution)/shard_map/ppermute | solution.py:230
  78.1 1.5 %collective-permute-done.6.side_own = f32[1024,128]{1,0:T(8,128)S(1)} collective-permute-done((f32[1024,128]{1,0:T(8,128)S(1)}, f32[1024,128]{1,0:T(8,128)S(1)}, u32[]{:S(2)}, u32[]{:S(2)}) %collective-permute-start.6) | collective-permute-done | bytes 524320 | tf_op jit(solution)/shard_map/ppermute | solution.py:230
  79.6 0.1 fusion
  79.7 13.3 %all_to_all.21.parts = f32[16,64,128]{2,1,0:T(8,128)S(1)} all-to-all(f32[16,64,128]{2,1,0:T(8,128)S(1)} %bitcast.25), channel_id=1, replica_groups={{0,8,16,24,32,40,48,56,64,72,80,88,96,104,112,120},{4,12,20,28,36,44,52..., dimensions={0} | all-to-all | bytes 1048576 | tf_op jit(solution)/shard_map/all_to_all | solution.py:226
  93.0 0.0 copy-done.11
  93.0 0.0 copy-start.9
  93.0 0.8 copy-done.9
  93.8 3.6 %all-to-all-start.3 = ((f32[16,64,128]{2,1,0:T(8,128)}), f32[16,64,128]{2,1,0:T(8,128)S(1)}, u32[]{:S(2)}, u32[]{:S(2)}) async-start(f32[16,64,128]{2,1,0:T(8,128)} %copy-done.9), calls=%async_computation.3 | async-start | bytes 1048576 | tf_op jit(solution)/shard_map/all_to_all | solution.py:226
  97.4 1.8 %collective-permute-start.8 = (f32[1024,128]{1,0:T(8,128)}, f32[1024,128]{1,0:T(8,128)}, u32[]{:S(2)}, u32[]{:S(2)}) collective-permute-start(f32[1024,128]{1,0:T(8,128)} %get-tuple-element.23), channel_id=1, source_target_pairs={{0,4},{4,0},{8,12},{12,8},{16,20},{20,16},{24,28},{28,24},{32,36},... | collective-permute-start | bytes 1572872 | tf_op jit(solution)/shard_map/ppermute | solution.py:230
  99.3 8.1 %all-to-all-done.3 = f32[16,64,128]{2,1,0:T(8,128)S(1)} async-done(((f32[16,64,128]{2,1,0:T(8,128)}), f32[16,64,128]{2,1,0:T(8,128)S(1)}, u32[]{:S(2)}, u32[]{:S(2)}) %all-to-all-start.3) | async-done | bytes 524320 | tf_op jit(solution)/shard_map/all_to_all | solution.py:226
  107.4 2.5 %collective-permute-start.7 = (f32[1024,128]{1,0:T(8,128)S(1)}, f32[1024,128]{1,0:T(8,128)S(1)}, u32[]{:S(2)}, u32[]{:S(2)}) collective-permute-start(f32[1024,128]{1,0:T(8,128)S(1)} %bitcast.18), channel_id=1, source_target_pairs={{0,4},{4,0},{8,12},{12,8},{16,20},{20,16},{24,28},{28,24},{32,36},... | collective-permute-start | bytes 1572872 | tf_op jit(solution)/shard_map/ppermute | solution.py:230
  109.9 0.0 copy-start.4
  109.9 1.6 %copy-done.4 = bf16[512,2048]{1,0:T(8,128)(2,1)S(1)} copy-done((bf16[512,2048]{1,0:T(8,128)(2,1)S(1)}, bf16[512,2048]{1,0:T(8,128)(2,1)}, u32[]{:S(2)}) %copy-start.4) | copy-done | bytes 2097176
  111.5 0.0 copy-start.7
  111.5 1.6 %copy-done.7 = bf16[512,2048]{1,0:T(8,128)(2,1)S(1)} copy-done((bf16[512,2048]{1,0:T(8,128)(2,1)S(1)}, bf16[512,2048]{1,0:T(8,128)(2,1)}, u32[]{:S(2)}) %copy-start.7) | copy-done | bytes 2097176
  113.1 0.0 copy-start.12
  113.1 1.6 %copy-done.12 = bf16[512,2048]{1,0:T(8,128)(2,1)S(1)} copy-done((bf16[512,2048]{1,0:T(8,128)(2,1)S(1)}, bf16[512,2048]{1,0:T(8,128)(2,1)}, u32[]{:S(2)}) %copy-start.12) | copy-done | bytes 2097176
  114.7 0.0 copy-start.14
  114.7 1.0 copy-done.14
  115.7 17.4 %shard_map.81 = (bf16[512,2048]{1,0:T(8,128)(2,1)}, f32[512,2048]{1,0:T(8,128)S(1)}, f32[512,2048]{1,0:T(8,128)S(1)}) custom-call(s32[1]{0:T(128)} %bitcast.core, bf16[512,2048]{1,0:T(8,128)(2,1)S(1)} %copy-done.1, bf16[512,2048]{1,0:T(8,128)(2,1)S(1)} %copy-done.4, bf16[512,2048]{1,0:T(8,128)(2,1)S(1)} %copy-done.7, bf16[512,2048]{1,0:T(8,128)(2,1)S(1)} %copy-done.12, ...), custom_call_target="tpu_custom_call" | custom-call | flops 5368709120 | bytes 18874368 | tf_op jit(solution)/shard_map/pallas_call | solution.py:282
  133.1 0.0 collective-permute-done.8.side_other
  133.1 0.0 collective-permute-done.7.base_other
  133.1 7.0 %shard_map.83 = (bf16[512,2048]{1,0:T(8,128)(2,1)}, bf16[512,2048]{1,0:T(8,128)(2,1)}) custom-call(s32[1]{0:T(128)} %bitcast.core, bf16[512,2048]{1,0:T(8,128)(2,1)S(1)} %copy-done.4, bf16[512,2048]{1,0:T(8,128)(2,1)S(1)} %copy-done.7, f32[512,2048]{1,0:T(8,128)S(1)} %get-tuple-element.18.key_part, f32[512,2048]{1,0:T(8,128)S(1)} %get-tuple-element.19.value_part, ...), custom_call_target="tpu_custom_call" | custom-call | flops 536870912 | bytes 18874368 | tf_op jit(solution)/shard_map/pallas_call | solution.py:290
  (2 shorter events, 0.1 us)
Async XLA Ops:
  0.6 1.6 %copy-start.2 = (bf16[512,2048]{1,0:T(8,128)(2,1)S(1)}, bf16[512,2048]{1,0:T(8,128)(2,1)}, u32[]{:S(2)}) copy-start(bf16[512,2048]{1,0:T(8,128)(2,1)} %k.7) | copy-start | bytes 6291460
  2.2 1.6 %copy-start.5 = (bf16[512,2048]{1,0:T(8,128)(2,1)S(1)}, bf16[512,2048]{1,0:T(8,128)(2,1)}, u32[]{:S(2)}) copy-start(bf16[512,2048]{1,0:T(8,128)(2,1)} %v.7) | copy-start | bytes 6291460
  7.7 37.3 %copy-start.1 = (bf16[512,2048]{1,0:T(8,128)(2,1)S(1)}, bf16[512,2048]{1,0:T(8,128)(2,1)}, u32[]{:S(2)}) copy-start(bf16[512,2048]{1,0:T(8,128)(2,1)} %q.7) | copy-start | bytes 6291460
  7.7 3.0 %collective-permute-start = (f32[1024,128]{1,0:T(8,128)S(1)}, f32[1024,128]{1,0:T(8,128)S(1)}, u32[]{:S(2)}, u32[]{:S(2)}) collective-permute-start(f32[1024,128]{1,0:T(8,128)S(1)} %get-tuple-element.26), channel_id=1, source_target_pairs={{0,4},{4,0},{8,12},{12,8},{16,20},{20,16},{24,28},{28,24},{32,36},... | collective-permute-start | bytes 1572872 | tf_op jit(solution)/shard_map/ppermute | solution.py:230
  28.1 0.8 copy-start.8
  28.9 13.5 %all-to-all-start.1 = ((f32[16,64,128]{2,1,0:T(8,128)}), f32[16,64,128]{2,1,0:T(8,128)S(1)}, u32[]{:S(2)}, u32[]{:S(2)}) async-start(f32[16,64,128]{2,1,0:T(8,128)} %copy-done.8), calls=%async_computation.1 | async-start | bytes 1048576 | tf_op jit(solution)/shard_map/all_to_all | solution.py:226
  32.5 24.5 %collective-permute-start.2 = (f32[1024,128]{1,0:T(8,128)}, f32[1024,128]{1,0:T(8,128)}, u32[]{:S(2)}, u32[]{:S(2)}) collective-permute-start(f32[1024,128]{1,0:T(8,128)} %get-tuple-element.25), channel_id=1, source_target_pairs={{0,4},{4,0},{8,12},{12,8},{16,20},{20,16},{24,28},{28,24},{32,36},... | collective-permute-start | bytes 1572872 | tf_op jit(solution)/shard_map/ppermute | solution.py:230
  42.5 14.6 %copy-start = (bf16[512,2048]{1,0:T(8,128)(2,1)S(1)}, bf16[512,2048]{1,0:T(8,128)(2,1)}, u32[]{:S(2)}) copy-start(bf16[512,2048]{1,0:T(8,128)(2,1)} %out_grad.3) | copy-start | bytes 6291460
  42.5 14.6 %collective-permute-start.1 = (f32[1024,128]{1,0:T(8,128)S(1)}, f32[1024,128]{1,0:T(8,128)S(1)}, u32[]{:S(2)}, u32[]{:S(2)}) collective-permute-start(f32[1024,128]{1,0:T(8,128)S(1)} %bitcast.20), channel_id=1, source_target_pairs={{0,4},{4,0},{8,12},{12,8},{16,20},{20,16},{24,28},{28,24},{32,36},... | collective-permute-start | bytes 1572872 | tf_op jit(solution)/shard_map/ppermute | solution.py:230
  45.0 1.6 %copy-start.3 = (bf16[512,2048]{1,0:T(8,128)(2,1)S(1)}, bf16[512,2048]{1,0:T(8,128)(2,1)}, u32[]{:S(2)}) copy-start(bf16[512,2048]{1,0:T(8,128)(2,1)} %k.7) | copy-start | bytes 6291460
  46.6 1.6 %copy-start.6 = (bf16[512,2048]{1,0:T(8,128)(2,1)S(1)}, bf16[512,2048]{1,0:T(8,128)(2,1)}, u32[]{:S(2)}) copy-start(bf16[512,2048]{1,0:T(8,128)(2,1)} %v.7) | copy-start | bytes 6291460
  48.2 8.8 %copy-start.10 = (f32[2048]{0:T(1024)S(1)}, f32[2048]{0:T(1024)}, u32[]{:S(2)}) copy-start(f32[2048]{0:T(1024)} %param.9) | copy-start | bytes 24580
  62.9 12.5 %copy-start.13 = (bf16[2,1024,128]{2,1,0:T(8,128)(2,1)}, bf16[2,1024,128]{2,1,0:T(8,128)(2,1)S(1)}, u32[]{:S(2)}) copy-start(bf16[2,1024,128]{2,1,0:T(8,128)(2,1)S(1)} %get-tuple-element.16.prefix_half) | copy-start | bytes 1572868
  63.0 4.6 %collective-permute-start.5 = (f32[2,512]{1,0:T(2,128)S(1)}, f32[2,512]{1,0:T(2,128)S(1)}, u32[]{:S(2)}, u32[]{:S(2)}) collective-permute-start(f32[2,512]{1,0:T(2,128)S(1)} %get-tuple-element.14.s0), channel_id=1, source_target_pairs={{0,3},{1,0},{2,1},{3,2},{4,7},{5,4},{6,5},{7,6},{8,11},{9,8},{10,9... | collective-permute-start | bytes 12296 | tf_op jit(solution)/shard_map/ppermute | solution.py:270
  66.8 4.0 %collective-permute-start.4 = (f32[2,512]{1,0:T(2,128)S(1)}, f32[2,512]{1,0:T(2,128)S(1)}, u32[]{:S(2)}, u32[]{:S(2)}) collective-permute-start(f32[2,512]{1,0:T(2,128)S(1)} %get-tuple-element.14.s0), channel_id=1, source_target_pairs={{0,2},{1,3},{2,0},{3,1},{4,6},{5,7},{6,4},{7,5},{8,10},{9,11},{10,... | collective-permute-start | bytes 12296 | tf_op jit(solution)/shard_map/ppermute | solution.py:270
  66.8 4.0 %collective-permute-start.3 = (f32[2,512]{1,0:T(2,128)S(1)}, f32[2,512]{1,0:T(2,128)S(1)}, u32[]{:S(2)}, u32[]{:S(2)}) collective-permute-start(f32[2,512]{1,0:T(2,128)S(1)} %get-tuple-element.14.s0), channel_id=1, source_target_pairs={{0,1},{1,2},{2,3},{3,0},{4,5},{5,6},{6,7},{7,4},{8,9},{9,10},{10,1... | collective-permute-start | bytes 12296 | tf_op jit(solution)/shard_map/ppermute | solution.py:270
  75.4 17.6 %copy-start.11 = (bf16[512,2048]{1,0:T(8,128)(2,1)}, bf16[512,2048]{1,0:T(8,128)(2,1)S(1)}, u32[]{:S(2)}) copy-start(bf16[512,2048]{1,0:T(8,128)(2,1)S(1)} %get-tuple-element.15.g) | copy-start | bytes 6291460
  76.5 3.1 %collective-permute-start.6 = (f32[1024,128]{1,0:T(8,128)S(1)}, f32[1024,128]{1,0:T(8,128)S(1)}, u32[]{:S(2)}, u32[]{:S(2)}) collective-permute-start(f32[1024,128]{1,0:T(8,128)S(1)} %get-tuple-element.24), channel_id=1, source_target_pairs={{0,4},{4,0},{8,12},{12,8},{16,20},{20,16},{24,28},{28,24},{32,36},... | collective-permute-start | bytes 1572872 | tf_op jit(solution)/shard_map/ppermute | solution.py:230
  93.0 0.8 copy-start.9
  93.8 13.6 %all-to-all-start.3 = ((f32[16,64,128]{2,1,0:T(8,128)}), f32[16,64,128]{2,1,0:T(8,128)S(1)}, u32[]{:S(2)}, u32[]{:S(2)}) async-start(f32[16,64,128]{2,1,0:T(8,128)} %copy-done.9), calls=%async_computation.3 | async-start | bytes 1048576 | tf_op jit(solution)/shard_map/all_to_all | solution.py:226
  97.4 35.7 %collective-permute-start.8 = (f32[1024,128]{1,0:T(8,128)}, f32[1024,128]{1,0:T(8,128)}, u32[]{:S(2)}, u32[]{:S(2)}) collective-permute-start(f32[1024,128]{1,0:T(8,128)} %get-tuple-element.23), channel_id=1, source_target_pairs={{0,4},{4,0},{8,12},{12,8},{16,20},{20,16},{24,28},{28,24},{32,36},... | collective-permute-start | bytes 1572872 | tf_op jit(solution)/shard_map/ppermute | solution.py:230
  107.4 25.7 %collective-permute-start.7 = (f32[1024,128]{1,0:T(8,128)S(1)}, f32[1024,128]{1,0:T(8,128)S(1)}, u32[]{:S(2)}, u32[]{:S(2)}) collective-permute-start(f32[1024,128]{1,0:T(8,128)S(1)} %bitcast.18), channel_id=1, source_target_pairs={{0,4},{4,0},{8,12},{12,8},{16,20},{20,16},{24,28},{28,24},{32,36},... | collective-permute-start | bytes 1572872 | tf_op jit(solution)/shard_map/ppermute | solution.py:230
  109.9 1.6 %copy-start.4 = (bf16[512,2048]{1,0:T(8,128)(2,1)S(1)}, bf16[512,2048]{1,0:T(8,128)(2,1)}, u32[]{:S(2)}) copy-start(bf16[512,2048]{1,0:T(8,128)(2,1)} %k.7) | copy-start | bytes 6291460
  111.5 1.6 %copy-start.7 = (bf16[512,2048]{1,0:T(8,128)(2,1)S(1)}, bf16[512,2048]{1,0:T(8,128)(2,1)}, u32[]{:S(2)}) copy-start(bf16[512,2048]{1,0:T(8,128)(2,1)} %v.7) | copy-start | bytes 6291460
  113.1 1.6 %copy-start.12 = (bf16[512,2048]{1,0:T(8,128)(2,1)S(1)}, bf16[512,2048]{1,0:T(8,128)(2,1)}, u32[]{:S(2)}) copy-start(bf16[512,2048]{1,0:T(8,128)(2,1)} %copy-done.11) | copy-start | bytes 6291460
  114.7 1.0 copy-start.14

commit v2 on v0

v2 whole, which is shorter than its diff:
```python
import functools

import jax
import jax.numpy as jnp
from jax import lax
from jax.experimental import pallas as pl
from jax.experimental.pallas import tpu as pltpu
from jax.sharding import PartitionSpec as P

DH = 128
BLOCK = 512
HALF = 256
WIDTH = 2048
SIDE = WIDTH // 2
WIDTH_ALL = 8192
HEADS_SIDE = SIDE // DH
PAIRS_SIDE = HEADS_SIDE // 2
ROWS = HEADS_SIDE * DH
CHIPS = 16
SLICE = ROWS // CHIPS
MIB = 1024 * 1024

epsilon = 1e-06

F32 = jnp.float32
BF16 = jnp.bfloat16

VMEM = pl.BlockSpec(memory_space=pltpu.VMEM)
SMEM = pl.BlockSpec(memory_space=pltpu.SMEM)
HBM = pl.BlockSpec(memory_space=pltpu.HBM)


def hbm(dims, kind):
    return pltpu.HBM(dims, kind)


SIDE_F32 = jax.ShapeDtypeStruct((BLOCK, SIDE), F32)
SIDE_BF16 = jax.ShapeDtypeStruct((BLOCK, SIDE), BF16)
STATE = jax.ShapeDtypeStruct((ROWS, DH), F32)
STATE_HALF = jax.ShapeDtypeStruct((ROWS, DH), BF16)
LANES = jax.ShapeDtypeStruct((BLOCK, DH), F32)
STATS = jax.ShapeDtypeStruct((2, BLOCK), F32)
WHOLE = hbm((BLOCK, WIDTH), BF16)
FAR_F32 = hbm((BLOCK, SIDE), F32)
FAR_BF16 = hbm((BLOCK, SIDE), BF16)
BUFFER_F32 = pltpu.VMEM((BLOCK, SIDE), F32)
FIRST_BUFFER = pltpu.VMEM((HEADS_SIDE * HALF, HALF), BF16)
LAST_BUFFER = pltpu.VMEM((HEADS_SIDE * BLOCK, HALF), BF16)
BUFFER_BF16 = pltpu.VMEM((BLOCK, SIDE), BF16)


def copies_of(pairs, sems):
    copies = []
    for place, (source, target) in enumerate(pairs):
        copy = pltpu.make_async_copy(source, target, sems.at[place])
        copy.start()
        copies.append(copy)
    return copies


def wait(copies):
    for copy in copies:
        copy.wait()


def call(name, body, in_specs, out_specs, out_shape, flops, moved, scratch=(), aliases=None):
    kernel = pl.pallas_call(
        body,
        in_specs=in_specs,
        out_specs=out_specs,
        out_shape=out_shape,
        scratch_shapes=list(scratch),
        input_output_aliases=aliases or {},
        compiler_params=pltpu.CompilerParams(vmem_limit_bytes=16 * MIB),
        cost_estimate=pl.CostEstimate(flops=flops, bytes_accessed=moved, transcendentals=0),
        name=name,
    )

    def run(*arrays):
        return kernel(
            *(
                pltpu.with_memory_space_constraint(array, pltpu.HBM) if spec is HBM else array
                for spec, array in zip(in_specs, arrays)
            )
        )

    return run


def dot(a, b):
    return lax.dot_general(a, b, (((1,), (0,)), ((), ())), preferred_element_type=F32)


def dot_nt(a, b):
    return lax.dot_general(a, b, (((1,), (1,)), ((), ())), preferred_element_type=F32)


def dot_tn(a, b):
    return lax.dot_general(a, b, (((0,), (0,)), ((), ())), preferred_element_type=F32)


def pair_columns(pair):
    return slice(pair * 2 * DH, (pair + 1) * 2 * DH)


def head_columns(head):
    return slice(head * DH, (head + 1) * DH)


def diagonal(states, pair):
    first = states[2 * pair * DH : (2 * pair + 1) * DH, :]
    second = states[(2 * pair + 1) * DH : (2 * pair + 2) * DH, :]
    zero = jnp.zeros_like(first)
    return jnp.concatenate(
        [jnp.concatenate([first, zero], axis=1), jnp.concatenate([zero, second], axis=1)], axis=0
    )


def store_states(out, pair, a, b):
    both = dot_tn(a, b)
    out[2 * pair * DH : (2 * pair + 1) * DH, :] = both[:DH, :DH]
    out[(2 * pair + 1) * DH : (2 * pair + 2) * DH, :] = both[DH:, DH:]


def seen_keys():
    rows = lax.broadcasted_iota(jnp.int32, (HALF, HALF), 0)
    cols = lax.broadcasted_iota(jnp.int32, (HALF, HALF), 1)
    return cols <= rows


def seen_queries():
    rows = lax.broadcasted_iota(jnp.int32, (HALF, HALF), 0)
    cols = lax.broadcasted_iota(jnp.int32, (HALF, HALF), 1)
    return cols >= rows


def keep(mask, array):
    return jnp.where(mask, array, 0.0).astype(BF16)


TOP = slice(0, HALF)
BOTTOM = slice(HALF, BLOCK)


def by_keys(mask, queries, keys):
    first = dot_nt(queries, keys[TOP])
    last = dot_nt(queries[BOTTOM], keys[BOTTOM])
    first = jnp.concatenate([keep(mask, first[TOP]), first[BOTTOM].astype(BF16)], axis=0)
    return first, keep(mask, last)


def by_queries(mask, keys, queries):
    first = dot_nt(keys[TOP], queries[TOP])
    last = dot_nt(keys, queries[BOTTOM])
    last = jnp.concatenate([last[TOP].astype(BF16), keep(mask, last[BOTTOM])], axis=0)
    return keep(mask, first), last


def side_start(core, side):
    half = core[0] if side == 0 else 1 - core[0]
    return pl.multiple_of(half * SIDE, SIDE)


def pair_window(core, side, pair):
    return pl.ds(pl.multiple_of(side_start(core, side) + pair * 2 * DH, 2 * DH), 2 * DH)


def head_window(core, side, head):
    return pl.ds(pl.multiple_of(side_start(core, side) + head * DH, DH), DH)


PAIRS = range(PAIRS_SIDE)


def local_state_body(side, core, k_all, v_all, out, k, v, sems):
    copies = copies_of(
        [
            (source.at[:, pair_window(core, side, pair)], target.at[:, pair_columns(pair)])
            for pair in PAIRS
            for source, target in ((k_all, k), (v_all, v))
        ],
        sems,
    )
    for pair in PAIRS:
        wait(copies[2 * pair : 2 * pair + 2])
        store_states(out, pair, k[:, pair_columns(pair)], v[:, pair_columns(pair)])


def local_state(side, core, keys, values):
    return call(
        f"state{side}",
        functools.partial(local_state_body, side),
        [SMEM, HBM, HBM],
        VMEM,
        STATE,
        2 * BLOCK * SIDE * DH,
        2 * MIB,
        [BUFFER_BF16, BUFFER_BF16, pltpu.SemaphoreType.DMA((2 * PAIRS_SIDE,))],
    )(core, keys, values)


def first_rows(pair):
    return pl.ds(2 * pair * HALF, 2 * HALF)


def last_rows(pair):
    return pl.ds(2 * pair * BLOCK, 2 * BLOCK)


def intra_body(
    side, core, q_all, k_all, v_all, far, first_far, last_far, q, k, v, out, first, last, sems, out_sems
):
    before, behind = seen_keys(), seen_queries()
    copies = copies_of(
        [
            (source.at[:, pair_window(core, side, pair)], target.at[:, pair_columns(pair)])
            for pair in PAIRS
            for source, target in ((q_all, q), (k_all, k), (v_all, v))
        ],
        sems,
    )
    results = []
    for pair in PAIRS:
        wait(copies[3 * pair : 3 * pair + 3])
        for head in (2 * pair, 2 * pair + 1):
            cols = head_columns(head)
            queries, keys, values = q[:, cols], k[:, cols], v[:, cols]
            scores0, scores1 = by_keys(before, queries, keys)
            first[pl.ds(head * HALF, HALF), :], last[pl.ds(head * BLOCK, BLOCK), :] = by_queries(
                behind, keys, queries
            )
            total = dot(scores0, values[TOP])
            out[TOP, cols] = total[TOP]
            out[BOTTOM, cols] = total[BOTTOM] + dot(scores1, values[BOTTOM])
        cols = pair_columns(pair)
        results += copies_of(
            [
                (out.at[:, cols], far.at[:, cols]),
                (first.at[first_rows(pair)], first_far.at[first_rows(pair)]),
                (last.at[last_rows(pair)], last_far.at[last_rows(pair)]),
            ],
            out_sems.at[pl.ds(3 * pair, 3)],
        )
    wait(results)


def intra_output(side, core, queries, keys, values):
    return call(
        f"intra{side}",
        functools.partial(intra_body, side),
        [SMEM, HBM, HBM, HBM],
        [HBM] * 3,
        [FAR_F32, hbm((HEADS_SIDE * HALF, HALF), BF16), hbm((HEADS_SIDE * BLOCK, HALF), BF16)],
        5 * BLOCK * BLOCK * SIDE,
        8 * MIB,
        [BUFFER_BF16] * 3
        + [BUFFER_F32, FIRST_BUFFER, LAST_BUFFER]
        + [pltpu.SemaphoreType.DMA((3 * PAIRS_SIDE,))] * 2,
    )(core, queries, keys, values)


def output_body(side, core, *refs):
    if side == 0:
        q_all, o_all, intra, intra1, gain, base, near = refs[:7]
        q, o, output, prefix_half, squares, products, q1, o1, near_output1, sems = refs[7:]
        copies = [
            (source.at[:, window], target.at[:, pair_columns(pair)])
            for pair in PAIRS
            for source, target, window in (
                (q_all, q, pair_window(core, 0, pair)),
                (intra, output, pair_columns(pair)),
                (o_all, o, pair_window(core, 0, pair)),
            )
        ]
        other = pl.ds(side_start(core, 1), SIDE)
        copies += [(q_all.at[:, other], q1), (o_all.at[:, other], o1), (intra1, near_output1)]
        copies = copies_of(copies, sems)
    else:
        q, o, intra, gain, base, near, squares_in, products_in = refs[:8]
        output, prefix_half, stats = refs[8:]
    weight = core[0].astype(F32)
    gains = gain[:, pl.ds(side_start(core, side), SIDE)]
    prefix_half[...] = (base[...] + weight * near[...]).astype(BF16)
    parts = (slice(0, HALF), slice(HALF, BLOCK))
    if side == 0:
        square_sums = [jnp.zeros((HALF, DH), F32) for rows in parts]
        product_sums = [jnp.zeros((HALF, DH), F32) for rows in parts]
    else:
        square_sums = [squares_in[rows, :] for rows in parts]
        product_sums = [products_in[rows, :] for rows in parts]
    for pair in PAIRS:
        cols = pair_columns(pair)
        if side == 0:
            wait(copies[3 * pair : 3 * pair + 3])
        states = diagonal(prefix_half, pair)
        for part, rows in enumerate(parts):
            start = output if side == 0 else intra
            value = start[rows, cols] + dot(q[rows, cols], states)
            output[rows, cols] = value
            terms = o[rows, cols].astype(F32) * gains[:, cols] * value
            value = value * value
            square_sums[part] = square_sums[part] + (value[:, :DH] + value[:, DH:])
            product_sums[part] = product_sums[part] + (terms[:, :DH] + terms[:, DH:])
    for part, rows in enumerate(parts):
        if side == 0:
            squares[rows, :] = square_sums[part]
            products[rows, :] = product_sums[part]
        else:
            stats[0:1, rows] = jnp.sum(square_sums[part].T, axis=0, keepdims=True)
            stats[1:2, rows] = jnp.sum(product_sums[part].T, axis=0, keepdims=True)
    if side == 0:
        wait(copies[3 * PAIRS_SIDE :])


def output_own(core, queries, out_grad, intra, intra1, gain, base, near):
    return call(
        "output0",
        functools.partial(output_body, 0),
        [SMEM] + [HBM] * 4 + [VMEM] * 3,
        [VMEM] * 9,
        [SIDE_BF16, SIDE_BF16, SIDE_F32, STATE_HALF, LANES, LANES, SIDE_BF16, SIDE_BF16, SIDE_F32],
        2 * BLOCK * SIDE * DH,
        8 * MIB,
        [pltpu.SemaphoreType.DMA((3 * PAIRS_SIDE + 3,))],
    )(core, queries, out_grad, intra, intra1, gain, base, near)


def output_other(core, q, o, intra, gain, base, near, squares, products):
    return call(
        "output1",
        functools.partial(output_body, 1),
        [SMEM] + [VMEM] * 8,
        [VMEM] * 3,
        [SIDE_F32, STATE_HALF, STATS],
        2 * BLOCK * SIDE * DH,
        MIB,
    )(core, q, o, intra, gain, base, near, squares, products)


def grad_body(side, core, q, output, o, gain, s0, s1, s2, s3, far, states, grad_out, sems):
    total = (s0[...] + s1[...]) + (s2[...] + s3[...])
    mean_square = total[0:1, :] / WIDTH_ALL + epsilon
    radius = jnp.sqrt(mean_square)
    scale = total[1:2, :] / (WIDTH_ALL * radius * radius)
    inverse = jnp.broadcast_to(1.0 / radius, (DH, BLOCK)).T
    coeff = jnp.broadcast_to(scale, (DH, BLOCK)).T
    gains = gain[:, pl.ds(side_start(core, side), SIDE)]
    for rows in range(0, BLOCK, DH):
        rows = slice(rows, rows + DH)
        inverse_rows, coeff_rows = inverse[rows, :], coeff[rows, :]
        for head in range(HEADS_SIDE):
            cols = head_columns(head)
            scaled = o[rows, cols].astype(F32) * gains[:, cols]
            grad = (scaled - output[rows, cols] * coeff_rows) * inverse_rows
            grad_out[rows, cols] = grad.astype(BF16)
    copies = copies_of([(grad_out, far)], sems)
    for pair in PAIRS:
        store_states(states, pair, q[:, pair_columns(pair)], grad_out[:, pair_columns(pair)])
    wait(copies)


def local_grad(side, core, q, output, o, gain, stats):
    return call(
        f"grad{side}",
        functools.partial(grad_body, side),
        [SMEM] + [VMEM] * 8,
        [HBM, VMEM],
        [FAR_BF16, STATE],
        2 * BLOCK * SIDE * DH,
        MIB,
        [BUFFER_BF16, pltpu.SemaphoreType.DMA((1,))],
    )(core, q, output, o, gain, *stats)


def query_body(side, core, k_all, v_all, grad_out, prefix, *refs):
    query_grad, k, v, g, result, sems, out_sems = refs[-7:]
    before = seen_keys()
    copies = copies_of(
        [
            (source.at[:, window], target.at[:, pair_columns(pair)])
            for pair in PAIRS
            for source, target, window in (
                (k_all, k, pair_window(core, side, pair)),
                (v_all, v, pair_window(core, side, pair)),
                (grad_out, g, pair_columns(pair)),
            )
        ],
        sems,
    )
    results = []
    for pair in PAIRS:
        wait(copies[3 * pair : 3 * pair + 3])
        across = dot_nt(g[:, pair_columns(pair)], diagonal(prefix, pair))
        for h in range(2):
            cols = head_columns(2 * pair + h)
            part = across[:, h * DH : (h + 1) * DH]
            mixing0, mixing1 = by_keys(before, g[:, cols], v[:, cols])
            total = part + dot(mixing0, k[TOP, cols])
            result[TOP, cols] = total[TOP].astype(BF16)
            result[BOTTOM, cols] = (total[BOTTOM] + dot(mixing1, k[BOTTOM, cols])).astype(BF16)
        results += copies_of(
            [(result.at[:, pair_columns(pair)], query_grad.at[:, pair_window(core, side, pair)])],
            out_sems.at[pl.ds(pair, 1)],
        )
    wait(results)


def query_gradient(side, core, keys, values, g, prefix, result=()):
    return call(
        f"query{side}",
        functools.partial(query_body, side),
        [SMEM, HBM, HBM, HBM, VMEM] + [HBM] * len(result),
        HBM,
        WHOLE,
        4 * BLOCK * BLOCK * SIDE,
        4 * MIB,
        [BUFFER_BF16] * 4
        + [pltpu.SemaphoreType.DMA((3 * PAIRS_SIDE,)), pltpu.SemaphoreType.DMA((PAIRS_SIDE,))],
        {5 + i: i for i in range(len(result))},
    )(core, keys, values, g, prefix, *result)


def part_body(side, core, q_all, v_all, g_far, first_far, last_far, key_far, value_far, *refs):
    q, v, g, first, last, key_part, value_part, sems, out_sems = refs
    behind = seen_queries()
    copies = copies_of(
        [
            (source.at[:, window], target.at[:, pair_columns(pair)])
            for pair in PAIRS
            for source, target, window in (
                (q_all, q, pair_window(core, side, pair)),
                (v_all, v, pair_window(core, side, pair)),
                (g_far, g, pair_columns(pair)),
            )
        ]
        + [
            (source.at[rows(pair)], target.at[rows(pair)])
            for pair in PAIRS
            for source, target, rows in ((first_far, first, first_rows), (last_far, last, last_rows))
        ],
        sems,
    )
    results = []
    for pair in PAIRS:
        wait(copies[3 * pair : 3 * pair + 3])
        wait(copies[3 * PAIRS_SIDE + 2 * pair : 3 * PAIRS_SIDE + 2 * pair + 2])
        for head in (2 * pair, 2 * pair + 1):
            cols = head_columns(head)
            mixing0, mixing1 = by_queries(behind, v[:, cols], g[:, cols])
            total = dot(last[pl.ds(head * BLOCK, BLOCK), :], g[BOTTOM, cols])
            value_part[TOP, cols] = total[TOP] + dot(first[pl.ds(head * HALF, HALF), :], g[TOP, cols])
            value_part[BOTTOM, cols] = total[BOTTOM]
            total = dot(mixing1, q[BOTTOM, cols])
            key_part[TOP, cols] = total[TOP] + dot(mixing0, q[TOP, cols])
            key_part[BOTTOM, cols] = total[BOTTOM]
        cols = pair_columns(pair)
        results += copies_of(
            [(key_part.at[:, cols], key_far.at[:, cols]), (value_part.at[:, cols], value_far.at[:, cols])],
            out_sems.at[pl.ds(2 * pair, 2)],
        )
    wait(results)


def key_value_parts(side, core, queries, values, g, turned):
    return call(
        f"part{side}",
        functools.partial(part_body, side),
        [SMEM] + [HBM] * 5,
        [HBM] * 2,
        [FAR_F32, FAR_F32],
        5 * BLOCK * BLOCK * SIDE,
        10 * MIB,
        [BUFFER_BF16] * 3
        + [FIRST_BUFFER, LAST_BUFFER]
        + [BUFFER_F32] * 2
        + [pltpu.SemaphoreType.DMA((5 * PAIRS_SIDE,)), pltpu.SemaphoreType.DMA((2 * PAIRS_SIDE,))],
    )(core, queries, values, g, *turned)


def last_body(side, core, *refs):
    if side == 0:
        k_all, v_all, key_far, value_far, key_far1, value_far1, base, near = refs[:8]
        key_grad, value_grad, k1, v1, key_part1, value_part1 = refs[8:14]
        k, v, key_part, value_part, key_half, value_half, sems, out_sems = refs[14:]
        other = pl.ds(side_start(core, 1), SIDE)
        copies = [
            (source.at[:, window], target.at[:, pair_columns(pair)])
            for pair in PAIRS
            for source, target, window in (
                (k_all, k, pair_window(core, 0, pair)),
                (v_all, v, pair_window(core, 0, pair)),
                (key_far, key_part, pair_columns(pair)),
                (value_far, value_part, pair_columns(pair)),
            )
        ]
        copies += [
            (k_all.at[:, other], k1),
            (v_all.at[:, other], v1),
            (key_far1, key_part1),
            (value_far1, value_part1),
        ]
        copies = copies_of(copies, sems)
    else:
        k, v, key_part, value_part, base, near = refs[:6]
        key_grad, value_grad, key_half, value_half, out_sems = refs[8:]
    weight = 1.0 - core[0].astype(F32)
    later = (base[...] + weight * near[...]).astype(BF16)
    results = []
    for pair in PAIRS:
        cols = pair_columns(pair)
        if side == 0:
            wait(copies[4 * pair : 4 * pair + 4])
        states = diagonal(later, pair)
        key_half[:, cols] = (key_part[:, cols] + dot_nt(v[:, cols], states)).astype(BF16)
        value_half[:, cols] = (value_part[:, cols] + dot(k[:, cols], states)).astype(BF16)
        window = pair_window(core, side, pair)
        results += copies_of(
            [(key_half.at[:, cols], key_grad.at[:, window]), (value_half.at[:, cols], value_grad.at[:, window])],
            out_sems.at[pl.ds(2 * pair, 2)],
        )
    wait(results)
    if side == 0:
        wait(copies[4 * PAIRS_SIDE :])


def last_own(core, keys, values, part, part1, base, near):
    return call(
        "last0",
        functools.partial(last_body, 0),
        [SMEM] + [HBM] * 6 + [VMEM] * 2,
        [HBM, HBM] + [VMEM] * 4,
        [WHOLE, WHOLE, SIDE_BF16, SIDE_BF16, SIDE_F32, SIDE_F32],
        4 * BLOCK * SIDE * DH,
        12 * MIB,
        [BUFFER_BF16, BUFFER_BF16, BUFFER_F32, BUFFER_F32, BUFFER_BF16, BUFFER_BF16]
        + [pltpu.SemaphoreType.DMA((4 * PAIRS_SIDE + 4,)), pltpu.SemaphoreType.DMA((2 * PAIRS_SIDE,))],
    )(core, keys, values, *part, *part1, base, near)


def last_other(core, k, v, key_part, value_part, base, near, key_grad, value_grad):
    return call(
        "last1",
        functools.partial(last_body, 1),
        [SMEM] + [VMEM] * 6 + [HBM] * 2,
        [HBM, HBM],
        [WHOLE, WHOLE],
        4 * BLOCK * SIDE * DH,
        2 * MIB,
        [BUFFER_BF16, BUFFER_BF16, pltpu.SemaphoreType.DMA((2 * PAIRS_SIDE,))],
        {7: 0, 8: 1},
    )(core, k, v, key_part, value_part, base, near, key_grad, value_grad)


def scan_body(reverse, parts, far, out, sems):
    state = jnp.zeros((SLICE, DH), F32)
    order = range(CHIPS - 1, -1, -1) if reverse else range(CHIPS)
    for place in order:
        out[place] = state
        state = state + parts[place]
    wait(copies_of([(out, far)], sems))


def chip_scan(parts, reverse):
    return call(
        f"scan{int(reverse)}",
        functools.partial(scan_body, reverse),
        [VMEM],
        HBM,
        hbm((CHIPS, SLICE, DH), F32),
        MIB,
        MIB,
        [pltpu.VMEM((CHIPS, SLICE, DH), F32), pltpu.SemaphoreType.DMA((1,))],
    )(parts)


PARTNERS = [(i, i ^ 1) for i in range(2 * CHIPS)]
SAME_CORE = [[core + 2 * chip for chip in range(CHIPS)] for core in range(2)]


def exchange(parts):
    return lax.all_to_all(parts, "ctx", 0, 0, axis_index_groups=SAME_CORE, tiled=True)


def swap(part):
    return lax.ppermute(part, "ctx", PARTNERS)


def along_heads(stats):
    hops = (1, 2, 3)
    return [lax.ppermute(stats, "head", [(i, (i + hop) % 4) for i in range(4)]) for hop in hops]


def after(value, *done):
    return lax.optimization_barrier((value,) + done)[0]


def local(query_rows, key_rows, value_rows, out_grad, norm_gain):
    core = (lax.axis_index("ctx") % 2).astype(jnp.int32).reshape(1)
    return device(core, query_rows, key_rows, value_rows, out_grad, norm_gain)


def device(core, query_rows, key_rows, value_rows, out_grad, norm_gain):
    gain = norm_gain.reshape(1, WIDTH)
    everything = (query_rows, key_rows, value_rows)

    state1 = local_state(1, core, key_rows, value_rows)
    near0 = swap(state1)
    state0 = local_state(0, core, key_rows, value_rows)
    parts = exchange((state0 + near0).reshape(CHIPS, SLICE, DH))
    near1 = swap(state0)
    intra0, *turned0 = intra_output(0, core, *everything)
    sums = chip_scan(after(parts, intra0), False)
    base0 = exchange(sums).reshape(ROWS, DH)
    intra1, *turned1 = intra_output(1, core, *everything)
    base0 = after(base0, intra1)
    base1 = swap(base0)
    q0, o0, output0, prefix0, squares, products, q1, o1, intra1 = output_own(
        core, query_rows, out_grad, intra0, intra1, gain, base0, near0
    )
    output1, prefix1, stats = output_other(
        core, q1, o1, intra1, gain, base1, near1, squares, products
    )
    stats = [stats] + along_heads(stats)

    g1, state1 = local_grad(1, core, q1, output1, o1, gain, stats)
    near0 = swap(state1)
    g0, state0 = local_grad(0, core, q0, output0, o0, gain, stats)
    parts = exchange((state0 + near0).reshape(CHIPS, SLICE, DH))
    near1 = swap(state0)
    part0 = key_value_parts(0, core, query_rows, value_rows, g0, turned0)
    query_grad = query_gradient(0, core, key_rows, value_rows, g0, prefix0)
    sums = chip_scan(after(parts, *part0, query_grad), True)
    base0 = exchange(sums).reshape(ROWS, DH)
    part1 = key_value_parts(1, core, query_rows, value_rows, g1, turned1)
    query_grad = query_gradient(1, core, key_rows, value_rows, g1, prefix1, (query_grad,))
    base0 = after(base0, *part1, query_grad)
    base1 = swap(base0)
    key_grad, value_grad, *rest = last_own(core, key_rows, value_rows, part0, part1, base0, near0)
    key_grad, value_grad = last_other(core, *rest, base1, near1, key_grad, value_grad)
    return query_grad, key_grad, value_grad


def solution(mesh):
    in_specs = (P("ctx", "head"), P("ctx", "head"), P("ctx", "head"), P("ctx", "head"), P("head"))
    out_specs = (P("ctx", "head"), P("ctx", "head"), P("ctx", "head"))
    return jax.shard_map(local, mesh=mesh, in_specs=in_specs, out_specs=out_specs, check_vma=False)
```

time: 394 us -> 105 us (0.27)
  waiting for transfers between devices: 232 us -> 10.4 us
  Pallas kernels: 0 us -> 56.2 us
  matrix products: 55.4 us -> 0 us
  other arithmetic: 50.1 us -> 1.77 us
  starting transfers between devices: 0.08 us -> 34.6 us
  local copies, waits for them, and re-layouts: 31.2 us -> 0.01 us
  between operations: 14.2 us -> 1.04 us
  blocking collectives: 8.96 us -> 0 us
    all_gather x2 -> x0, waiting for transfers between devices: 232 us -> none  [entering(): gathered = lax.all_gather(part, axis)]
    pallas_call x0 -> x16, Pallas kernels: none -> 56.2 us  [run(): kernel(*(pltpu.with_memory_space_constraint(array, pltpu.HBM) if spec is...]
    dot_general x12 -> x0, matrix products: 55.4 us -> none  [the longest x1 7.34 us: local(): jnp.einsum('hts,thj->shj', score_half, grad_out, preferred_element_type=j...]
    add x31 -> x2, other arithmetic: 46.2 us -> 1.77 us  [device(): parts = exchange((state0 + near0).reshape(CHIPS, SLICE, DH))]
    all_to_all x0 -> x4, starting transfers between devices: none -> 20.6 us  [exchange(): lax.all_to_all(parts, 'ctx', 0, 0, axis_index_groups=SAME_CORE, tiled=True)]
    unnamed x24 -> x2, local copies, waits for them, and re-layouts: 20 us -> 0.01 us
    ppermute x0 -> x9, starting transfers between devices: none -> 14 us  [the longest x6 8.29 us: swap(): return lax.ppermute(part, 'ctx', PARTNERS)]
    psum x1 -> x0, blocking collectives: 8.96 us -> none  [local(): squares, products = lax.psum((squares, products), 'head')]
  transfers between devices with their start and end apart: 2 -> 13, of which waited for: 2 -> 4; matrix products, arithmetic and copies ran while one was open for 10% -> 0% of each run, Pallas kernels for 0% -> 46%
where the time goes in v2:
time: 105 us; the launch traced here: 104 us
  Pallas kernels  56.2 us (54%)
  starting transfers between devices  34.6 us (33%)
  waiting for transfers between devices  10.4 us (10%)
  other arithmetic  1.77 us (2%)
    pallas_call x16, Pallas kernels, run(): kernel(*(pltpu.with_memory_space_constraint(array, pltpu.HBM) if spec is...  56.2 us
    all_to_all x4, starting transfers between devices, exchange(): lax.all_to_all(parts, 'ctx', 0, 0, axis_index_groups=SAME_CORE, tiled=True)  20.6 us
    all_to_all x4, waiting for transfers between devices, exchange(): lax.all_to_all(parts, 'ctx', 0, 0, axis_index_groups=SAME_CORE, tiled=True)  8.63 us
    ppermute x6, starting transfers between devices, swap(): return lax.ppermute(part, 'ctx', PARTNERS)  8.29 us
    ppermute x3, starting transfers between devices, along_heads(): lax.ppermute(stats, 'head', [(i, (i + hop) % 4) for i in range(4)])  5.74 us
  transfers between devices with their start and end apart: 13, of which 4 were waited for; matrix products, arithmetic and copies ran while one was open for 0% of the time, Pallas kernels for 46%

profile of v2, /device:TPU:1, one launch (start us, length us, event | category | flops | bytes accessed | tf_op | source)
XLA Modules:
  0.0 104.0 jit_solution(6074324278719952936)
XLA Ops:
  0.6 2.4 %state1.1 = f32[1024,128]{1,0:T(8,128)S(1)} custom-call(s32[1]{0:T(128)} %bitcast.core, bf16[512,2048]{1,0:T(8,128)(2,1)} %refs_0_.3, bf16[512,2048]{1,0:T(8,128)(2,1)} %refs_1_.3), custom_call_target="tpu_custom_call" | custom-call | flops 134217728 | bytes 2097152 | tf_op jit(solution)/shard_map/state1/pallas_call | solution.py:80
  3.0 1.5 %collective-permute-start = (f32[1024,128]{1,0:T(8,128)S(1)}, f32[1024,128]{1,0:T(8,128)S(1)}, u32[]{:S(2)}, u32[]{:S(2)}) collective-permute-start(f32[1024,128]{1,0:T(8,128)S(1)} %state1.1), channel_id=1, source_target_pairs={{0,4},{4,0},{8,12},{12,8},{16,20},{20,16},{24,28},{28,24},{32,36},... | collective-permute-start | bytes 1572872 | tf_op jit(solution)/shard_map/ppermute | solution.py:585
  4.5 2.4 %state0.1 = f32[1024,128]{1,0:T(8,128)S(1)} custom-call(s32[1]{0:T(128)} %bitcast.core, bf16[512,2048]{1,0:T(8,128)(2,1)} %refs_0_.3, bf16[512,2048]{1,0:T(8,128)(2,1)} %refs_1_.3), custom_call_target="tpu_custom_call" | custom-call | flops 134217728 | bytes 2097152 | tf_op jit(solution)/shard_map/state0/pallas_call | solution.py:80
  6.9 0.0 collective-permute-done.refs_6_
  6.9 0.8 add.11
  7.7 6.8 %all-to-all-start = ((f32[16,64,128]{2,1,0:T(8,128)}), f32[16,64,128]{2,1,0:T(8,128)S(1)}, u32[]{:S(2)}, u32[]{:S(2)}) async-start(f32[16,64,128]{2,1,0:T(8,128)} %bitcast.2), calls=%async_computation | async-start | bytes 1048576 | tf_op jit(solution)/shard_map/all_to_all | solution.py:581
  14.6 5.5 %intra0.1 = (f32[512,1024]{1,0:T(8,128)}, bf16[2048,256]{1,0:T(8,128)(2,1)}, bf16[4096,256]{1,0:T(8,128)(2,1)}) custom-call(s32[1]{0:T(128)} %bitcast.core, bf16[512,2048]{1,0:T(8,128)(2,1)} %q_all.7, bf16[512,2048]{1,0:T(8,128)(2,1)} %refs_0_.3, bf16[512,2048]{1,0:T(8,128)(2,1)} %refs_1_.3), custom_call_target="tpu_custom_call" | custom-call | flops 1342177280 | bytes 8388608 | tf_op jit(solution)/shard_map/intra0/pallas_call | solution.py:80
  20.1 5.5 %all-to-all-done.parts = f32[16,64,128]{2,1,0:T(8,128)S(1)} async-done(((f32[16,64,128]{2,1,0:T(8,128)}), f32[16,64,128]{2,1,0:T(8,128)S(1)}, u32[]{:S(2)}, u32[]{:S(2)}) %all-to-all-start) | async-done | bytes 524320 | tf_op jit(solution)/shard_map/all_to_all | solution.py:581
  25.7 0.8 scan0.1
  26.5 3.6 %all-to-all-start.1 = ((f32[16,64,128]{2,1,0:T(8,128)}), f32[16,64,128]{2,1,0:T(8,128)S(1)}, u32[]{:S(2)}, u32[]{:S(2)}) async-start(f32[16,64,128]{2,1,0:T(8,128)} %scan0.1), calls=%async_computation.1 | async-start | bytes 1048576 | tf_op jit(solution)/shard_map/all_to_all | solution.py:581
  30.1 0.0 copy-start
  30.1 1.5 %collective-permute-start.2 = (f32[1024,128]{1,0:T(8,128)S(1)}, f32[1024,128]{1,0:T(8,128)S(1)}, u32[]{:S(2)}, u32[]{:S(2)}) collective-permute-start(f32[1024,128]{1,0:T(8,128)S(1)} %state0.1), channel_id=1, source_target_pairs={{0,4},{4,0},{8,12},{12,8},{16,20},{20,16},{24,28},{28,24},{32,36},... | collective-permute-start | bytes 1572872 | tf_op jit(solution)/shard_map/ppermute | solution.py:585
  31.6 5.5 %intra1.1 = (f32[512,1024]{1,0:T(8,128)}, bf16[2048,256]{1,0:T(8,128)(2,1)}, bf16[4096,256]{1,0:T(8,128)(2,1)}) custom-call(s32[1]{0:T(128)} %bitcast.core, bf16[512,2048]{1,0:T(8,128)(2,1)} %q_all.7, bf16[512,2048]{1,0:T(8,128)(2,1)} %refs_0_.3, bf16[512,2048]{1,0:T(8,128)(2,1)} %refs_1_.3), custom_call_target="tpu_custom_call" | custom-call | flops 1342177280 | bytes 8388608 | tf_op jit(solution)/shard_map/intra1/pallas_call | solution.py:80
  37.2 3.1 %all-to-all-done.1 = f32[16,64,128]{2,1,0:T(8,128)S(1)} async-done(((f32[16,64,128]{2,1,0:T(8,128)}), f32[16,64,128]{2,1,0:T(8,128)S(1)}, u32[]{:S(2)}, u32[]{:S(2)}) %all-to-all-start.1) | async-done | bytes 524320 | tf_op jit(solution)/shard_map/all_to_all | solution.py:581
  40.3 2.3 %collective-permute-start.1 = (f32[1024,128]{1,0:T(8,128)S(1)}, f32[1024,128]{1,0:T(8,128)S(1)}, u32[]{:S(2)}, u32[]{:S(2)}) collective-permute-start(f32[1024,128]{1,0:T(8,128)S(1)} %bitcast.6), channel_id=1, source_target_pairs={{0,4},{4,0},{8,12},{12,8},{16,20},{20,16},{24,28},{28,24},{32,36},... | collective-permute-start | bytes 1572872 | tf_op jit(solution)/shard_map/ppermute | solution.py:585
  42.6 0.0 copy-done
  42.6 3.7 %output0.1 = (bf16[512,1024]{1,0:T(8,128)(2,1)S(1)}, bf16[512,1024]{1,0:T(8,128)(2,1)S(1)}, f32[512,1024]{1,0:T(8,128)S(1)}, bf16[1024,128]{1,0:T(8,128)(2,1)S(1...) custom-call(s32[1]{0:T(128)} %bitcast.core, ...), custom_call_target="tpu_custom_call" | custom-call | flops 134217728 | bytes 8388608 | tf_op jit(solution)/shard_map/output0/pallas_call | solution.py:80
  46.3 0.0 collective-permute-done.2.refs_5_
  46.3 0.0 collective-permute-done.1.refs_4_
  46.3 1.0 output1.1
  47.3 1.7 %collective-permute-start.3 = (f32[2,512]{1,0:T(2,128)S(1)}, f32[2,512]{1,0:T(2,128)S(1)}, u32[]{:S(2)}, u32[]{:S(2)}) collective-permute-start(f32[2,512]{1,0:T(2,128)S(1)} %get-tuple-element.51.s0), channel_id=1, source_target_pairs={{0,1},{1,2},{2,3},{3,0},{4,5},{5,6},{6,7},{7,4},{8,9},{9,10},{10,1... | collective-permute-start | bytes 12296 | tf_op jit(solution)/shard_map/ppermute | solution.py:590
  49.0 3.3 %collective-permute-start.4 = (f32[2,512]{1,0:T(2,128)S(1)}, f32[2,512]{1,0:T(2,128)S(1)}, u32[]{:S(2)}, u32[]{:S(2)}) collective-permute-start(f32[2,512]{1,0:T(2,128)S(1)} %get-tuple-element.51.s0), channel_id=1, source_target_pairs={{0,2},{1,3},{2,0},{3,1},{4,6},{5,7},{6,4},{7,5},{8,10},{9,11},{10,... | collective-permute-start | bytes 12296 | tf_op jit(solution)/shard_map/ppermute | solution.py:590
  52.3 0.7 collective-permute-start.5
  53.0 0.0 collective-permute-done.3.s1
  53.0 0.3 collective-permute-done.4.s2
  53.3 1.4 %collective-permute-done.5.s3 = f32[2,512]{1,0:T(2,128)S(1)} collective-permute-done((f32[2,512]{1,0:T(2,128)S(1)}, f32[2,512]{1,0:T(2,128)S(1)}, u32[]{:S(2)}, u32[]{:S(2)}) %collective-permute-start.5) | collective-permute-done | bytes 4128 | tf_op jit(solution)/shard_map/ppermute | solution.py:590
  54.7 1.6 %grad1.1 = (bf16[512,1024]{1,0:T(8,128)(2,1)}, f32[1024,128]{1,0:T(8,128)S(1)}) custom-call(s32[1]{0:T(128)} %bitcast.core, bf16[512,1024]{1,0:T(8,128)(2,1)S(1)} %get-tuple-element.45.refs_0_.q, f32[512,1024]{1,0:T(8,128)S(1)} %get-tuple-element.50.output, bf16[512,1024]{1,0:T(8,128)(2,1)S(1)} %get-tuple-element.46.refs_1_.o, f32[1,2048]{1,0:T(1,128)S(1)} %bitcast.12, ...), custom_call_target="tpu_custom_call" | custom-call | flops 134217728 | bytes 1048576 | tf_op jit(solution)/shard_map/grad1/pallas_call | solution.py:80
  56.3 1.8 %collective-permute-start.6 = (f32[1024,128]{1,0:T(8,128)S(1)}, f32[1024,128]{1,0:T(8,128)S(1)}, u32[]{:S(2)}, u32[]{:S(2)}) collective-permute-start(f32[1024,128]{1,0:T(8,128)S(1)} %get-tuple-element.68), channel_id=1, source_target_pairs={{0,4},{4,0},{8,12},{12,8},{16,20},{20,16},{24,28},{28,24},{32,36},... | collective-permute-start | bytes 1572872 | tf_op jit(solution)/shard_map/ppermute | solution.py:585
  58.1 1.6 %grad0.1 = (bf16[512,1024]{1,0:T(8,128)(2,1)}, f32[1024,128]{1,0:T(8,128)S(1)}) custom-call(s32[1]{0:T(128)} %bitcast.core, bf16[512,1024]{1,0:T(8,128)(2,1)S(1)} %get-tuple-element.54.q, f32[512,1024]{1,0:T(8,128)S(1)} %get-tuple-element.55.output, bf16[512,1024]{1,0:T(8,128)(2,1)S(1)} %get-tuple-element.56.o, f32[1,2048]{1,0:T(1,128)S(1)} %bitcast.13, ...), custom_call_target="tpu_custom_call" | custom-call | flops 134217728 | bytes 1048576 | tf_op jit(solution)/shard_map/grad0/pallas_call | solution.py:80
  59.8 0.0 collective-permute-done.6.refs_7_
  59.8 0.9 add.12
  60.7 3.6 %all-to-all-start.2 = ((f32[16,64,128]{2,1,0:T(8,128)}), f32[16,64,128]{2,1,0:T(8,128)S(1)}, u32[]{:S(2)}, u32[]{:S(2)}) async-start(f32[16,64,128]{2,1,0:T(8,128)} %bitcast.4), calls=%async_computation.2 | async-start | bytes 1048576 | tf_op jit(solution)/shard_map/all_to_all | solution.py:581
  64.3 5.0 %query0.1.refs_0_ = bf16[512,2048]{1,0:T(8,128)(2,1)} custom-call(s32[1]{0:T(128)} %bitcast.core, bf16[512,2048]{1,0:T(8,128)(2,1)} %refs_0_.3, bf16[512,2048]{1,0:T(8,128)(2,1)} %refs_1_.3, bf16[512,1024]{1,0:T(8,128)(2,1)} %get-tuple-element.57.grad_out.g_far, bf16[1024,128]{1,0:T(8,128)(2,1)S(1)} %get-tuple-element.58.prefix), custom_call_target="tpu_custom_call" | custom-call | flops 1073741824 | bytes 4194304 | tf_op jit(solution)/shard_map/query0/pallas_call | solution.py:80
  69.3 6.6 %part0.1 = (f32[512,1024]{1,0:T(8,128)}, f32[512,1024]{1,0:T(8,128)}) custom-call(s32[1]{0:T(128)} %bitcast.core, bf16[512,2048]{1,0:T(8,128)(2,1)} %q_all.7, bf16[512,2048]{1,0:T(8,128)(2,1)} %refs_1_.3, bf16[512,1024]{1,0:T(8,128)(2,1)} %get-tuple-element.57.grad_out.g_far, bf16[2048,256]{1,0:T(8,128)(2,1)} %get-tuple-element.59.first_far, ...), custom_call_target="tpu_custom_call" | custom-call | flops 1342177280 | bytes 10485760 | tf_op jit(solution)/shard_map/part0/pallas_call | solution.py:80
  75.9 0.0 all-to-all-done.2.parts
  75.9 0.8 scan1.1
  76.8 6.6 %all-to-all-start.3 = ((f32[16,64,128]{2,1,0:T(8,128)}), f32[16,64,128]{2,1,0:T(8,128)S(1)}, u32[]{:S(2)}, u32[]{:S(2)}) async-start(f32[16,64,128]{2,1,0:T(8,128)} %scan1.1), calls=%async_computation.3 | async-start | bytes 1048576 | tf_op jit(solution)/shard_map/all_to_all | solution.py:581
  83.4 1.1 %collective-permute-start.8 = (f32[1024,128]{1,0:T(8,128)S(1)}, f32[1024,128]{1,0:T(8,128)S(1)}, u32[]{:S(2)}, u32[]{:S(2)}) collective-permute-start(f32[1024,128]{1,0:T(8,128)S(1)} %get-tuple-element.67), channel_id=1, source_target_pairs={{0,4},{4,0},{8,12},{12,8},{16,20},{20,16},{24,28},{28,24},{32,36},... | collective-permute-start | bytes 1572872 | tf_op jit(solution)/shard_map/ppermute | solution.py:585
  84.5 6.6 %part1.1 = (f32[512,1024]{1,0:T(8,128)}, f32[512,1024]{1,0:T(8,128)}) custom-call(s32[1]{0:T(128)} %bitcast.core, bf16[512,2048]{1,0:T(8,128)(2,1)} %q_all.7, bf16[512,2048]{1,0:T(8,128)(2,1)} %refs_1_.3, bf16[512,1024]{1,0:T(8,128)(2,1)} %get-tuple-element.52.grad_out.g_far, bf16[2048,256]{1,0:T(8,128)(2,1)} %get-tuple-element.63.first_far, ...), custom_call_target="tpu_custom_call" | custom-call | flops 1342177280 | bytes 10485760 | tf_op jit(solution)/shard_map/part1/pallas_call | solution.py:80
  91.1 5.0 %query1.1 = bf16[512,2048]{1,0:T(8,128)(2,1)} custom-call(s32[1]{0:T(128)} %bitcast.core, bf16[512,2048]{1,0:T(8,128)(2,1)} %refs_0_.3, bf16[512,2048]{1,0:T(8,128)(2,1)} %refs_1_.3, bf16[512,1024]{1,0:T(8,128)(2,1)} %get-tuple-element.52.grad_out.g_far, bf16[1024,128]{1,0:T(8,128)(2,1)S(1)} %get-tuple-element.53.prefix, ...), custom_call_target="tpu_custom_call", output_to_operand_aliasing={{}: (5, {})} | custom-call | flops 1073741824 | bytes 4194304 | tf_op jit(solution)/shard_map/query1/pallas_call | solution.py:80
  96.2 0.0 all-to-all-done.3
  96.2 0.1 collective-permute-start.7
  96.3 5.8 %last0.1 = (bf16[512,2048]{1,0:T(8,128)(2,1)}, bf16[512,2048]{1,0:T(8,128)(2,1)}, bf16[512,1024]{1,0:T(8,128)(2,1)S(1)}, bf16[512,1024]{1,0:T(8,128)(2,1)S(1)}, ...) custom-call(s32[1]{0:T(128)} %bitcast.core, bf16[512,2048]{1,0:T(8,128)(2,1)} %refs_0_.3, bf16[512,2048]{1,0:T(8,128)(2,1)} %refs_1_.3, ...), custom_call_target="tpu_custom_call" | custom-call | flops 268435456 | bytes 12582912 | tf_op jit(solution)/shard_map/last0/pallas_call | solution.py:80
  102.1 0.0 collective-permute-done.8.refs_5_
  102.1 0.0 collective-permute-done.7.refs_4_
  102.1 1.7 %last1.1 = (bf16[512,2048]{1,0:T(8,128)(2,1)}, bf16[512,2048]{1,0:T(8,128)(2,1)}) custom-call(s32[1]{0:T(128)} %bitcast.core, bf16[512,1024]{1,0:T(8,128)(2,1)S(1)} %get-tuple-element.71.refs_0_, bf16[512,1024]{1,0:T(8,128)(2,1)S(1)} %get-tuple-element.72.refs_1_, ...), custom_call_target="tpu_custom_call", output_to_operand_aliasing={{0}: (7, {}), {1}: (8, {})} | custom-call | flops 268435456 | bytes 2097152 | tf_op jit(solution)/shard_map/last1/pallas_call | solution.py:80
Async XLA Ops:
  3.0 3.9 %collective-permute-start = (f32[1024,128]{1,0:T(8,128)S(1)}, f32[1024,128]{1,0:T(8,128)S(1)}, u32[]{:S(2)}, u32[]{:S(2)}) collective-permute-start(f32[1024,128]{1,0:T(8,128)S(1)} %state1.1), channel_id=1, source_target_pairs={{0,4},{4,0},{8,12},{12,8},{16,20},{20,16},{24,28},{28,24},{32,36},... | collective-permute-start | bytes 1572872 | tf_op jit(solution)/shard_map/ppermute | solution.py:585
  7.7 17.9 %all-to-all-start = ((f32[16,64,128]{2,1,0:T(8,128)}), f32[16,64,128]{2,1,0:T(8,128)S(1)}, u32[]{:S(2)}, u32[]{:S(2)}) async-start(f32[16,64,128]{2,1,0:T(8,128)} %bitcast.2), calls=%async_computation | async-start | bytes 1048576 | tf_op jit(solution)/shard_map/all_to_all | solution.py:581
  26.5 13.8 %all-to-all-start.1 = ((f32[16,64,128]{2,1,0:T(8,128)}), f32[16,64,128]{2,1,0:T(8,128)S(1)}, u32[]{:S(2)}, u32[]{:S(2)}) async-start(f32[16,64,128]{2,1,0:T(8,128)} %scan0.1), calls=%async_computation.1 | async-start | bytes 1048576 | tf_op jit(solution)/shard_map/all_to_all | solution.py:581
  30.1 12.5 %copy-start = (f32[2048]{0:T(1024)S(1)}, f32[2048]{0:T(1024)}, u32[]{:S(2)}) copy-start(f32[2048]{0:T(1024)} %param.9) | copy-start | bytes 24580
  30.1 16.1 %collective-permute-start.2 = (f32[1024,128]{1,0:T(8,128)S(1)}, f32[1024,128]{1,0:T(8,128)S(1)}, u32[]{:S(2)}, u32[]{:S(2)}) collective-permute-start(f32[1024,128]{1,0:T(8,128)S(1)} %state0.1), channel_id=1, source_target_pairs={{0,4},{4,0},{8,12},{12,8},{16,20},{20,16},{24,28},{28,24},{32,36},... | collective-permute-start | bytes 1572872 | tf_op jit(solution)/shard_map/ppermute | solution.py:585
  40.3 6.0 %collective-permute-start.1 = (f32[1024,128]{1,0:T(8,128)S(1)}, f32[1024,128]{1,0:T(8,128)S(1)}, u32[]{:S(2)}, u32[]{:S(2)}) collective-permute-start(f32[1024,128]{1,0:T(8,128)S(1)} %bitcast.6), channel_id=1, source_target_pairs={{0,4},{4,0},{8,12},{12,8},{16,20},{20,16},{24,28},{28,24},{32,36},... | collective-permute-start | bytes 1572872 | tf_op jit(solution)/shard_map/ppermute | solution.py:585
  47.3 5.7 %collective-permute-start.3 = (f32[2,512]{1,0:T(2,128)S(1)}, f32[2,512]{1,0:T(2,128)S(1)}, u32[]{:S(2)}, u32[]{:S(2)}) collective-permute-start(f32[2,512]{1,0:T(2,128)S(1)} %get-tuple-element.51.s0), channel_id=1, source_target_pairs={{0,1},{1,2},{2,3},{3,0},{4,5},{5,6},{6,7},{7,4},{8,9},{9,10},{10,1... | collective-permute-start | bytes 12296 | tf_op jit(solution)/shard_map/ppermute | solution.py:590
  49.0 4.3 %collective-permute-start.4 = (f32[2,512]{1,0:T(2,128)S(1)}, f32[2,512]{1,0:T(2,128)S(1)}, u32[]{:S(2)}, u32[]{:S(2)}) collective-permute-start(f32[2,512]{1,0:T(2,128)S(1)} %get-tuple-element.51.s0), channel_id=1, source_target_pairs={{0,2},{1,3},{2,0},{3,1},{4,6},{5,7},{6,4},{7,5},{8,10},{9,11},{10,... | collective-permute-start | bytes 12296 | tf_op jit(solution)/shard_map/ppermute | solution.py:590
  52.3 2.5 %collective-permute-start.5 = (f32[2,512]{1,0:T(2,128)S(1)}, f32[2,512]{1,0:T(2,128)S(1)}, u32[]{:S(2)}, u32[]{:S(2)}) collective-permute-start(f32[2,512]{1,0:T(2,128)S(1)} %get-tuple-element.51.s0), channel_id=1, source_target_pairs={{0,3},{1,0},{2,1},{3,2},{4,7},{5,4},{6,5},{7,6},{8,11},{9,8},{10,9... | collective-permute-start | bytes 12296 | tf_op jit(solution)/shard_map/ppermute | solution.py:590
  56.3 3.5 %collective-permute-start.6 = (f32[1024,128]{1,0:T(8,128)S(1)}, f32[1024,128]{1,0:T(8,128)S(1)}, u32[]{:S(2)}, u32[]{:S(2)}) collective-permute-start(f32[1024,128]{1,0:T(8,128)S(1)} %get-tuple-element.68), channel_id=1, source_target_pairs={{0,4},{4,0},{8,12},{12,8},{16,20},{20,16},{24,28},{28,24},{32,36},... | collective-permute-start | bytes 1572872 | tf_op jit(solution)/shard_map/ppermute | solution.py:585
  60.7 15.2 %all-to-all-start.2 = ((f32[16,64,128]{2,1,0:T(8,128)}), f32[16,64,128]{2,1,0:T(8,128)S(1)}, u32[]{:S(2)}, u32[]{:S(2)}) async-start(f32[16,64,128]{2,1,0:T(8,128)} %bitcast.4), calls=%async_computation.2 | async-start | bytes 1048576 | tf_op jit(solution)/shard_map/all_to_all | solution.py:581
  76.8 19.4 %all-to-all-start.3 = ((f32[16,64,128]{2,1,0:T(8,128)}), f32[16,64,128]{2,1,0:T(8,128)S(1)}, u32[]{:S(2)}, u32[]{:S(2)}) async-start(f32[16,64,128]{2,1,0:T(8,128)} %scan1.1), calls=%async_computation.3 | async-start | bytes 1048576 | tf_op jit(solution)/shard_map/all_to_all | solution.py:581
  83.4 18.7 %collective-permute-start.8 = (f32[1024,128]{1,0:T(8,128)S(1)}, f32[1024,128]{1,0:T(8,128)S(1)}, u32[]{:S(2)}, u32[]{:S(2)}) collective-permute-start(f32[1024,128]{1,0:T(8,128)S(1)} %get-tuple-element.67), channel_id=1, source_target_pairs={{0,4},{4,0},{8,12},{12,8},{16,20},{20,16},{24,28},{28,24},{32,36},... | collective-permute-start | bytes 1572872 | tf_op jit(solution)/shard_map/ppermute | solution.py:585
  96.2 5.9 %collective-permute-start.7 = (f32[1024,128]{1,0:T(8,128)S(1)}, f32[1024,128]{1,0:T(8,128)S(1)}, u32[]{:S(2)}, u32[]{:S(2)}) collective-permute-start(f32[1024,128]{1,0:T(8,128)S(1)} %bitcast.8), channel_id=1, source_target_pairs={{0,4},{4,0},{8,12},{12,8},{16,20},{20,16},{24,28},{28,24},{32,36},... | collective-permute-start | bytes 1572872 | tf_op jit(solution)/shard_map/ppermute | solution.py:585

commit v3 on v2

--- a/solution.py
+++ b/solution.py
@@ -71,7 +71,7 @@
         out_shape=out_shape,
         scratch_shapes=list(scratch),
         input_output_aliases=aliases or {},
-        compiler_params=pltpu.CompilerParams(vmem_limit_bytes=16 * MIB),
+        compiler_params=pltpu.CompilerParams(vmem_limit_bytes=20 * MIB),
         cost_estimate=pl.CostEstimate(flops=flops, bytes_accessed=moved, transcendentals=0),
         name=name,
     )
@@ -345,17 +345,15 @@
     inverse = jnp.broadcast_to(1.0 / radius, (DH, BLOCK)).T
     coeff = jnp.broadcast_to(scale, (DH, BLOCK)).T
     gains = gain[:, pl.ds(side_start(core, side), SIDE)]
-    for rows in range(0, BLOCK, DH):
-        rows = slice(rows, rows + DH)
-        inverse_rows, coeff_rows = inverse[rows, :], coeff[rows, :]
-        for head in range(HEADS_SIDE):
+    copies = []
+    for pair in PAIRS:
+        for head in (2 * pair, 2 * pair + 1):
             cols = head_columns(head)
-            scaled = o[rows, cols].astype(F32) * gains[:, cols]
-            grad = (scaled - output[rows, cols] * coeff_rows) * inverse_rows
-            grad_out[rows, cols] = grad.astype(BF16)
-    copies = copies_of([(grad_out, far)], sems)
-    for pair in PAIRS:
-        store_states(states, pair, q[:, pair_columns(pair)], grad_out[:, pair_columns(pair)])
+            scaled = o[:, cols].astype(F32) * gains[:, cols]
+            grad_out[:, cols] = ((scaled - output[:, cols] * coeff) * inverse).astype(BF16)
+        cols = pair_columns(pair)
+        copies += copies_of([(grad_out.at[:, cols], far.at[:, cols])], sems.at[pl.ds(pair, 1)])
+        store_states(states, pair, q[:, cols], grad_out[:, cols])
     wait(copies)
 
 
@@ -368,113 +366,76 @@
         [FAR_BF16, STATE],
         2 * BLOCK * SIDE * DH,
         MIB,
-        [BUFFER_BF16, pltpu.SemaphoreType.DMA((1,))],
+        [BUFFER_BF16, pltpu.SemaphoreType.DMA((PAIRS_SIDE,))],
     )(core, q, output, o, gain, *stats)
 
 
-def query_body(side, core, k_all, v_all, grad_out, prefix, *refs):
-    query_grad, k, v, g, result, sems, out_sems = refs[-7:]
-    before = seen_keys()
+def middle_body(side, core, q_all, k_all, v_all, g_far, first_far, last_far, prefix, *refs):
+    query_grad, key_far, value_far = refs[-14:-11]
+    q, k, v, g, first, last, result, key_part, value_part, sems, out_sems = refs[-11:]
+    before, behind = seen_keys(), seen_queries()
     copies = copies_of(
         [
-            (source.at[:, window], target.at[:, pair_columns(pair)])
+            copy
             for pair in PAIRS
-            for source, target, window in (
-                (k_all, k, pair_window(core, side, pair)),
-                (v_all, v, pair_window(core, side, pair)),
-                (grad_out, g, pair_columns(pair)),
+            for copy in (
+                (v_all.at[:, pair_window(core, side, pair)], v.at[:, pair_columns(pair)]),
+                (g_far.at[:, pair_columns(pair)], g.at[:, pair_columns(pair)]),
+                (k_all.at[:, pair_window(core, side, pair)], k.at[:, pair_columns(pair)]),
+                (q_all.at[:, pair_window(core, side, pair)], q.at[:, pair_columns(pair)]),
+                (first_far.at[first_rows(pair)], first.at[first_rows(pair)]),
+                (last_far.at[last_rows(pair)], last.at[last_rows(pair)]),
             )
         ],
         sems,
     )
     results = []
     for pair in PAIRS:
-        wait(copies[3 * pair : 3 * pair + 3])
+        wait(copies[6 * pair : 6 * pair + 6])
         across = dot_nt(g[:, pair_columns(pair)], diagonal(prefix, pair))
         for h in range(2):
-            cols = head_columns(2 * pair + h)
+            head = 2 * pair + h
+            cols = head_columns(head)
             part = across[:, h * DH : (h + 1) * DH]
             mixing0, mixing1 = by_keys(before, g[:, cols], v[:, cols])
+            turned0, turned1 = by_queries(behind, v[:, cols], g[:, cols])
+            total = dot(last[pl.ds(head * BLOCK, BLOCK), :], g[BOTTOM, cols])
+            first_total = total[TOP] + dot(first[pl.ds(head * HALF, HALF), :], g[TOP, cols])
+            value_part[TOP, cols] = first_total.astype(BF16)
+            value_part[BOTTOM, cols] = total[BOTTOM].astype(BF16)
             total = part + dot(mixing0, k[TOP, cols])
             result[TOP, cols] = total[TOP].astype(BF16)
             result[BOTTOM, cols] = (total[BOTTOM] + dot(mixing1, k[BOTTOM, cols])).astype(BF16)
+            total = dot(turned1, q[BOTTOM, cols])
+            key_part[TOP, cols] = (total[TOP] + dot(turned0, q[TOP, cols])).astype(BF16)
+            key_part[BOTTOM, cols] = total[BOTTOM].astype(BF16)
+        cols = pair_columns(pair)
         results += copies_of(
-            [(result.at[:, pair_columns(pair)], query_grad.at[:, pair_window(core, side, pair)])],
-            out_sems.at[pl.ds(pair, 1)],
+            [
+                (result.at[:, cols], query_grad.at[:, pair_window(core, side, pair)]),
+                (key_part.at[:, cols], key_far.at[:, cols]),
+                (value_part.at[:, cols], value_far.at[:, cols]),
+            ],
+            out_sems.at[pl.ds(3 * pair, 3)],
         )
     wait(results)
 
 
-def query_gradient(side, core, keys, values, g, prefix, result=()):
-    return call(
-        f"query{side}",
-        functools.partial(query_body, side),
-        [SMEM, HBM, HBM, HBM, VMEM] + [HBM] * len(result),
-        HBM,
-        WHOLE,
-        4 * BLOCK * BLOCK * SIDE,
-        4 * MIB,
+def middle_gradients(side, core, queries, keys, values, g, turned, prefix, result=()):
+    return call(
+        f"middle{side}",
+        functools.partial(middle_body, side),
+        [SMEM] + [HBM] * 6 + [VMEM] + [HBM] * len(result),
+        [HBM] * 3,
+        [WHOLE, FAR_BF16, FAR_BF16],
+        9 * BLOCK * BLOCK * SIDE,
+        10 * MIB,
         [BUFFER_BF16] * 4
-        + [pltpu.SemaphoreType.DMA((3 * PAIRS_SIDE,)), pltpu.SemaphoreType.DMA((PAIRS_SIDE,))],
-        {5 + i: i for i in range(len(result))},
-    )(core, keys, values, g, prefix, *result)
-
-
-def part_body(side, core, q_all, v_all, g_far, first_far, last_far, key_far, value_far, *refs):
-    q, v, g, first, last, key_part, value_part, sems, out_sems = refs
-    behind = seen_queries()
-    copies = copies_of(
-        [
-            (source.at[:, window], target.at[:, pair_columns(pair)])
-            for pair in PAIRS
-            for source, target, window in (
-                (q_all, q, pair_window(core, side, pair)),
-                (v_all, v, pair_window(core, side, pair)),
-                (g_far, g, pair_columns(pair)),
-            )
-        ]
-        + [
-            (source.at[rows(pair)], target.at[rows(pair)])
-            for pair in PAIRS
-            for source, target, rows in ((first_far, first, first_rows), (last_far, last, last_rows))
-        ],
-        sems,
-    )
-    results = []
-    for pair in PAIRS:
-        wait(copies[3 * pair : 3 * pair + 3])
-        wait(copies[3 * PAIRS_SIDE + 2 * pair : 3 * PAIRS_SIDE + 2 * pair + 2])
-        for head in (2 * pair, 2 * pair + 1):
-            cols = head_columns(head)
-            mixing0, mixing1 = by_queries(behind, v[:, cols], g[:, cols])
-            total = dot(last[pl.ds(head * BLOCK, BLOCK), :], g[BOTTOM, cols])
-            value_part[TOP, cols] = total[TOP] + dot(first[pl.ds(head * HALF, HALF), :], g[TOP, cols])
-            value_part[BOTTOM, cols] = total[BOTTOM]
-            total = dot(mixing1, q[BOTTOM, cols])
-            key_part[TOP, cols] = total[TOP] + dot(mixing0, q[TOP, cols])
-            key_part[BOTTOM, cols] = total[BOTTOM]
-        cols = pair_columns(pair)
-        results += copies_of(
-            [(key_part.at[:, cols], key_far.at[:, cols]), (value_part.at[:, cols], value_far.at[:, cols])],
-            out_sems.at[pl.ds(2 * pair, 2)],
-        )
-    wait(results)
-
-
-def key_value_parts(side, core, queries, values, g, turned):
-    return call(
-        f"part{side}",
-        functools.partial(part_body, side),
-        [SMEM] + [HBM] * 5,
-        [HBM] * 2,
-        [FAR_F32, FAR_F32],
-        5 * BLOCK * BLOCK * SIDE,
-        10 * MIB,
-        [BUFFER_BF16] * 3
         + [FIRST_BUFFER, LAST_BUFFER]
-        + [BUFFER_F32] * 2
-        + [pltpu.SemaphoreType.DMA((5 * PAIRS_SIDE,)), pltpu.SemaphoreType.DMA((2 * PAIRS_SIDE,))],
-    )(core, queries, values, g, *turned)
+        + [BUFFER_BF16] * 3
+        + [pltpu.SemaphoreType.DMA((6 * PAIRS_SIDE,)), pltpu.SemaphoreType.DMA((3 * PAIRS_SIDE,))],
+        {8 + i: i for i in range(len(result))},
+    )(core, queries, keys, values, g, *turned, prefix, *result)
 
 
 def last_body(side, core, *refs):
@@ -511,8 +472,10 @@
         if side == 0:
             wait(copies[4 * pair : 4 * pair + 4])
         states = diagonal(later, pair)
-        key_half[:, cols] = (key_part[:, cols] + dot_nt(v[:, cols], states)).astype(BF16)
-        value_half[:, cols] = (value_part[:, cols] + dot(k[:, cols], states)).astype(BF16)
+        key_total = key_part[:, cols].astype(F32) + dot_nt(v[:, cols], states)
+        value_total = value_part[:, cols].astype(F32) + dot(k[:, cols], states)
+        key_half[:, cols] = key_total.astype(BF16)
+        value_half[:, cols] = value_total.astype(BF16)
         window = pair_window(core, side, pair)
         results += copies_of(
             [(key_half.at[:, cols], key_grad.at[:, window]), (value_half.at[:, cols], value_grad.at[:, window])],
@@ -529,10 +492,10 @@
         functools.partial(last_body, 0),
         [SMEM] + [HBM] * 6 + [VMEM] * 2,
         [HBM, HBM] + [VMEM] * 4,
-        [WHOLE, WHOLE, SIDE_BF16, SIDE_BF16, SIDE_F32, SIDE_F32],
+        [WHOLE, WHOLE, SIDE_BF16, SIDE_BF16, SIDE_BF16, SIDE_BF16],
         4 * BLOCK * SIDE * DH,
-        12 * MIB,
-        [BUFFER_BF16, BUFFER_BF16, BUFFER_F32, BUFFER_F32, BUFFER_BF16, BUFFER_BF16]
+        10 * MIB,
+        [BUFFER_BF16] * 6
         + [pltpu.SemaphoreType.DMA((4 * PAIRS_SIDE + 4,)), pltpu.SemaphoreType.DMA((2 * PAIRS_SIDE,))],
     )(core, keys, values, *part, *part1, base, near)
 
@@ -627,13 +590,13 @@
     g0, state0 = local_grad(0, core, q0, output0, o0, gain, stats)
     parts = exchange((state0 + near0).reshape(CHIPS, SLICE, DH))
     near1 = swap(state0)
-    part0 = key_value_parts(0, core, query_rows, value_rows, g0, turned0)
-    query_grad = query_gradient(0, core, key_rows, value_rows, g0, prefix0)
-    sums = chip_scan(after(parts, *part0, query_grad), True)
+    query_grad, *part0 = middle_gradients(0, core, *everything, g0, turned0, prefix0)
+    sums = chip_scan(after(parts, *part0), True)
     base0 = exchange(sums).reshape(ROWS, DH)
-    part1 = key_value_parts(1, core, query_rows, value_rows, g1, turned1)
-    query_grad = query_gradient(1, core, key_rows, value_rows, g1, prefix1, (query_grad,))
-    base0 = after(base0, *part1, query_grad)
+    query_grad, *part1 = middle_gradients(
+        1, core, *everything, g1, turned1, prefix1, (query_grad,)
+    )
+    base0 = after(base0, *part1)
     base1 = swap(base0)
     key_grad, value_grad, *rest = last_own(core, key_rows, value_rows, part0, part1, base0, near0)
     key_grad, value_grad = last_other(core, *rest, base1, near1, key_grad, value_grad)

time: 105 us -> 99 us (0.943)
  Pallas kernels: 56.2 us -> 47.1 us
  waiting for transfers between devices: 10.4 us -> 14.1 us
    pallas_call x16 -> x14, Pallas kernels: 56.2 us -> 47.1 us  [run(): kernel(*(pltpu.with_memory_space_constraint(array, pltpu.HBM) if spec is...]
    all_to_all x4, waiting for transfers between devices: 8.63 us -> 12.4 us  [exchange(): lax.all_to_all(parts, 'ctx', 0, 0, axis_index_groups=SAME_CORE, tiled=True)]
    all_to_all x4, starting transfers between devices: 20.6 us -> 17.6 us  [exchange(): lax.all_to_all(parts, 'ctx', 0, 0, axis_index_groups=SAME_CORE, tiled=True)]
    ppermute x6, starting transfers between devices: 8.29 us -> 11.1 us  [swap(): return lax.ppermute(part, 'ctx', PARTNERS)]
  transfers between devices with their start and end apart: 13 -> 13, of which waited for: 4 -> 6; matrix products, arithmetic and copies ran while one was open for 0% -> 0% of each run, Pallas kernels for 46% -> 39%
where the time goes in v3:
time: 99 us; the launch traced here: 98.4 us
  Pallas kernels  47.1 us (48%)
  starting transfers between devices  34.4 us (35%)
  waiting for transfers between devices  14.1 us (14%)
  other arithmetic  1.7 us (2%)
  between operations  1.01 us (1%)
    pallas_call x14, Pallas kernels, run(): kernel(*(pltpu.with_memory_space_constraint(array, pltpu.HBM) if spec is...  47.1 us
    all_to_all x4, starting transfers between devices, exchange(): lax.all_to_all(parts, 'ctx', 0, 0, axis_index_groups=SAME_CORE, tiled=True)  17.6 us
    all_to_all x4, waiting for transfers between devices, exchange(): lax.all_to_all(parts, 'ctx', 0, 0, axis_index_groups=SAME_CORE, tiled=True)  12.4 us
    ppermute x6, starting transfers between devices, swap(): return lax.ppermute(part, 'ctx', PARTNERS)  11.1 us
    ppermute x3, starting transfers between devices, along_heads(): lax.ppermute(stats, 'head', [(i, (i + hop) % 4) for i in range(4)])  5.74 us
  transfers between devices with their start and end apart: 13, of which 6 were waited for; matrix products, arithmetic and copies ran while one was open for 0% of the time, Pallas kernels for 39%

profile of v3, /device:TPU:1, one launch (start us, length us, event | category | flops | bytes accessed | tf_op | source)
XLA Modules:
  0.0 98.4 jit_solution(3392066495817163467)
XLA Ops:
  0.6 2.4 %state1.1 = f32[1024,128]{1,0:T(8,128)S(1)} custom-call(s32[1]{0:T(128)} %bitcast.core, bf16[512,2048]{1,0:T(8,128)(2,1)} %refs_0_.3, bf16[512,2048]{1,0:T(8,128)(2,1)} %refs_1_.3), custom_call_target="tpu_custom_call" | custom-call | flops 134217728 | bytes 2097152 | tf_op jit(solution)/shard_map/state1/pallas_call | solution.py:80
  3.0 1.5 %collective-permute-start = (f32[1024,128]{1,0:T(8,128)S(1)}, f32[1024,128]{1,0:T(8,128)S(1)}, u32[]{:S(2)}, u32[]{:S(2)}) collective-permute-start(f32[1024,128]{1,0:T(8,128)S(1)} %state1.1), channel_id=1, source_target_pairs={{0,4},{4,0},{8,12},{12,8},{16,20},{20,16},{24,28},{28,24},{32,36},... | collective-permute-start | bytes 1572872 | tf_op jit(solution)/shard_map/ppermute | solution.py:548
  4.5 2.4 %state0.1 = f32[1024,128]{1,0:T(8,128)S(1)} custom-call(s32[1]{0:T(128)} %bitcast.core, bf16[512,2048]{1,0:T(8,128)(2,1)} %refs_0_.3, bf16[512,2048]{1,0:T(8,128)(2,1)} %refs_1_.3), custom_call_target="tpu_custom_call" | custom-call | flops 134217728 | bytes 2097152 | tf_op jit(solution)/shard_map/state0/pallas_call | solution.py:80
  6.9 0.0 collective-permute-done.refs_6_
  6.9 0.8 add.11
  7.7 6.8 %all-to-all-start = ((f32[16,64,128]{2,1,0:T(8,128)}), f32[16,64,128]{2,1,0:T(8,128)S(1)}, u32[]{:S(2)}, u32[]{:S(2)}) async-start(f32[16,64,128]{2,1,0:T(8,128)} %bitcast.2), calls=%async_computation | async-start | bytes 1048576 | tf_op jit(solution)/shard_map/all_to_all | solution.py:544
  14.6 5.5 %intra0.1 = (f32[512,1024]{1,0:T(8,128)}, bf16[2048,256]{1,0:T(8,128)(2,1)}, bf16[4096,256]{1,0:T(8,128)(2,1)}) custom-call(s32[1]{0:T(128)} %bitcast.core, bf16[512,2048]{1,0:T(8,128)(2,1)} %q_all.7, bf16[512,2048]{1,0:T(8,128)(2,1)} %refs_0_.3, bf16[512,2048]{1,0:T(8,128)(2,1)} %refs_1_.3), custom_call_target="tpu_custom_call" | custom-call | flops 1342177280 | bytes 8388608 | tf_op jit(solution)/shard_map/intra0/pallas_call | solution.py:80
  20.1 5.5 %all-to-all-done.parts = f32[16,64,128]{2,1,0:T(8,128)S(1)} async-done(((f32[16,64,128]{2,1,0:T(8,128)}), f32[16,64,128]{2,1,0:T(8,128)S(1)}, u32[]{:S(2)}, u32[]{:S(2)}) %all-to-all-start) | async-done | bytes 524320 | tf_op jit(solution)/shard_map/all_to_all | solution.py:544
  25.7 0.8 scan0.1
  26.5 3.6 %all-to-all-start.1 = ((f32[16,64,128]{2,1,0:T(8,128)}), f32[16,64,128]{2,1,0:T(8,128)S(1)}, u32[]{:S(2)}, u32[]{:S(2)}) async-start(f32[16,64,128]{2,1,0:T(8,128)} %scan0.1), calls=%async_computation.1 | async-start | bytes 1048576 | tf_op jit(solution)/shard_map/all_to_all | solution.py:544
  30.1 0.0 copy-start
  30.1 1.5 %collective-permute-start.2 = (f32[1024,128]{1,0:T(8,128)S(1)}, f32[1024,128]{1,0:T(8,128)S(1)}, u32[]{:S(2)}, u32[]{:S(2)}) collective-permute-start(f32[1024,128]{1,0:T(8,128)S(1)} %state0.1), channel_id=1, source_target_pairs={{0,4},{4,0},{8,12},{12,8},{16,20},{20,16},{24,28},{28,24},{32,36},... | collective-permute-start | bytes 1572872 | tf_op jit(solution)/shard_map/ppermute | solution.py:548
  31.6 5.5 %intra1.1 = (f32[512,1024]{1,0:T(8,128)}, bf16[2048,256]{1,0:T(8,128)(2,1)}, bf16[4096,256]{1,0:T(8,128)(2,1)}) custom-call(s32[1]{0:T(128)} %bitcast.core, bf16[512,2048]{1,0:T(8,128)(2,1)} %q_all.7, bf16[512,2048]{1,0:T(8,128)(2,1)} %refs_0_.3, bf16[512,2048]{1,0:T(8,128)(2,1)} %refs_1_.3), custom_call_target="tpu_custom_call" | custom-call | flops 1342177280 | bytes 8388608 | tf_op jit(solution)/shard_map/intra1/pallas_call | solution.py:80
  37.2 3.1 %all-to-all-done.1 = f32[16,64,128]{2,1,0:T(8,128)S(1)} async-done(((f32[16,64,128]{2,1,0:T(8,128)}), f32[16,64,128]{2,1,0:T(8,128)S(1)}, u32[]{:S(2)}, u32[]{:S(2)}) %all-to-all-start.1) | async-done | bytes 524320 | tf_op jit(solution)/shard_map/all_to_all | solution.py:544
  40.3 2.3 %collective-permute-start.1 = (f32[1024,128]{1,0:T(8,128)S(1)}, f32[1024,128]{1,0:T(8,128)S(1)}, u32[]{:S(2)}, u32[]{:S(2)}) collective-permute-start(f32[1024,128]{1,0:T(8,128)S(1)} %bitcast.8), channel_id=1, source_target_pairs={{0,4},{4,0},{8,12},{12,8},{16,20},{20,16},{24,28},{28,24},{32,36},... | collective-permute-start | bytes 1572872 | tf_op jit(solution)/shard_map/ppermute | solution.py:548
  42.6 0.0 copy-done
  42.6 3.7 %output0.1 = (bf16[512,1024]{1,0:T(8,128)(2,1)S(1)}, bf16[512,1024]{1,0:T(8,128)(2,1)S(1)}, f32[512,1024]{1,0:T(8,128)S(1)}, bf16[1024,128]{1,0:T(8,128)(2,1)S(1...) custom-call(s32[1]{0:T(128)} %bitcast.core, ...), custom_call_target="tpu_custom_call" | custom-call | flops 134217728 | bytes 8388608 | tf_op jit(solution)/shard_map/output0/pallas_call | solution.py:80
  46.3 0.0 collective-permute-done.2.refs_5_
  46.3 0.0 collective-permute-done.1.refs_4_
  46.3 1.0 %output1.1 = (f32[512,1024]{1,0:T(8,128)S(1)}, bf16[1024,128]{1,0:T(8,128)(2,1)S(1)}, f32[2,512]{1,0:T(2,128)S(1)}) custom-call(s32[1]{0:T(128)} %bitcast.core, bf16[512,1024]{1,0:T(8,128)(2,1)S(1)} %get-tuple-element.47.refs_0_.q, bf16[512,1024]{1,0:T(8,128)(2,1)S(1)} %get-tuple-element.48.refs_1_.o, f32[512,1024]{1,0:T(8,128)S(1)} %get-tuple-element.49.refs_2_, ...), custom_call_target="tpu_custom_call" | custom-call | flops 134217728 | bytes 1048576 | tf_op jit(solution)/shard_map/output1/pallas_call | solution.py:80
  47.3 1.7 %collective-permute-start.3 = (f32[2,512]{1,0:T(2,128)S(1)}, f32[2,512]{1,0:T(2,128)S(1)}, u32[]{:S(2)}, u32[]{:S(2)}) collective-permute-start(f32[2,512]{1,0:T(2,128)S(1)} %get-tuple-element.53.s0), channel_id=1, source_target_pairs={{0,1},{1,2},{2,3},{3,0},{4,5},{5,6},{6,7},{7,4},{8,9},{9,10},{10,1... | collective-permute-start | bytes 12296 | tf_op jit(solution)/shard_map/ppermute | solution.py:553
  49.0 3.3 %collective-permute-start.4 = (f32[2,512]{1,0:T(2,128)S(1)}, f32[2,512]{1,0:T(2,128)S(1)}, u32[]{:S(2)}, u32[]{:S(2)}) collective-permute-start(f32[2,512]{1,0:T(2,128)S(1)} %get-tuple-element.53.s0), channel_id=1, source_target_pairs={{0,2},{1,3},{2,0},{3,1},{4,6},{5,7},{6,4},{7,5},{8,10},{9,11},{10,... | collective-permute-start | bytes 12296 | tf_op jit(solution)/shard_map/ppermute | solution.py:553
  52.3 0.7 collective-permute-start.5
  53.0 0.0 collective-permute-done.3.s1
  53.0 0.3 collective-permute-done.4.s2
  53.3 1.4 %collective-permute-done.5.s3 = f32[2,512]{1,0:T(2,128)S(1)} collective-permute-done((f32[2,512]{1,0:T(2,128)S(1)}, f32[2,512]{1,0:T(2,128)S(1)}, u32[]{:S(2)}, u32[]{:S(2)}) %collective-permute-start.5) | collective-permute-done | bytes 4128 | tf_op jit(solution)/shard_map/ppermute | solution.py:553
  54.8 1.5 %grad1.1 = (bf16[512,1024]{1,0:T(8,128)(2,1)}, f32[1024,128]{1,0:T(8,128)S(1)}) custom-call(s32[1]{0:T(128)} %bitcast.core, bf16[512,1024]{1,0:T(8,128)(2,1)S(1)} %get-tuple-element.47.refs_0_.q, f32[512,1024]{1,0:T(8,128)S(1)} %get-tuple-element.52.output, bf16[512,1024]{1,0:T(8,128)(2,1)S(1)} %get-tuple-element.48.refs_1_.o, f32[1,2048]{1,0:T(1,128)S(1)} %bitcast.12, ...), custom_call_target="tpu_custom_call" | custom-call | flops 134217728 | bytes 1048576 | tf_op jit(solution)/shard_map/grad1/pallas_call | solution.py:80
  56.3 1.8 %collective-permute-start.6 = (f32[1024,128]{1,0:T(8,128)S(1)}, f32[1024,128]{1,0:T(8,128)S(1)}, u32[]{:S(2)}, u32[]{:S(2)}) collective-permute-start(f32[1024,128]{1,0:T(8,128)S(1)} %get-tuple-element.72), channel_id=1, source_target_pairs={{0,4},{4,0},{8,12},{12,8},{16,20},{20,16},{24,28},{28,24},{32,36},... | collective-permute-start | bytes 1572872 | tf_op jit(solution)/shard_map/ppermute | solution.py:548
  58.1 1.6 %grad0.1 = (bf16[512,1024]{1,0:T(8,128)(2,1)}, f32[1024,128]{1,0:T(8,128)S(1)}) custom-call(s32[1]{0:T(128)} %bitcast.core, bf16[512,1024]{1,0:T(8,128)(2,1)S(1)} %get-tuple-element.58.q, f32[512,1024]{1,0:T(8,128)S(1)} %get-tuple-element.59.output, bf16[512,1024]{1,0:T(8,128)(2,1)S(1)} %get-tuple-element.60.o, f32[1,2048]{1,0:T(1,128)S(1)} %bitcast.13, ...), custom_call_target="tpu_custom_call" | custom-call | flops 134217728 | bytes 1048576 | tf_op jit(solution)/shard_map/grad0/pallas_call | solution.py:80
  59.7 0.0 collective-permute-done.6.refs_7_
  59.7 0.8 add.12
  60.5 3.6 %all-to-all-start.2 = ((f32[16,64,128]{2,1,0:T(8,128)}), f32[16,64,128]{2,1,0:T(8,128)S(1)}, u32[]{:S(2)}, u32[]{:S(2)}) async-start(f32[16,64,128]{2,1,0:T(8,128)} %bitcast.4), calls=%async_computation.2 | async-start | bytes 1048576 | tf_op jit(solution)/shard_map/all_to_all | solution.py:544
  64.1 7.8 %middle0.1 = (bf16[512,2048]{1,0:T(8,128)(2,1)}, bf16[512,1024]{1,0:T(8,128)(2,1)}, bf16[512,1024]{1,0:T(8,128)(2,1)}) custom-call(s32[1]{0:T(128)} %bitcast.core, bf16[512,2048]{1,0:T(8,128)(2,1)} %q_all.7, bf16[512,2048]{1,0:T(8,128)(2,1)} %refs_0_.3, bf16[512,2048]{1,0:T(8,128)(2,1)} %refs_1_.3, bf16[512,1024]{1,0:T(8,128)(2,1)} %get-tuple-element.61.g_far, ...), custom_call_target="tpu_custom_call" | custom-call | flops 2415919104 | bytes 10485760 | tf_op jit(solution)/shard_map/middle0/pallas_call | solution.py:80
  71.9 3.2 %all-to-all-done.2.parts = f32[16,64,128]{2,1,0:T(8,128)S(1)} async-done(((f32[16,64,128]{2,1,0:T(8,128)}), f32[16,64,128]{2,1,0:T(8,128)S(1)}, u32[]{:S(2)}, u32[]{:S(2)}) %all-to-all-start.2) | async-done | bytes 524320 | tf_op jit(solution)/shard_map/all_to_all | solution.py:544
  75.1 0.8 scan1.1
  76.0 3.6 %all-to-all-start.3 = ((f32[16,64,128]{2,1,0:T(8,128)}), f32[16,64,128]{2,1,0:T(8,128)S(1)}, u32[]{:S(2)}, u32[]{:S(2)}) async-start(f32[16,64,128]{2,1,0:T(8,128)} %scan1.1), calls=%async_computation.3 | async-start | bytes 1048576 | tf_op jit(solution)/shard_map/all_to_all | solution.py:544
  79.6 1.7 %collective-permute-start.8 = (f32[1024,128]{1,0:T(8,128)S(1)}, f32[1024,128]{1,0:T(8,128)S(1)}, u32[]{:S(2)}, u32[]{:S(2)}) collective-permute-start(f32[1024,128]{1,0:T(8,128)S(1)} %get-tuple-element.71), channel_id=1, source_target_pairs={{0,4},{4,0},{8,12},{12,8},{16,20},{20,16},{24,28},{28,24},{32,36},... | collective-permute-start | bytes 1572872 | tf_op jit(solution)/shard_map/ppermute | solution.py:548
  81.3 7.8 %middle1.1 = (bf16[512,2048]{1,0:T(8,128)(2,1)}, bf16[512,1024]{1,0:T(8,128)(2,1)}, bf16[512,1024]{1,0:T(8,128)(2,1)}) custom-call(s32[1]{0:T(128)} %bitcast.core, bf16[512,2048]{1,0:T(8,128)(2,1)} %q_all.7, bf16[512,2048]{1,0:T(8,128)(2,1)} %refs_0_.3, bf16[512,2048]{1,0:T(8,128)(2,1)} %refs_1_.3, ...), custom_call_target="tpu_custom_call", output_to_operand_aliasing={{0}: (8, {})} | custom-call | flops 2415919104 | bytes 10485760 | tf_op jit(solution)/shard_map/middle1/pallas_call | solution.py:80
  89.1 0.6 all-to-all-done.3
  89.7 2.3 %collective-permute-start.7 = (f32[1024,128]{1,0:T(8,128)S(1)}, f32[1024,128]{1,0:T(8,128)S(1)}, u32[]{:S(2)}, u32[]{:S(2)}) collective-permute-start(f32[1024,128]{1,0:T(8,128)S(1)} %bitcast.6), channel_id=1, source_target_pairs={{0,4},{4,0},{8,12},{12,8},{16,20},{20,16},{24,28},{28,24},{32,36},... | collective-permute-start | bytes 1572872 | tf_op jit(solution)/shard_map/ppermute | solution.py:548
  92.0 4.5 %last0.1 = (bf16[512,2048]{1,0:T(8,128)(2,1)}, bf16[512,2048]{1,0:T(8,128)(2,1)}, bf16[512,1024]{1,0:T(8,128)(2,1)S(1)}, bf16[512,1024]{1,0:T(8,128)(2,1)S(1)}, ...) custom-call(s32[1]{0:T(128)} %bitcast.core, bf16[512,2048]{1,0:T(8,128)(2,1)} %refs_0_.3, ...), custom_call_target="tpu_custom_call" | custom-call | flops 268435456 | bytes 10485760 | tf_op jit(solution)/shard_map/last0/pallas_call | solution.py:80
  96.5 0.0 collective-permute-done.8.refs_5_
  96.5 0.0 collective-permute-done.7.refs_4_
  96.5 1.7 %last1.1 = (bf16[512,2048]{1,0:T(8,128)(2,1)}, bf16[512,2048]{1,0:T(8,128)(2,1)}) custom-call(s32[1]{0:T(128)} %bitcast.core, bf16[512,1024]{1,0:T(8,128)(2,1)S(1)} %get-tuple-element.75.refs_0_, bf16[512,1024]{1,0:T(8,128)(2,1)S(1)} %get-tuple-element.76.refs_1_, ...), custom_call_target="tpu_custom_call", output_to_operand_aliasing={{0}: (7, {}), {1}: (8, {})} | custom-call | flops 268435456 | bytes 2097152 | tf_op jit(solution)/shard_map/last1/pallas_call | solution.py:80
Async XLA Ops:
  3.0 3.9 %collective-permute-start = (f32[1024,128]{1,0:T(8,128)S(1)}, f32[1024,128]{1,0:T(8,128)S(1)}, u32[]{:S(2)}, u32[]{:S(2)}) collective-permute-start(f32[1024,128]{1,0:T(8,128)S(1)} %state1.1), channel_id=1, source_target_pairs={{0,4},{4,0},{8,12},{12,8},{16,20},{20,16},{24,28},{28,24},{32,36},... | collective-permute-start | bytes 1572872 | tf_op jit(solution)/shard_map/ppermute | solution.py:548
  7.7 17.9 %all-to-all-start = ((f32[16,64,128]{2,1,0:T(8,128)}), f32[16,64,128]{2,1,0:T(8,128)S(1)}, u32[]{:S(2)}, u32[]{:S(2)}) async-start(f32[16,64,128]{2,1,0:T(8,128)} %bitcast.2), calls=%async_computation | async-start | bytes 1048576 | tf_op jit(solution)/shard_map/all_to_all | solution.py:544
  26.5 13.8 %all-to-all-start.1 = ((f32[16,64,128]{2,1,0:T(8,128)}), f32[16,64,128]{2,1,0:T(8,128)S(1)}, u32[]{:S(2)}, u32[]{:S(2)}) async-start(f32[16,64,128]{2,1,0:T(8,128)} %scan0.1), calls=%async_computation.1 | async-start | bytes 1048576 | tf_op jit(solution)/shard_map/all_to_all | solution.py:544
  30.1 12.5 %copy-start = (f32[2048]{0:T(1024)S(1)}, f32[2048]{0:T(1024)}, u32[]{:S(2)}) copy-start(f32[2048]{0:T(1024)} %param.9) | copy-start | bytes 24580
  30.1 16.1 %collective-permute-start.2 = (f32[1024,128]{1,0:T(8,128)S(1)}, f32[1024,128]{1,0:T(8,128)S(1)}, u32[]{:S(2)}, u32[]{:S(2)}) collective-permute-start(f32[1024,128]{1,0:T(8,128)S(1)} %state0.1), channel_id=1, source_target_pairs={{0,4},{4,0},{8,12},{12,8},{16,20},{20,16},{24,28},{28,24},{32,36},... | collective-permute-start | bytes 1572872 | tf_op jit(solution)/shard_map/ppermute | solution.py:548
  40.3 6.0 %collective-permute-start.1 = (f32[1024,128]{1,0:T(8,128)S(1)}, f32[1024,128]{1,0:T(8,128)S(1)}, u32[]{:S(2)}, u32[]{:S(2)}) collective-permute-start(f32[1024,128]{1,0:T(8,128)S(1)} %bitcast.8), channel_id=1, source_target_pairs={{0,4},{4,0},{8,12},{12,8},{16,20},{20,16},{24,28},{28,24},{32,36},... | collective-permute-start | bytes 1572872 | tf_op jit(solution)/shard_map/ppermute | solution.py:548
  47.3 5.7 %collective-permute-start.3 = (f32[2,512]{1,0:T(2,128)S(1)}, f32[2,512]{1,0:T(2,128)S(1)}, u32[]{:S(2)}, u32[]{:S(2)}) collective-permute-start(f32[2,512]{1,0:T(2,128)S(1)} %get-tuple-element.53.s0), channel_id=1, source_target_pairs={{0,1},{1,2},{2,3},{3,0},{4,5},{5,6},{6,7},{7,4},{8,9},{9,10},{10,1... | collective-permute-start | bytes 12296 | tf_op jit(solution)/shard_map/ppermute | solution.py:553
  49.0 4.3 %collective-permute-start.4 = (f32[2,512]{1,0:T(2,128)S(1)}, f32[2,512]{1,0:T(2,128)S(1)}, u32[]{:S(2)}, u32[]{:S(2)}) collective-permute-start(f32[2,512]{1,0:T(2,128)S(1)} %get-tuple-element.53.s0), channel_id=1, source_target_pairs={{0,2},{1,3},{2,0},{3,1},{4,6},{5,7},{6,4},{7,5},{8,10},{9,11},{10,... | collective-permute-start | bytes 12296 | tf_op jit(solution)/shard_map/ppermute | solution.py:553
  52.3 2.5 %collective-permute-start.5 = (f32[2,512]{1,0:T(2,128)S(1)}, f32[2,512]{1,0:T(2,128)S(1)}, u32[]{:S(2)}, u32[]{:S(2)}) collective-permute-start(f32[2,512]{1,0:T(2,128)S(1)} %get-tuple-element.53.s0), channel_id=1, source_target_pairs={{0,3},{1,0},{2,1},{3,2},{4,7},{5,4},{6,5},{7,6},{8,11},{9,8},{10,9... | collective-permute-start | bytes 12296 | tf_op jit(solution)/shard_map/ppermute | solution.py:553
  56.3 3.4 %collective-permute-start.6 = (f32[1024,128]{1,0:T(8,128)S(1)}, f32[1024,128]{1,0:T(8,128)S(1)}, u32[]{:S(2)}, u32[]{:S(2)}) collective-permute-start(f32[1024,128]{1,0:T(8,128)S(1)} %get-tuple-element.72), channel_id=1, source_target_pairs={{0,4},{4,0},{8,12},{12,8},{16,20},{20,16},{24,28},{28,24},{32,36},... | collective-permute-start | bytes 1572872 | tf_op jit(solution)/shard_map/ppermute | solution.py:548
  60.5 14.6 %all-to-all-start.2 = ((f32[16,64,128]{2,1,0:T(8,128)}), f32[16,64,128]{2,1,0:T(8,128)S(1)}, u32[]{:S(2)}, u32[]{:S(2)}) async-start(f32[16,64,128]{2,1,0:T(8,128)} %bitcast.4), calls=%async_computation.2 | async-start | bytes 1048576 | tf_op jit(solution)/shard_map/all_to_all | solution.py:544
  76.0 13.7 %all-to-all-start.3 = ((f32[16,64,128]{2,1,0:T(8,128)}), f32[16,64,128]{2,1,0:T(8,128)S(1)}, u32[]{:S(2)}, u32[]{:S(2)}) async-start(f32[16,64,128]{2,1,0:T(8,128)} %scan1.1), calls=%async_computation.3 | async-start | bytes 1048576 | tf_op jit(solution)/shard_map/all_to_all | solution.py:544
  79.6 17.0 %collective-permute-start.8 = (f32[1024,128]{1,0:T(8,128)S(1)}, f32[1024,128]{1,0:T(8,128)S(1)}, u32[]{:S(2)}, u32[]{:S(2)}) collective-permute-start(f32[1024,128]{1,0:T(8,128)S(1)} %get-tuple-element.71), channel_id=1, source_target_pairs={{0,4},{4,0},{8,12},{12,8},{16,20},{20,16},{24,28},{28,24},{32,36},... | collective-permute-start | bytes 1572872 | tf_op jit(solution)/shard_map/ppermute | solution.py:548
  89.7 6.8 %collective-permute-start.7 = (f32[1024,128]{1,0:T(8,128)S(1)}, f32[1024,128]{1,0:T(8,128)S(1)}, u32[]{:S(2)}, u32[]{:S(2)}) collective-permute-start(f32[1024,128]{1,0:T(8,128)S(1)} %bitcast.6), channel_id=1, source_target_pairs={{0,4},{4,0},{8,12},{12,8},{16,20},{20,16},{24,28},{28,24},{32,36},... | collective-permute-start | bytes 1572872 | tf_op jit(solution)/shard_map/ppermute | solution.py:548

commit v4 on v3

v4 whole, which is shorter than its diff:
```python
import functools

import jax
import jax.numpy as jnp
from jax import lax
from jax.experimental import pallas as pl
from jax.experimental.pallas import tpu as pltpu
from jax.sharding import PartitionSpec as P

DH = 128
BLOCK = 512
HALF = 256
WIDTH = 2048
SIDE = WIDTH // 2
WIDTH_ALL = 8192
HEADS_SIDE = SIDE // DH
PAIRS_SIDE = HEADS_SIDE // 2
ROWS = HEADS_SIDE * DH
LINE = 4
QUARTER = ROWS // LINE
MIB = 1024 * 1024

epsilon = 1e-06

F32 = jnp.float32
BF16 = jnp.bfloat16

VMEM = pl.BlockSpec(memory_space=pltpu.VMEM)
SMEM = pl.BlockSpec(memory_space=pltpu.SMEM)
HBM = pl.BlockSpec(memory_space=pltpu.HBM)


def hbm(dims, kind):
    return pltpu.HBM(dims, kind)


SIDE_F32 = jax.ShapeDtypeStruct((BLOCK, SIDE), F32)
SIDE_BF16 = jax.ShapeDtypeStruct((BLOCK, SIDE), BF16)
STATE = jax.ShapeDtypeStruct((ROWS, DH), F32)
STATE_HALF = jax.ShapeDtypeStruct((ROWS, DH), BF16)
LANES = jax.ShapeDtypeStruct((BLOCK, DH), F32)
STATS = jax.ShapeDtypeStruct((2, BLOCK), F32)
WHOLE = hbm((BLOCK, WIDTH), BF16)
PIECE = jax.ShapeDtypeStruct((QUARTER, DH), F32)
PAIR_F32 = jax.ShapeDtypeStruct((BLOCK, 2 * DH), F32)
FIRST_SCORES = jax.ShapeDtypeStruct((HEADS_SIDE * HALF, HALF), BF16)
LAST_SCORES = jax.ShapeDtypeStruct((HEADS_SIDE * BLOCK, HALF), BF16)
BUFFER_BF16 = pltpu.VMEM((BLOCK, SIDE), BF16)


def copies_of(pairs, sems):
    copies = []
    for place, (source, target) in enumerate(pairs):
        copy = pltpu.make_async_copy(source, target, sems.at[place])
        copy.start()
        copies.append(copy)
    return copies


def wait(copies):
    for copy in copies:
        copy.wait()


def call(name, body, in_specs, out_specs, out_shape, flops, moved, scratch=(), aliases=None):
    kernel = pl.pallas_call(
        body,
        in_specs=in_specs,
        out_specs=out_specs,
        out_shape=out_shape,
        scratch_shapes=list(scratch),
        input_output_aliases=aliases or {},
        compiler_params=pltpu.CompilerParams(vmem_limit_bytes=12 * MIB),
        cost_estimate=pl.CostEstimate(flops=flops, bytes_accessed=moved, transcendentals=0),
        name=name,
    )

    def run(*arrays):
        return kernel(
            *(
                pltpu.with_memory_space_constraint(array, pltpu.HBM) if spec is HBM else array
                for spec, array in zip(in_specs, arrays)
            )
        )

    return run


def dot(a, b):
    return lax.dot_general(a, b, (((1,), (0,)), ((), ())), preferred_element_type=F32)


def dot_nt(a, b):
    return lax.dot_general(a, b, (((1,), (1,)), ((), ())), preferred_element_type=F32)


def dot_tn(a, b):
    return lax.dot_general(a, b, (((0,), (0,)), ((), ())), preferred_element_type=F32)


def pair_columns(pair):
    return slice(pair * 2 * DH, (pair + 1) * 2 * DH)


def head_columns(head):
    return slice(head * DH, (head + 1) * DH)


def diagonal(states, pair):
    first = states[2 * pair * DH : (2 * pair + 1) * DH, :]
    second = states[(2 * pair + 1) * DH : (2 * pair + 2) * DH, :]
    zero = jnp.zeros_like(first)
    return jnp.concatenate(
        [jnp.concatenate([first, zero], axis=1), jnp.concatenate([zero, second], axis=1)], axis=0
    )


def store_states(out, pair, a, b):
    both = dot_tn(a, b)
    out[2 * pair * DH : (2 * pair + 1) * DH, :] = both[:DH, :DH]
    out[(2 * pair + 1) * DH : (2 * pair + 2) * DH, :] = both[DH:, DH:]


def seen_keys():
    rows = lax.broadcasted_iota(jnp.int32, (HALF, HALF), 0)
    cols = lax.broadcasted_iota(jnp.int32, (HALF, HALF), 1)
    return cols <= rows


def seen_queries():
    rows = lax.broadcasted_iota(jnp.int32, (HALF, HALF), 0)
    cols = lax.broadcasted_iota(jnp.int32, (HALF, HALF), 1)
    return cols >= rows


def keep(mask, array):
    return jnp.where(mask, array, 0.0).astype(BF16)


TOP = slice(0, HALF)
BOTTOM = slice(HALF, BLOCK)


def by_keys(mask, queries, keys):
    first = dot_nt(queries, keys[TOP])
    last = dot_nt(queries[BOTTOM], keys[BOTTOM])
    first = jnp.concatenate([keep(mask, first[TOP]), first[BOTTOM].astype(BF16)], axis=0)
    return first, keep(mask, last)


def by_queries(mask, keys, queries):
    first = dot_nt(keys[TOP], queries[TOP])
    last = dot_nt(keys, queries[BOTTOM])
    last = jnp.concatenate([last[TOP].astype(BF16), keep(mask, last[BOTTOM])], axis=0)
    return keep(mask, first), last


def side_start(core, side):
    half = core[0] if side == 0 else 1 - core[0]
    return pl.multiple_of(half * SIDE, SIDE)


def pair_window(core, side, pair):
    return pl.ds(pl.multiple_of(side_start(core, side) + pair * 2 * DH, 2 * DH), 2 * DH)


def head_window(core, side, head):
    return pl.ds(pl.multiple_of(side_start(core, side) + head * DH, DH), DH)


PAIRS = range(PAIRS_SIDE)


def local_state_body(side, core, k_all, v_all, k, v, out, sems):
    window = pl.ds(side_start(core, side), SIDE)
    copies = copies_of(
        [
            (source.at[rows, window], target.at[rows])
            for rows in (pl.ds(0, HALF), pl.ds(HALF, HALF))
            for source, target in ((k_all, k), (v_all, v))
        ],
        sems,
    )
    for part, rows in enumerate((TOP, BOTTOM)):
        wait(copies[2 * part : 2 * part + 2])
        for pair in PAIRS:
            both = dot_tn(k[rows, pair_columns(pair)], v[rows, pair_columns(pair)])
            for h in range(2):
                place = head_columns(2 * pair + h)
                state = both[head_columns(h), head_columns(h)]
                out[place, :] = state if part == 0 else out[place, :] + state


def local_state(side, core, keys, values):
    return call(
        f"state{side}",
        functools.partial(local_state_body, side),
        [SMEM, HBM, HBM],
        [VMEM] * 3,
        [SIDE_BF16, SIDE_BF16, STATE],
        2 * BLOCK * SIDE * DH,
        2 * MIB,
        [pltpu.SemaphoreType.DMA((4,))],
    )(core, keys, values)


def intra_body(side, pairs, core, q_all, o_all, k, v, *refs):
    q, o, out, first, last, sems = refs[-6:]
    before, behind = seen_keys(), seen_queries()
    copies = copies_of(
        [
            (source.at[:, pair_window(core, side, pair)], target.at[:, pair_columns(pair)])
            for source, target in ((q_all, q), (o_all, o))
            for pair in pairs
        ],
        sems,
    )
    for place, pair in enumerate(pairs):
        wait(copies[place : place + 1])
        for head in (2 * pair, 2 * pair + 1):
            cols = head_columns(head)
            queries, keys, values = q[:, cols], k[:, cols], v[:, cols]
            scores0, scores1 = by_keys(before, queries, keys)
            first[pl.ds(head * HALF, HALF), :], last[pl.ds(head * BLOCK, BLOCK), :] = by_queries(
                behind, keys, queries
            )
            total = dot(scores0, values[TOP])
            out[TOP, cols] = total[TOP]
            out[BOTTOM, cols] = total[BOTTOM] + dot(scores1, values[BOTTOM])
    wait(copies[len(pairs) :])


def intra_output(number, side, pairs, core, queries, out_grad, k, v, begun=()):
    return call(
        f"intra{number}",
        functools.partial(intra_body, side, pairs),
        [SMEM, HBM, HBM, VMEM, VMEM] + [VMEM] * len(begun),
        [VMEM] * 5,
        [SIDE_BF16, SIDE_BF16, SIDE_F32, FIRST_SCORES, LAST_SCORES],
        5 * BLOCK * BLOCK * SIDE * len(pairs) // 4,
        2 * MIB * len(pairs),
        [pltpu.SemaphoreType.DMA((2 * len(pairs),))],
        {5 + i: i for i in range(len(begun))},
    )(core, queries, out_grad, k, v, *begun)


def output_body(side, core, q, o, intra, gain, base, near, *refs):
    if side == 0:
        output, prefix_half, squares, products = refs
    else:
        squares_in, products_in, output, prefix_half, stats = refs
    weight = core[0].astype(F32)
    gains = gain[:, pl.ds(side_start(core, side), SIDE)]
    prefix_half[...] = (base[...] + weight * near[...]).astype(BF16)
    parts = (TOP, BOTTOM)
    if side == 0:
        square_sums = [jnp.zeros((HALF, DH), F32) for rows in parts]
        product_sums = [jnp.zeros((HALF, DH), F32) for rows in parts]
    else:
        square_sums = [squares_in[rows, :] for rows in parts]
        product_sums = [products_in[rows, :] for rows in parts]
    for pair in PAIRS:
        cols = pair_columns(pair)
        states = diagonal(prefix_half, pair)
        for part, rows in enumerate(parts):
            value = intra[rows, cols] + dot(q[rows, cols], states)
            output[rows, cols] = value
            terms = o[rows, cols].astype(F32) * gains[:, cols] * value
            value = value * value
            square_sums[part] = square_sums[part] + (value[:, :DH] + value[:, DH:])
            product_sums[part] = product_sums[part] + (terms[:, :DH] + terms[:, DH:])
    for part, rows in enumerate(parts):
        if side == 0:
            squares[rows, :] = square_sums[part]
            products[rows, :] = product_sums[part]
        else:
            stats[0:1, rows] = jnp.sum(square_sums[part].T, axis=0, keepdims=True)
            stats[1:2, rows] = jnp.sum(product_sums[part].T, axis=0, keepdims=True)


def whole_output(side, core, q, o, intra, gain, base, near, sums=()):
    return call(
        f"output{side}",
        functools.partial(output_body, side),
        [SMEM] + [VMEM] * (6 + len(sums)),
        [VMEM] * (4 if side == 0 else 3),
        [SIDE_F32, STATE_HALF] + ([LANES, LANES] if side == 0 else [STATS]),
        2 * BLOCK * SIDE * DH,
        MIB,
    )(core, q, o, intra, gain, base, near, *sums)


def grad_body(side, core, q, output, o, gain, s0, s1, s2, s3, grad_out, states):
    total = (s0[...] + s1[...]) + (s2[...] + s3[...])
    mean_square = total[0:1, :] / WIDTH_ALL + epsilon
    radius = jnp.sqrt(mean_square)
    scale = total[1:2, :] / (WIDTH_ALL * radius * radius)
    inverse = jnp.broadcast_to(1.0 / radius, (DH, BLOCK)).T
    coeff = jnp.broadcast_to(scale, (DH, BLOCK)).T
    gains = gain[:, pl.ds(side_start(core, side), SIDE)]
    for pair in PAIRS:
        for head in (2 * pair, 2 * pair + 1):
            cols = head_columns(head)
            scaled = o[:, cols].astype(F32) * gains[:, cols]
            grad_out[:, cols] = ((scaled - output[:, cols] * coeff) * inverse).astype(BF16)
        cols = pair_columns(pair)
        store_states(states, pair, q[:, cols], grad_out[:, cols])


def local_grad(side, core, q, output, o, gain, stats):
    return call(
        f"grad{side}",
        functools.partial(grad_body, side),
        [SMEM] + [VMEM] * 8,
        [VMEM] * 2,
        [SIDE_BF16, STATE],
        2 * BLOCK * SIDE * DH,
        MIB,
    )(core, q, output, o, gain, *stats)


SIDE_ARRAYS = 7


def middle_body(jobs, core, *refs):
    before, behind = seen_keys(), seen_queries()
    sides = sorted({side for side, _ in jobs})
    arrays = {
        side: refs[place * SIDE_ARRAYS : (place + 1) * SIDE_ARRAYS] for place, side in enumerate(sides)
    }
    outputs = refs[len(refs) - 3 - 2 * len(jobs) :]
    query_grad, parts, result, sems = outputs[0], outputs[1:-2], outputs[-2], outputs[-1]
    results = []
    for place, (side, pair) in enumerate(jobs):
        q, k, v, g, prefix, first, last = arrays[side]
        key_part, value_part = parts[2 * place : 2 * place + 2]
        across = dot_nt(g[:, pair_columns(pair)], diagonal(prefix, pair))
        for h in range(2):
            head = 2 * pair + h
            cols, here = head_columns(head), head_columns(h)
            part = across[:, here]
            mixing0, mixing1 = by_keys(before, g[:, cols], v[:, cols])
            turned0, turned1 = by_queries(behind, v[:, cols], g[:, cols])
            total = dot(last[pl.ds(head * BLOCK, BLOCK), :], g[BOTTOM, cols])
            value_part[TOP, here] = total[TOP] + dot(first[pl.ds(head * HALF, HALF), :], g[TOP, cols])
            value_part[BOTTOM, here] = total[BOTTOM]
            there = head_columns(2 * place + h)
            total = part + dot(mixing0, k[TOP, cols])
            result[TOP, there] = total[TOP].astype(BF16)
            result[BOTTOM, there] = (total[BOTTOM] + dot(mixing1, k[BOTTOM, cols])).astype(BF16)
            total = dot(turned1, q[BOTTOM, cols])
            key_part[TOP, here] = total[TOP] + dot(turned0, q[TOP, cols])
            key_part[BOTTOM, here] = total[BOTTOM]
        results += copies_of(
            [(result.at[:, pair_columns(place)], query_grad.at[:, pair_window(core, side, pair)])],
            sems.at[pl.ds(place, 1)],
        )
    wait(results)


def middle_gradients(number, jobs, core, arrays, result=()):
    sides = sorted({side for side, _ in jobs})
    inputs = [array for side in sides for array in arrays[side]]
    query_grad, *parts = call(
        f"middle{number}",
        functools.partial(middle_body, jobs),
        [SMEM] + [VMEM] * len(inputs) + [HBM] * len(result),
        [HBM] + [VMEM] * (2 * len(jobs)),
        [WHOLE] + [PAIR_F32] * (2 * len(jobs)),
        2 * BLOCK * BLOCK * SIDE * len(jobs),
        MIB * len(jobs),
        [
            pltpu.VMEM((BLOCK, len(jobs) * 2 * DH), BF16),
            pltpu.SemaphoreType.DMA((len(jobs),)),
        ],
        {1 + len(inputs) + i: i for i in range(len(result))},
    )(core, *inputs, *result)
    return query_grad, {job: parts[2 * i : 2 * i + 2] for i, job in enumerate(jobs)}


def last_body(side, core, k, v, base, near, *refs):
    parts = refs[: 2 * PAIRS_SIDE]
    if side == 0:
        key_half, value_half = refs[2 * PAIRS_SIDE :]
    else:
        key_own, value_own, key_grad, value_grad, key_half, value_half, sems = refs[2 * PAIRS_SIDE :]
        own = pl.ds(side_start(core, 0), SIDE)
        results = copies_of(
            [(key_own, key_grad.at[:, own]), (value_own, value_grad.at[:, own])],
            sems.at[pl.ds(2 * PAIRS_SIDE, 2)],
        )
    weight = 1.0 - core[0].astype(F32)
    later = (base[...] + weight * near[...]).astype(BF16)
    for pair in PAIRS:
        cols = pair_columns(pair)
        states = diagonal(later, pair)
        key_half[:, cols] = (parts[2 * pair][...] + dot_nt(v[:, cols], states)).astype(BF16)
        value_half[:, cols] = (parts[2 * pair + 1][...] + dot(k[:, cols], states)).astype(BF16)
        if side == 1:
            window = pair_window(core, side, pair)
            results += copies_of(
                [(key_half.at[:, cols], key_grad.at[:, window]), (value_half.at[:, cols], value_grad.at[:, window])],
                sems.at[pl.ds(2 * pair, 2)],
            )
    if side == 1:
        wait(results)


def last_gradients(side, core, k, v, base, near, parts, own=()):
    inputs = [k, v, base, near] + [array for pair in PAIRS for array in parts[side, pair]] + list(own)
    return call(
        f"last{side}",
        functools.partial(last_body, side),
        [SMEM] + [VMEM] * len(inputs),
        [VMEM, VMEM] if side == 0 else [HBM, HBM],
        [SIDE_BF16, SIDE_BF16] if side == 0 else [WHOLE, WHOLE],
        4 * BLOCK * SIDE * DH,
        2 * MIB,
        []
        if side == 0
        else [BUFFER_BF16, BUFFER_BF16, pltpu.SemaphoreType.DMA((2 * PAIRS_SIDE + 2,))],
    )(core, *inputs)


def quarter(place):
    return pl.ds(pl.multiple_of(place * QUARTER, QUARTER), QUARTER)


def split_body(x, own, near, *outs):
    for hop, out in enumerate(outs):
        rows = quarter(lax.rem(x[0] + hop, LINE))
        out[...] = own[rows, :] + near[rows, :]


def split(chip, own, near):
    return call(
        "split", split_body, [SMEM, VMEM, VMEM], [VMEM] * LINE, [PIECE] * LINE, MIB, MIB
    )(chip[0], own, near)


def line_body(a, b, c, d, out):
    out[...] = (a[...] + b[...]) + (c[...] + d[...])


def line_sum(pieces):
    return call("line", line_body, [VMEM] * LINE, VMEM, PIECE, MIB, MIB)(*pieces)


def enter_body(reverse, x, y, *refs):
    pieces, sums, outs = refs[:LINE], refs[LINE : 2 * LINE - 1], refs[2 * LINE - 1 :]
    lines_ahead = LINE - 1 - y[0] if reverse else y[0]
    start = jnp.zeros((QUARTER, DH), F32)
    for hop, part in enumerate(sums, 1):
        start = start + (hop <= lines_ahead).astype(jnp.int32).astype(F32) * part[...]
    values = [piece[...] for piece in pieces]
    places = [lax.rem(x[0] + LINE - hop, LINE) for hop in range(LINE)]
    for hop, out in enumerate(outs):
        target = lax.rem(x[0] + hop, LINE)
        total = start
        for place, value in zip(places, values):
            ahead = place > target if reverse else place < target
            total = total + ahead.astype(jnp.int32).astype(F32) * value
        out[...] = total


def entering(chip, pieces, sums, reverse):
    return call(
        f"enter{int(reverse)}",
        functools.partial(enter_body, reverse),
        [SMEM] * 2 + [VMEM] * (2 * LINE - 1),
        [VMEM] * LINE,
        [PIECE] * LINE,
        MIB,
        MIB,
    )(*chip, *pieces, *sums)


def join_body(x, a, b, c, d, out):
    for hop, piece in enumerate((a, b, c, d)):
        out[quarter(lax.rem(x[0] + LINE - hop, LINE)), :] = piece[...]


def join(chip, pieces):
    return call("join", join_body, [SMEM] + [VMEM] * LINE, VMEM, STATE, MIB, MIB)(chip[0], *pieces)


def device_index(y, x, core):
    return (y * LINE + x) * 2 + core


DEVICES = [(y, x, core) for y in range(LINE) for x in range(LINE) for core in range(2)]
PARTNERS = [(i, i ^ 1) for i in range(len(DEVICES))]
HOPS = (2, 1, 3)


def along_x(pieces):
    got = {0: pieces[0]}
    for hop in HOPS:
        pairs = [
            (device_index(y, x, core), device_index(y, (x + hop) % LINE, core)) for y, x, core in DEVICES
        ]
        got[hop] = lax.ppermute(pieces[hop], "ctx", pairs)
    return [got[hop] for hop in range(LINE)]


def along_y(part, reverse):
    got = {}
    for hop in HOPS:
        step = -hop if reverse else hop
        pairs = [
            (device_index(y, x, core), device_index((y + step) % LINE, x, core)) for y, x, core in DEVICES
        ]
        got[hop] = lax.ppermute(part, "ctx", pairs)
    return [got[hop] for hop in (1, 2, 3)]


def swap(part):
    return lax.ppermute(part, "ctx", PARTNERS)


def along_heads(stats):
    hops = (1, 2, 3)
    return [lax.ppermute(stats, "head", [(i, (i + hop) % 4) for i in range(4)]) for hop in hops]


def after(value, *done):
    return lax.optimization_barrier((value,) + done)[0]


def local(query_rows, key_rows, value_rows, out_grad, norm_gain):
    place = lax.axis_index("ctx").astype(jnp.int32)
    core = (place % 2).reshape(1)
    chip = ((place // 2 % LINE).reshape(1), (place // (2 * LINE)).reshape(1))
    return device(core, chip, query_rows, key_rows, value_rows, out_grad, norm_gain)


def device(core, chip, query_rows, key_rows, value_rows, out_grad, norm_gain):
    gain = norm_gain.reshape(1, WIDTH)

    k1, v1, state1 = local_state(1, core, key_rows, value_rows)
    near0 = swap(state1)
    k0, v0, state0 = local_state(0, core, key_rows, value_rows)
    pieces = along_x(split(chip, state0, near0))
    q0, o0, intra0, *turned0 = intra_output(0, 0, PAIRS, core, query_rows, out_grad, k0, v0)
    pieces[1] = after(pieces[1], intra0)
    sums = along_y(line_sum(pieces), False)
    begun = intra_output(1, 1, PAIRS[:2], core, query_rows, out_grad, k1, v1)
    sums[0] = after(sums[0], begun[2])
    pieces = along_x(entering(chip, pieces, sums, False))
    near1 = swap(after(state0, sums[0]))
    q1, o1, intra1, *turned1 = intra_output(2, 1, PAIRS[2:], core, query_rows, out_grad, k1, v1, begun)
    pieces[1] = after(pieces[1], intra1)
    base0 = join(chip, pieces)
    base1 = swap(base0)
    output0, prefix0, *lanes = whole_output(0, core, q0, o0, intra0, gain, base0, near0)
    output1, prefix1, stats = whole_output(1, core, q1, o1, intra1, gain, base1, near1, lanes)
    stats = [stats] + along_heads(stats)

    g1, state1 = local_grad(1, core, q1, output1, o1, gain, stats)
    near0 = swap(state1)
    g0, state0 = local_grad(0, core, q0, output0, o0, gain, stats)
    arrays = ((q0, k0, v0, g0, prefix0, *turned0), (q1, k1, v1, g1, prefix1, *turned1))
    pieces = along_x(split(chip, state0, near0))
    query_grad, parts = middle_gradients(0, ((0, 0), (0, 1), (0, 2)), core, arrays)
    pieces[1] = after(pieces[1], query_grad)
    sums = along_y(line_sum(pieces), True)
    query_grad, more = middle_gradients(1, ((0, 3), (1, 0), (1, 1)), core, arrays, (query_grad,))
    parts.update(more)
    sums[0] = after(sums[0], query_grad)
    pieces = along_x(entering(chip, pieces, sums, True))
    near1 = swap(after(state0, sums[0]))
    query_grad, more = middle_gradients(2, ((1, 2), (1, 3)), core, arrays, (query_grad,))
    parts.update(more)
    pieces[1] = after(pieces[1], query_grad)
    base0 = join(chip, pieces)
    base1 = swap(base0)
    results = last_gradients(0, core, k0, v0, base0, near0, parts)
    key_grad, value_grad = last_gradients(1, core, k1, v1, base1, near1, parts, results)
    return query_grad, key_grad, value_grad


def solution(mesh):
    in_specs = (P("ctx", "head"), P("ctx", "head"), P("ctx", "head"), P("ctx", "head"), P("head"))
    out_specs = (P("ctx", "head"), P("ctx", "head"), P("ctx", "head"))
    return jax.shard_map(local, mesh=mesh, in_specs=in_specs, out_specs=out_specs, check_vma=False)
```

time: 99 us -> 95.1 us (0.961)
  Pallas kernels: 47.1 us -> 34.5 us
  local copies, waits for them, and re-layouts: 0.01 us -> 7 us
  starting transfers between devices: 34.4 us -> 40.6 us
  waiting for transfers between devices: 14.1 us -> 11.6 us
  other arithmetic: 1.7 us -> 0 us
    ppermute x0 -> x18, starting transfers between devices: none -> 23.3 us  [the longest x12 16.2 us: along_x(): got[hop] = lax.ppermute(pieces[hop], 'ctx', pairs)]
    all_to_all x4 -> x0, starting transfers between devices: 17.6 us -> none  [exchange(): lax.all_to_all(parts, 'ctx', 0, 0, axis_index_groups=SAME_CORE, tiled=True)]
    pallas_call x14 -> x22, Pallas kernels: 47.1 us -> 34.5 us  [run(): kernel(*(pltpu.with_memory_space_constraint(array, pltpu.HBM) if spec is...]
    all_to_all x4 -> x0, waiting for transfers between devices: 12.4 us -> none  [exchange(): lax.all_to_all(parts, 'ctx', 0, 0, axis_index_groups=SAME_CORE, tiled=True)]
    unnamed x2 -> x38, local copies, waits for them, and re-layouts: 0.01 us -> 7 us
    ppermute x0 -> x18, waiting for transfers between devices: none -> 6.32 us  [the longest x6 4.3 us: along_y(): got[hop] = lax.ppermute(part, 'ctx', pairs)]
    ppermute x6, waiting for transfers between devices: 0.02 us -> 2.06 us  [swap(): return lax.ppermute(part, 'ctx', PARTNERS)]
    add x2 -> x0, other arithmetic: 1.7 us -> none  [device(): parts = exchange((state0 + near0).reshape(CHIPS, SLICE, DH))]
  transfers between devices with their start and end apart: 13 -> 27, of which waited for: 6 -> 9; matrix products, arithmetic and copies ran while one was open for 0% -> 0% of each run, Pallas kernels for 39% -> 27%
where the time goes in v4:
time: 95.1 us; the launch traced here: 94.9 us
  starting transfers between devices  40.6 us (43%)
  Pallas kernels  34.5 us (36%)
  waiting for transfers between devices  11.6 us (12%)
  local copies, waits for them, and re-layouts  7 us (7%)
  between operations  1.14 us (1%)
    pallas_call x22, Pallas kernels, run(): kernel(*(pltpu.with_memory_space_constraint(array, pltpu.HBM) if spec is...  34.5 us
    ppermute x12, starting transfers between devices, along_x(): got[hop] = lax.ppermute(pieces[hop], 'ctx', pairs)  16.2 us
    ppermute x6, starting transfers between devices, swap(): return lax.ppermute(part, 'ctx', PARTNERS)  12.7 us
    ppermute x6, starting transfers between devices, along_y(): got[hop] = lax.ppermute(part, 'ctx', pairs)  7.17 us
    unnamed x38, local copies, waits for them, and re-layouts  7 us
    ppermute x3, starting transfers between devices, along_heads(): lax.ppermute(stats, 'head', [(i, (i + hop) % 4) for i in range(4)])  4.53 us
    ppermute x6, waiting for transfers between devices, along_y(): got[hop] = lax.ppermute(part, 'ctx', pairs)  4.3 us
    ppermute x3, waiting for transfers between devices, along_heads(): lax.ppermute(stats, 'head', [(i, (i + hop) % 4) for i in range(4)])  3.26 us
  transfers between devices with their start and end apart: 27, of which 9 were waited for; matrix products, arithmetic and copies ran while one was open for 0% of the time, Pallas kernels for 27%

profile of v4, /device:TPU:1, one launch (start us, length us, event | category | flops | bytes accessed | tf_op | source)
XLA Modules:
  0.0 94.9 jit_solution(10797305434317227603)
XLA Ops:
  0.6 2.7 %state1.1 = (bf16[512,1024]{1,0:T(8,128)(2,1)S(1)}, bf16[512,1024]{1,0:T(8,128)(2,1)S(1)}, f32[1024,128]{1,0:T(8,128)}) custom-call(s32[1]{0:T(128)} %bitcast.core, bf16[512,2048]{1,0:T(8,128)(2,1)} %k_all.3, bf16[512,2048]{1,0:T(8,128)(2,1)} %v_all.3), custom_call_target="tpu_custom_call" | custom-call | flops 134217728 | bytes 2097152 | tf_op jit(solution)/shard_map/state1/pallas_call | solution.py:79
  3.4 1.5 %collective-permute-start = (f32[1024,128]{1,0:T(8,128)}, f32[1024,128]{1,0:T(8,128)S(1)}, u32[]{:S(2)}, u32[]{:S(2)}) collective-permute-start(f32[1024,128]{1,0:T(8,128)} %get-tuple-element.93), channel_id=1, source_target_pairs={{0,4},{4,0},{8,12},{12,8},{16,20},{20,16},{24,28},{28,24},{32,36},... | collective-permute-start | bytes 1572872 | tf_op jit(solution)/shard_map/ppermute | solution.py:518
  4.9 1.9 %state0.1 = (bf16[512,1024]{1,0:T(8,128)(2,1)S(1)}, bf16[512,1024]{1,0:T(8,128)(2,1)S(1)}, f32[1024,128]{1,0:T(8,128)S(1)}) custom-call(s32[1]{0:T(128)} %bitcast.core, bf16[512,2048]{1,0:T(8,128)(2,1)} %k_all.3, bf16[512,2048]{1,0:T(8,128)(2,1)} %v_all.3), custom_call_target="tpu_custom_call" | custom-call | flops 134217728 | bytes 2097152 | tf_op jit(solution)/shard_map/state0/pallas_call | solution.py:79
  6.8 0.0 collective-permute-done.near
  6.8 0.1 split.2
  6.9 0.9 copy-done.12
  7.8 0.8 copy-done.16
  8.6 1.3 %collective-permute-start.1 = (f32[256,128]{1,0:T(8,128)S(1)}, f32[256,128]{1,0:T(8,128)S(1)}, u32[]{:S(2)}, u32[]{:S(2)}) collective-permute-start(f32[256,128]{1,0:T(8,128)S(1)} %get-tuple-element.95), channel_id=1, source_target_pairs={{0,8},{4,12},{8,16},{12,20},{16,24},{20,28},{24,0},{28,4},{32,40},... | collective-permute-start | bytes 393224 | tf_op jit(solution)/shard_map/ppermute | solution.py:502
  9.9 2.4 %collective-permute-start.2 = (f32[256,128]{1,0:T(8,128)S(1)}, f32[256,128]{1,0:T(8,128)S(1)}, u32[]{:S(2)}, u32[]{:S(2)}) collective-permute-start(f32[256,128]{1,0:T(8,128)S(1)} %get-tuple-element.100), channel_id=1, source_target_pairs={{0,16},{4,20},{8,24},{12,28},{16,0},{20,4},{24,8},{28,12},{32,48},... | collective-permute-start | bytes 393224 | tf_op jit(solution)/shard_map/ppermute | solution.py:502
  12.4 1.2 %collective-permute-start.3 = (f32[256,128]{1,0:T(8,128)S(1)}, f32[256,128]{1,0:T(8,128)S(1)}, u32[]{:S(2)}, u32[]{:S(2)}) collective-permute-start(f32[256,128]{1,0:T(8,128)S(1)} %get-tuple-element.101), channel_id=1, source_target_pairs={{0,24},{4,28},{8,0},{12,4},{16,8},{20,12},{24,16},{28,20},{32,56},... | collective-permute-start | bytes 393224 | tf_op jit(solution)/shard_map/ppermute | solution.py:502
  13.5 4.2 %intra0.1 = (bf16[512,1024]{1,0:T(8,128)(2,1)S(1)}, bf16[512,1024]{1,0:T(8,128)(2,1)S(1)}, f32[512,1024]{1,0:T(8,128)S(1)}, bf16[2048,256]{1,0:T(8,128)(2,1)S(1)}, bf16[4096,256]{1,0:T(8,128)(2,1)S(1)}) custom-call(s32[1]{0:T(128)} %bitcast.core, bf16[512,2048]{1,0:T(8,128)(2,1)} %q_all.5, bf16[512,2048]{1,0:T(8,128)(2,1)} %o_all.5, ...), custom_call_target="tpu_custom_call" | custom-call | flops 1342177280 | bytes 8388608 | tf_op jit(solution)/shard_map/intra0/pallas_call | solution.py:79
  17.8 0.0 copy-start.4
  17.8 1.3 %copy-done.4 = bf16[4096,256]{1,0:T(8,128)(2,1)} copy-done((bf16[4096,256]{1,0:T(8,128)(2,1)}, bf16[4096,256]{1,0:T(8,128)(2,1)S(1)}, u32[]{:S(2)}) %copy-start.4) | copy-done | bytes 2097176
  19.1 1.0 %copy-done.6 = bf16[2048,256]{1,0:T(8,128)(2,1)} copy-done((bf16[2048,256]{1,0:T(8,128)(2,1)}, bf16[2048,256]{1,0:T(8,128)(2,1)S(1)}, u32[]{:S(2)}) %copy-start.6) | copy-done | bytes 1048600
  20.1 1.0 %copy-done.8 = bf16[512,1024]{1,0:T(8,128)(2,1)} copy-done((bf16[512,1024]{1,0:T(8,128)(2,1)}, bf16[512,1024]{1,0:T(8,128)(2,1)S(1)}, u32[]{:S(2)}) %copy-start.8) | copy-done | bytes 1048600
  21.0 1.3 %copy-done.10 = f32[512,1024]{1,0:T(8,128)} copy-done((f32[512,1024]{1,0:T(8,128)}, f32[512,1024]{1,0:T(8,128)S(1)}, u32[]{:S(2)}) %copy-start.10) | copy-done | bytes 2097176
  22.4 0.0 collective-permute-done.3.d.refs_3_
  22.4 0.7 line.2
  23.0 0.6 copy-done.14
  23.7 1.3 %collective-permute-start.4 = (f32[256,128]{1,0:T(8,128)}, f32[256,128]{1,0:T(8,128)}, u32[]{:S(2)}, u32[]{:S(2)}) collective-permute-start(f32[256,128]{1,0:T(8,128)} %line.2), channel_id=1, source_target_pairs={{0,32},{4,36},{8,40},{12,44},{16,48},{20,52},{24,56},{28,60},{32,6... | collective-permute-start | bytes 393224 | tf_op jit(solution)/shard_map/ppermute | solution.py:513
  25.0 1.4 %collective-permute-start.6 = (f32[256,128]{1,0:T(8,128)}, f32[256,128]{1,0:T(8,128)}, u32[]{:S(2)}, u32[]{:S(2)}) collective-permute-start(f32[256,128]{1,0:T(8,128)} %line.2), channel_id=1, source_target_pairs={{0,96},{4,100},{8,104},{12,108},{16,112},{20,116},{24,120},{28,124... | collective-permute-start | bytes 393224 | tf_op jit(solution)/shard_map/ppermute | solution.py:513
  26.4 1.6 %collective-permute-start.5 = (f32[256,128]{1,0:T(8,128)}, f32[256,128]{1,0:T(8,128)}, u32[]{:S(2)}, u32[]{:S(2)}) collective-permute-start(f32[256,128]{1,0:T(8,128)} %line.2), channel_id=1, source_target_pairs={{0,64},{4,68},{8,72},{12,76},{16,80},{20,84},{24,88},{28,92},{32,9... | collective-permute-start | bytes 393224 | tf_op jit(solution)/shard_map/ppermute | solution.py:513
  28.1 2.6 %intra1.1 = (bf16[512,1024]{1,0:T(8,128)(2,1)S(1)}, bf16[512,1024]{1,0:T(8,128)(2,1)S(1)}, f32[512,1024]{1,0:T(8,128)S(1)}, bf16[2048,256]{1,0:T(8,128)(2,1)S(1)}, bf16[4096,256]{1,0:T(8,128)(2,1)S(1)}) custom-call(s32[1]{0:T(128)} %bitcast.core, bf16[512,2048]{1,0:T(8,128)(2,1)} %q_all.5, bf16[512,2048]{1,0:T(8,128)(2,1)} %o_all.5, ...), custom_call_target="tpu_custom_call" | custom-call | flops 671088640 | bytes 4194304 | tf_op jit(solution)/shard_map/intra1/pallas_call | solution.py:79
  30.7 0.0 collective-permute-done.4.refs_4_
  30.7 3.0 %collective-permute-done.5.refs_5_ = f32[256,128]{1,0:T(8,128)} collective-permute-done((f32[256,128]{1,0:T(8,128)}, f32[256,128]{1,0:T(8,128)}, u32[]{:S(2)}, u32[]{:S(2)}) %collective-permute-start.5) | collective-permute-done | bytes 131104 | tf_op jit(solution)/shard_map/ppermute | solution.py:513
  33.8 1.2 %enter0.1 = (f32[256,128]{1,0:T(8,128)S(1)}, f32[256,128]{1,0:T(8,128)S(1)}, f32[256,128]{1,0:T(8,128)S(1)}, f32[256,128]{1,0:T(8,128)S(1)}) custom-call(s32[1]{0:T(128)} %bitcast.2.x, s32[1]{0:T(128)} %bitcast.3.y, f32[256,128]{1,0:T(8,128)S(1)} %get-tuple-element.94.a.refs_0_, f32[256,128]{1,0:T(8,128)S(1)} %collective-permute-done.1.b.refs_1_, ...), custom_call_target="tpu_custom_call" | custom-call | flops 1048576 | bytes 1048576 | tf_op jit(solution)/shard_map/enter0/pallas_call | solution.py:79
  35.0 0.4 collective-permute-start.7
  35.4 0.8 collective-permute-start.8
  36.2 1.7 %collective-permute-start.9 = (f32[256,128]{1,0:T(8,128)S(1)}, f32[256,128]{1,0:T(8,128)S(1)}, u32[]{:S(2)}, u32[]{:S(2)}) collective-permute-start(f32[256,128]{1,0:T(8,128)S(1)} %get-tuple-element.107), channel_id=1, source_target_pairs={{0,24},{4,28},{8,0},{12,4},{16,8},{20,12},{24,16},{28,20},{32,56},... | collective-permute-start | bytes 393224 | tf_op jit(solution)/shard_map/ppermute | solution.py:502
  37.9 2.1 %collective-permute-start.11 = (f32[1024,128]{1,0:T(8,128)S(1)}, f32[1024,128]{1,0:T(8,128)S(1)}, u32[]{:S(2)}, u32[]{:S(2)}) collective-permute-start(f32[1024,128]{1,0:T(8,128)S(1)} %copy-done.17), channel_id=1, source_target_pairs={{0,4},{4,0},{8,12},{12,8},{16,20},{20,16},{24,28},{28,24},{32,36},... | collective-permute-start | bytes 1572872 | tf_op jit(solution)/shard_map/ppermute | solution.py:518
  40.0 2.7 %intra2.1 = (bf16[512,1024]{1,0:T(8,128)(2,1)S(1)}, bf16[512,1024]{1,0:T(8,128)(2,1)S(1)}, f32[512,1024]{1,0:T(8,128)S(1)}, bf16[2048,256]{1,0:T(8,128)(2,1)S(1)}, bf16[4096,256]{1,0:T(8,128)(2,1)S(1)}) custom-call(s32[1]{0:T(128)} %bitcast.core, ...), custom_call_target="tpu_custom_call", output_to_operand_aliasing={{0}: (5, {}), {1}: (6, {}), {2}: (7, {}), {3}: (8, {}), {4}... | custom-call | flops 671088640 | bytes 4194304 | tf_op jit(solution)/shard_map/intra2/pallas_call | solution.py:79
  42.7 0.0 collective-permute-done.8.c
  42.7 0.2 collective-permute-done.9.d
  43.0 2.9 %collective-permute-start.10 = (f32[1024,128]{1,0:T(8,128)S(1)}, f32[1024,128]{1,0:T(8,128)S(1)}, u32[]{:S(2)}, u32[]{:S(2)}) collective-permute-start(f32[1024,128]{1,0:T(8,128)S(1)} %join.2.base), channel_id=1, source_target_pairs={{0,4},{4,0},{8,12},{12,8},{16,20},{20,16},{24,28},{28,24},{32,36},... | collective-permute-start | bytes 1572872 | tf_op jit(solution)/shard_map/ppermute | solution.py:518
  45.9 0.8 output0.1
  46.7 0.7 collective-permute-done.10.base
  47.5 1.0 %output1.1 = (f32[512,1024]{1,0:T(8,128)S(1)}, bf16[1024,128]{1,0:T(8,128)(2,1)S(1)}, f32[2,512]{1,0:T(2,128)S(1)}) custom-call(s32[1]{0:T(128)} %bitcast.core, bf16[512,1024]{1,0:T(8,128)(2,1)S(1)} %get-tuple-element.89.q.refs_7_.refs_0_, bf16[512,1024]{1,0:T(8,128)(2,1)S(1)} %get-tuple-element.90.o, f32[512,1024]{1,0:T(8,128)S(1)} %get-tuple-element.91.intra, ...), custom_call_target="tpu_custom_call" | custom-call | flops 134217728 | bytes 1048576 | tf_op jit(solution)/shard_map/output1/pallas_call | solution.py:79
  48.4 3.8 %collective-permute-start.14 = (f32[2,512]{1,0:T(2,128)S(1)}, f32[2,512]{1,0:T(2,128)S(1)}, u32[]{:S(2)}, u32[]{:S(2)}) collective-permute-start(f32[2,512]{1,0:T(2,128)S(1)} %get-tuple-element.114.s0), channel_id=1, source_target_pairs={{0,3},{1,0},{2,1},{3,2},{4,7},{5,4},{6,5},{7,6},{8,11},{9,8},{10,9... | collective-permute-start | bytes 12296 | tf_op jit(solution)/shard_map/ppermute | solution.py:523
  52.2 0.7 collective-permute-start.12
  52.9 0.1 collective-permute-done.14.s3
  53.0 3.2 %collective-permute-done.13.s2 = f32[2,512]{1,0:T(2,128)S(1)} collective-permute-done((f32[2,512]{1,0:T(2,128)S(1)}, f32[2,512]{1,0:T(2,128)S(1)}, u32[]{:S(2)}, u32[]{:S(2)}) %collective-permute-start.13) | collective-permute-done | bytes 4128 | tf_op jit(solution)/shard_map/ppermute | solution.py:523
  56.2 1.0 %grad1.1 = (bf16[512,1024]{1,0:T(8,128)(2,1)S(1)}, f32[1024,128]{1,0:T(8,128)S(1)}) custom-call(s32[1]{0:T(128)} %bitcast.core, bf16[512,1024]{1,0:T(8,128)(2,1)S(1)} %get-tuple-element.89.q.refs_7_.refs_0_, f32[512,1024]{1,0:T(8,128)S(1)} %get-tuple-element.113.output, bf16[512,1024]{1,0:T(8,128)(2,1)S(1)} %get-tuple-element.90.o, f32[1,2048]{1,0:T(1,128)S(1)} %bitcast.6, ...), custom_call_target="tpu_custom_call" | custom-call | flops 134217728 | bytes 1048576 | tf_op jit(solution)/shard_map/grad1/pallas_call | solution.py:79
  57.2 1.9 %collective-permute-start.15 = (f32[1024,128]{1,0:T(8,128)S(1)}, f32[1024,128]{1,0:T(8,128)S(1)}, u32[]{:S(2)}, u32[]{:S(2)}) collective-permute-start(f32[1024,128]{1,0:T(8,128)S(1)} %get-tuple-element.128), channel_id=1, source_target_pairs={{0,4},{4,0},{8,12},{12,8},{16,20},{20,16},{24,28},{28,24},{32,36},... | collective-permute-start | bytes 1572872 | tf_op jit(solution)/shard_map/ppermute | solution.py:518
  59.1 1.0 %grad0.1 = (bf16[512,1024]{1,0:T(8,128)(2,1)S(1)}, f32[1024,128]{1,0:T(8,128)S(1)}) custom-call(s32[1]{0:T(128)} %bitcast.core, bf16[512,1024]{1,0:T(8,128)(2,1)S(1)} %get-tuple-element.109.q.refs_0_, f32[512,1024]{1,0:T(8,128)S(1)} %get-tuple-element.119.output, bf16[512,1024]{1,0:T(8,128)(2,1)S(1)} %copy-done.9, f32[1,2048]{1,0:T(1,128)S(1)} %bitcast.7, ...), custom_call_target="tpu_custom_call" | custom-call | flops 134217728 | bytes 1048576 | tf_op jit(solution)/shard_map/grad0/pallas_call | solution.py:79
  60.1 0.5 collective-permute-done.15.near
  60.6 0.1 split.3
  60.6 0.1 collective-permute-start.16
  60.8 3.3 %collective-permute-start.17 = (f32[256,128]{1,0:T(8,128)S(1)}, f32[256,128]{1,0:T(8,128)S(1)}, u32[]{:S(2)}, u32[]{:S(2)}) collective-permute-start(f32[256,128]{1,0:T(8,128)S(1)} %get-tuple-element.132), channel_id=1, source_target_pairs={{0,16},{4,20},{8,24},{12,28},{16,0},{20,4},{24,8},{28,12},{32,48},... | collective-permute-start | bytes 393224 | tf_op jit(solution)/shard_map/ppermute | solution.py:502
  64.1 4.2 %middle0.1 = (bf16[512,2048]{1,0:T(8,128)(2,1)}, f32[512,256]{1,0:T(8,128)S(1)}, f32[512,256]{1,0:T(8,128)S(1)}, f32[512,256]{1,0:T(8,128)S(1)}, f32[512,256]{1,...) custom-call(s32[1]{0:T(128)} %bitcast.core, bf16[512,1024]{1,0:T(8,128)(2,1)S(1)} %get-tuple-element.109.q.refs_0_, ...), custom_call_target="tpu_custom_call" | custom-call | flops 1610612736 | bytes 3145728 | tf_op jit(solution)/shard_map/middle0/pallas_call | solution.py:79
  68.3 1.8 %collective-permute-done.17.c.refs_2_ = f32[256,128]{1,0:T(8,128)S(1)} collective-permute-done((f32[256,128]{1,0:T(8,128)S(1)}, f32[256,128]{1,0:T(8,128)S(1)}, u32[]{:S(2)}, u32[]{:S(2)}) %collective-permute-start.17) | collective-permute-done | bytes 131104 | tf_op jit(solution)/shard_map/ppermute | solution.py:502
  70.2 0.3 collective-permute-start.21
  70.4 2.4 %collective-permute-start.20 = (f32[256,128]{1,0:T(8,128)S(1)}, f32[256,128]{1,0:T(8,128)S(1)}, u32[]{:S(2)}, u32[]{:S(2)}) collective-permute-start(f32[256,128]{1,0:T(8,128)S(1)} %line.3), channel_id=1, source_target_pairs={{0,64},{4,68},{8,72},{12,76},{16,80},{20,84},{24,88},{28,92},{32,9... | collective-permute-start | bytes 393224 | tf_op jit(solution)/shard_map/ppermute | solution.py:513
  72.9 0.1 collective-permute-start.19
  73.0 4.2 %middle1.1 = (bf16[512,2048]{1,0:T(8,128)(2,1)}, f32[512,256]{1,0:T(8,128)S(1)}, f32[512,256]{1,0:T(8,128)S(1)}, f32[512,256]{1,0:T(8,128)S(1)}, f32[512,256]{1,...) custom-call(s32[1]{0:T(128)} %bitcast.core, ...), custom_call_target="tpu_custom_call", output_to_operand_aliasing={{0}: (15, {})} | custom-call | flops 1610612736 | bytes 3145728 | tf_op jit(solution)/shard_map/middle1/pallas_call | solution.py:79
  77.2 1.3 %collective-permute-done.19.refs_4_ = f32[256,128]{1,0:T(8,128)S(1)} collective-permute-done((f32[256,128]{1,0:T(8,128)S(1)}, f32[256,128]{1,0:T(8,128)S(1)}, u32[]{:S(2)}, u32[]{:S(2)}) %collective-permute-start.19) | collective-permute-done | bytes 131104 | tf_op jit(solution)/shard_map/ppermute | solution.py:513
  78.4 0.2 enter1.1
  78.6 0.4 collective-permute-start.22
  79.1 4.5 %collective-permute-start.23 = (f32[256,128]{1,0:T(8,128)S(1)}, f32[256,128]{1,0:T(8,128)S(1)}, u32[]{:S(2)}, u32[]{:S(2)}) collective-permute-start(f32[256,128]{1,0:T(8,128)S(1)} %get-tuple-element.138), channel_id=1, source_target_pairs={{0,16},{4,20},{8,24},{12,28},{16,0},{20,4},{24,8},{28,12},{32,48},... | collective-permute-start | bytes 393224 | tf_op jit(solution)/shard_map/ppermute | solution.py:502
  83.6 2.2 %collective-permute-start.26 = (f32[1024,128]{1,0:T(8,128)S(1)}, f32[1024,128]{1,0:T(8,128)S(1)}, u32[]{:S(2)}, u32[]{:S(2)}) collective-permute-start(f32[1024,128]{1,0:T(8,128)S(1)} %get-tuple-element.140.own), channel_id=1, source_target_pairs={{0,4},{4,0},{8,12},{12,8},{16,20},{20,16},{24,28},{28,24},{32,36},... | collective-permute-start | bytes 1572872 | tf_op jit(solution)/shard_map/ppermute | solution.py:518
  85.8 3.1 %middle2.1 = (bf16[512,2048]{1,0:T(8,128)(2,1)}, f32[512,256]{1,0:T(8,128)S(1)}, f32[512,256]{1,0:T(8,128)S(1)}, f32[512,256]{1,0:T(8,128)S(1)}, f32[512,256]{1,0:T(8,128)S(1)}) custom-call(s32[1]{0:T(128)} %bitcast.core, bf16[512,1024]{1,0:T(8,128)(2,1)S(1)} %get-tuple-element.89.q.refs_7_.refs_0_, ...), custom_call_target="tpu_custom_call", output_to_operand_aliasing={{0}: (8, {})} | custom-call | flops 1073741824 | bytes 2097152 | tf_op jit(solution)/shard_map/middle2/pallas_call | solution.py:79
  89.0 2.1 %collective-permute-start.25 = (f32[1024,128]{1,0:T(8,128)S(1)}, f32[1024,128]{1,0:T(8,128)S(1)}, u32[]{:S(2)}, u32[]{:S(2)}) collective-permute-start(f32[1024,128]{1,0:T(8,128)S(1)} %join.3.base), channel_id=1, source_target_pairs={{0,4},{4,0},{8,12},{12,8},{16,20},{20,16},{24,28},{28,24},{32,36},... | collective-permute-start | bytes 1572872 | tf_op jit(solution)/shard_map/ppermute | solution.py:518
  91.1 0.7 last0.1
  91.8 0.8 collective-permute-done.25.base
  92.6 2.1 %last1.1 = (bf16[512,2048]{1,0:T(8,128)(2,1)}, bf16[512,2048]{1,0:T(8,128)(2,1)}) custom-call(s32[1]{0:T(128)} %bitcast.core, bf16[512,1024]{1,0:T(8,128)(2,1)S(1)} %get-tuple-element.82.k.refs_8_.refs_1_, bf16[512,1024]{1,0:T(8,128)(2,1)S(1)} %get-tuple-element.83.v.refs_9_.refs_2_, f32[1024,128]{1,0:T(8,128)S(1)} %collective-permute-done.25.base, ...), custom_call_target="tpu_custom_call" | custom-call | flops 268435456 | bytes 2097152 | tf_op jit(solution)/shard_map/last1/pallas_call | solution.py:79
  (50 shorter events, 0.2 us)
Async XLA Ops:
  3.4 3.5 %collective-permute-start = (f32[1024,128]{1,0:T(8,128)}, f32[1024,128]{1,0:T(8,128)S(1)}, u32[]{:S(2)}, u32[]{:S(2)}) collective-permute-start(f32[1024,128]{1,0:T(8,128)} %get-tuple-element.93), channel_id=1, source_target_pairs={{0,4},{4,0},{8,12},{12,8},{16,20},{20,16},{24,28},{28,24},{32,36},... | collective-permute-start | bytes 1572872 | tf_op jit(solution)/shard_map/ppermute | solution.py:518
  6.8 11.0 %copy-start = (bf16[512,1024]{1,0:T(8,128)(2,1)}, bf16[512,1024]{1,0:T(8,128)(2,1)S(1)}, u32[]{:S(2)}) copy-start(bf16[512,1024]{1,0:T(8,128)(2,1)S(1)} %get-tuple-element.96.k.refs_1_) | copy-start | bytes 3145732
  6.8 11.0 %copy-start.2 = (bf16[512,1024]{1,0:T(8,128)(2,1)}, bf16[512,1024]{1,0:T(8,128)(2,1)S(1)}, u32[]{:S(2)}) copy-start(bf16[512,1024]{1,0:T(8,128)(2,1)S(1)} %get-tuple-element.97.v.refs_2_) | copy-start | bytes 3145732
  6.9 0.9 copy-start.12
  7.8 0.8 copy-start.16
  8.6 13.7 %collective-permute-start.1 = (f32[256,128]{1,0:T(8,128)S(1)}, f32[256,128]{1,0:T(8,128)S(1)}, u32[]{:S(2)}, u32[]{:S(2)}) collective-permute-start(f32[256,128]{1,0:T(8,128)S(1)} %get-tuple-element.95), channel_id=1, source_target_pairs={{0,8},{4,12},{8,16},{12,20},{16,24},{20,28},{24,0},{28,4},{32,40},... | collective-permute-start | bytes 393224 | tf_op jit(solution)/shard_map/ppermute | solution.py:502
  9.9 12.4 %collective-permute-start.2 = (f32[256,128]{1,0:T(8,128)S(1)}, f32[256,128]{1,0:T(8,128)S(1)}, u32[]{:S(2)}, u32[]{:S(2)}) collective-permute-start(f32[256,128]{1,0:T(8,128)S(1)} %get-tuple-element.100), channel_id=1, source_target_pairs={{0,16},{4,20},{8,24},{12,28},{16,0},{20,4},{24,8},{28,12},{32,48},... | collective-permute-start | bytes 393224 | tf_op jit(solution)/shard_map/ppermute | solution.py:502
  12.4 10.0 %collective-permute-start.3 = (f32[256,128]{1,0:T(8,128)S(1)}, f32[256,128]{1,0:T(8,128)S(1)}, u32[]{:S(2)}, u32[]{:S(2)}) collective-permute-start(f32[256,128]{1,0:T(8,128)S(1)} %get-tuple-element.101), channel_id=1, source_target_pairs={{0,24},{4,28},{8,0},{12,4},{16,8},{20,12},{24,16},{28,20},{32,56},... | collective-permute-start | bytes 393224 | tf_op jit(solution)/shard_map/ppermute | solution.py:502
  17.8 1.3 %copy-start.4 = (bf16[4096,256]{1,0:T(8,128)(2,1)}, bf16[4096,256]{1,0:T(8,128)(2,1)S(1)}, u32[]{:S(2)}) copy-start(bf16[4096,256]{1,0:T(8,128)(2,1)S(1)} %get-tuple-element.123.refs_6_) | copy-start | bytes 6291460
  19.1 1.0 %copy-start.6 = (bf16[2048,256]{1,0:T(8,128)(2,1)}, bf16[2048,256]{1,0:T(8,128)(2,1)S(1)}, u32[]{:S(2)}) copy-start(bf16[2048,256]{1,0:T(8,128)(2,1)S(1)} %get-tuple-element.122.refs_5_) | copy-start | bytes 3145732
  20.1 1.0 %copy-start.8 = (bf16[512,1024]{1,0:T(8,128)(2,1)}, bf16[512,1024]{1,0:T(8,128)(2,1)S(1)}, u32[]{:S(2)}) copy-start(bf16[512,1024]{1,0:T(8,128)(2,1)S(1)} %get-tuple-element.110.o) | copy-start | bytes 3145732
  21.0 1.3 %copy-start.10 = (f32[512,1024]{1,0:T(8,128)}, f32[512,1024]{1,0:T(8,128)S(1)}, u32[]{:S(2)}) copy-start(f32[512,1024]{1,0:T(8,128)S(1)} %get-tuple-element.98.intra) | copy-start | bytes 6291460
  23.0 0.6 copy-start.14
  23.7 7.0 %collective-permute-start.4 = (f32[256,128]{1,0:T(8,128)}, f32[256,128]{1,0:T(8,128)}, u32[]{:S(2)}, u32[]{:S(2)}) collective-permute-start(f32[256,128]{1,0:T(8,128)} %line.2), channel_id=1, source_target_pairs={{0,32},{4,36},{8,40},{12,44},{16,48},{20,52},{24,56},{28,60},{32,6... | collective-permute-start | bytes 393224 | tf_op jit(solution)/shard_map/ppermute | solution.py:513
  25.0 5.7 %collective-permute-start.6 = (f32[256,128]{1,0:T(8,128)}, f32[256,128]{1,0:T(8,128)}, u32[]{:S(2)}, u32[]{:S(2)}) collective-permute-start(f32[256,128]{1,0:T(8,128)} %line.2), channel_id=1, source_target_pairs={{0,96},{4,100},{8,104},{12,108},{16,112},{20,116},{24,120},{28,124... | collective-permute-start | bytes 393224 | tf_op jit(solution)/shard_map/ppermute | solution.py:513
  26.4 7.3 %collective-permute-start.5 = (f32[256,128]{1,0:T(8,128)}, f32[256,128]{1,0:T(8,128)}, u32[]{:S(2)}, u32[]{:S(2)}) collective-permute-start(f32[256,128]{1,0:T(8,128)} %line.2), channel_id=1, source_target_pairs={{0,64},{4,68},{8,72},{12,76},{16,80},{20,84},{24,88},{28,92},{32,9... | collective-permute-start | bytes 393224 | tf_op jit(solution)/shard_map/ppermute | solution.py:513
  28.1 5.7 %copy-start.15 = (f32[256,128]{1,0:T(8,128)S(1)}, f32[256,128]{1,0:T(8,128)}, u32[]{:S(2)}) copy-start(f32[256,128]{1,0:T(8,128)} %copy-done.14) | copy-start | bytes 393220
  28.1 9.8 %copy-start.17 = (f32[1024,128]{1,0:T(8,128)S(1)}, f32[1024,128]{1,0:T(8,128)}, u32[]{:S(2)}) copy-start(f32[1024,128]{1,0:T(8,128)} %copy-done.16) | copy-start | bytes 1572868
  35.0 7.7 %collective-permute-start.7 = (f32[256,128]{1,0:T(8,128)S(1)}, f32[256,128]{1,0:T(8,128)S(1)}, u32[]{:S(2)}, u32[]{:S(2)}) collective-permute-start(f32[256,128]{1,0:T(8,128)S(1)} %get-tuple-element.104), channel_id=1, source_target_pairs={{0,8},{4,12},{8,16},{12,20},{16,24},{20,28},{24,0},{28,4},{32,40},... | collective-permute-start | bytes 393224 | tf_op jit(solution)/shard_map/ppermute | solution.py:502
  35.4 7.3 %collective-permute-start.8 = (f32[256,128]{1,0:T(8,128)S(1)}, f32[256,128]{1,0:T(8,128)S(1)}, u32[]{:S(2)}, u32[]{:S(2)}) collective-permute-start(f32[256,128]{1,0:T(8,128)S(1)} %get-tuple-element.106), channel_id=1, source_target_pairs={{0,16},{4,20},{8,24},{12,28},{16,0},{20,4},{24,8},{28,12},{32,48},... | collective-permute-start | bytes 393224 | tf_op jit(solution)/shard_map/ppermute | solution.py:502
  36.2 6.7 %collective-permute-start.9 = (f32[256,128]{1,0:T(8,128)S(1)}, f32[256,128]{1,0:T(8,128)S(1)}, u32[]{:S(2)}, u32[]{:S(2)}) collective-permute-start(f32[256,128]{1,0:T(8,128)S(1)} %get-tuple-element.107), channel_id=1, source_target_pairs={{0,24},{4,28},{8,0},{12,4},{16,8},{20,12},{24,16},{28,20},{32,56},... | collective-permute-start | bytes 393224 | tf_op jit(solution)/shard_map/ppermute | solution.py:502
  37.9 8.9 %collective-permute-start.11 = (f32[1024,128]{1,0:T(8,128)S(1)}, f32[1024,128]{1,0:T(8,128)S(1)}, u32[]{:S(2)}, u32[]{:S(2)}) collective-permute-start(f32[1024,128]{1,0:T(8,128)S(1)} %copy-done.17), channel_id=1, source_target_pairs={{0,4},{4,0},{8,12},{12,8},{16,20},{20,16},{24,28},{28,24},{32,36},... | collective-permute-start | bytes 1572872 | tf_op jit(solution)/shard_map/ppermute | solution.py:518
  39.9 6.0 %copy-start.9 = (bf16[512,1024]{1,0:T(8,128)(2,1)S(1)}, bf16[512,1024]{1,0:T(8,128)(2,1)}, u32[]{:S(2)}) copy-start(bf16[512,1024]{1,0:T(8,128)(2,1)} %copy-done.8) | copy-start | bytes 3145732
  40.0 6.0 %copy-start.11 = (f32[512,1024]{1,0:T(8,128)S(1)}, f32[512,1024]{1,0:T(8,128)}, u32[]{:S(2)}) copy-start(f32[512,1024]{1,0:T(8,128)} %copy-done.10) | copy-start | bytes 6291460
  40.0 6.0 %copy-start.13 = (f32[1024,128]{1,0:T(8,128)S(1)}, f32[1024,128]{1,0:T(8,128)}, u32[]{:S(2)}) copy-start(f32[1024,128]{1,0:T(8,128)} %copy-done.12) | copy-start | bytes 1572868
  40.0 6.0 %copy-start.18 = (f32[2048]{0:T(1024)S(1)}, f32[2048]{0:T(1024)}, u32[]{:S(2)}) copy-start(f32[2048]{0:T(1024)} %param.9) | copy-start | bytes 24580
  43.0 4.5 %collective-permute-start.10 = (f32[1024,128]{1,0:T(8,128)S(1)}, f32[1024,128]{1,0:T(8,128)S(1)}, u32[]{:S(2)}, u32[]{:S(2)}) collective-permute-start(f32[1024,128]{1,0:T(8,128)S(1)} %join.2.base), channel_id=1, source_target_pairs={{0,4},{4,0},{8,12},{12,8},{16,20},{20,16},{24,28},{28,24},{32,36},... | collective-permute-start | bytes 1572872 | tf_op jit(solution)/shard_map/ppermute | solution.py:518
  48.4 4.6 %collective-permute-start.14 = (f32[2,512]{1,0:T(2,128)S(1)}, f32[2,512]{1,0:T(2,128)S(1)}, u32[]{:S(2)}, u32[]{:S(2)}) collective-permute-start(f32[2,512]{1,0:T(2,128)S(1)} %get-tuple-element.114.s0), channel_id=1, source_target_pairs={{0,3},{1,0},{2,1},{3,2},{4,7},{5,4},{6,5},{7,6},{8,11},{9,8},{10,9... | collective-permute-start | bytes 12296 | tf_op jit(solution)/shard_map/ppermute | solution.py:523
  52.2 4.0 %collective-permute-start.13 = (f32[2,512]{1,0:T(2,128)S(1)}, f32[2,512]{1,0:T(2,128)S(1)}, u32[]{:S(2)}, u32[]{:S(2)}) collective-permute-start(f32[2,512]{1,0:T(2,128)S(1)} %get-tuple-element.114.s0), channel_id=1, source_target_pairs={{0,2},{1,3},{2,0},{3,1},{4,6},{5,7},{6,4},{7,5},{8,10},{9,11},{10,... | collective-permute-start | bytes 12296 | tf_op jit(solution)/shard_map/ppermute | solution.py:523
  52.2 4.0 %collective-permute-start.12 = (f32[2,512]{1,0:T(2,128)S(1)}, f32[2,512]{1,0:T(2,128)S(1)}, u32[]{:S(2)}, u32[]{:S(2)}) collective-permute-start(f32[2,512]{1,0:T(2,128)S(1)} %get-tuple-element.114.s0), channel_id=1, source_target_pairs={{0,1},{1,2},{2,3},{3,0},{4,5},{5,6},{6,7},{7,4},{8,9},{9,10},{10,1... | collective-permute-start | bytes 12296 | tf_op jit(solution)/shard_map/ppermute | solution.py:523
  57.2 3.4 %collective-permute-start.15 = (f32[1024,128]{1,0:T(8,128)S(1)}, f32[1024,128]{1,0:T(8,128)S(1)}, u32[]{:S(2)}, u32[]{:S(2)}) collective-permute-start(f32[1024,128]{1,0:T(8,128)S(1)} %get-tuple-element.128), channel_id=1, source_target_pairs={{0,4},{4,0},{8,12},{12,8},{16,20},{20,16},{24,28},{28,24},{32,36},... | collective-permute-start | bytes 1572872 | tf_op jit(solution)/shard_map/ppermute | solution.py:518
  59.1 5.0 %copy-start.1 = (bf16[512,1024]{1,0:T(8,128)(2,1)S(1)}, bf16[512,1024]{1,0:T(8,128)(2,1)}, u32[]{:S(2)}) copy-start(bf16[512,1024]{1,0:T(8,128)(2,1)} %copy-done) | copy-start | bytes 3145732
  59.1 5.0 %copy-start.3 = (bf16[512,1024]{1,0:T(8,128)(2,1)S(1)}, bf16[512,1024]{1,0:T(8,128)(2,1)}, u32[]{:S(2)}) copy-start(bf16[512,1024]{1,0:T(8,128)(2,1)} %copy-done.2) | copy-start | bytes 3145732
  59.1 5.0 %copy-start.5 = (bf16[4096,256]{1,0:T(8,128)(2,1)S(1)}, bf16[4096,256]{1,0:T(8,128)(2,1)}, u32[]{:S(2)}) copy-start(bf16[4096,256]{1,0:T(8,128)(2,1)} %copy-done.4) | copy-start | bytes 6291460
  59.1 5.0 %copy-start.7 = (bf16[2048,256]{1,0:T(8,128)(2,1)S(1)}, bf16[2048,256]{1,0:T(8,128)(2,1)}, u32[]{:S(2)}) copy-start(bf16[2048,256]{1,0:T(8,128)(2,1)} %copy-done.6) | copy-start | bytes 3145732
  60.6 7.7 %collective-permute-start.16 = (f32[256,128]{1,0:T(8,128)S(1)}, f32[256,128]{1,0:T(8,128)S(1)}, u32[]{:S(2)}, u32[]{:S(2)}) collective-permute-start(f32[256,128]{1,0:T(8,128)S(1)} %get-tuple-element.130), channel_id=1, source_target_pairs={{0,8},{4,12},{8,16},{12,20},{16,24},{20,28},{24,0},{28,4},{32,40},... | collective-permute-start | bytes 393224 | tf_op jit(solution)/shard_map/ppermute | solution.py:502
  60.8 9.3 %collective-permute-start.17 = (f32[256,128]{1,0:T(8,128)S(1)}, f32[256,128]{1,0:T(8,128)S(1)}, u32[]{:S(2)}, u32[]{:S(2)}) collective-permute-start(f32[256,128]{1,0:T(8,128)S(1)} %get-tuple-element.132), channel_id=1, source_target_pairs={{0,16},{4,20},{8,24},{12,28},{16,0},{20,4},{24,8},{28,12},{32,48},... | collective-permute-start | bytes 393224 | tf_op jit(solution)/shard_map/ppermute | solution.py:502
  64.1 6.1 %collective-permute-start.18 = (f32[256,128]{1,0:T(8,128)S(1)}, f32[256,128]{1,0:T(8,128)S(1)}, u32[]{:S(2)}, u32[]{:S(2)}) collective-permute-start(f32[256,128]{1,0:T(8,128)S(1)} %get-tuple-element.133), channel_id=1, source_target_pairs={{0,24},{4,28},{8,0},{12,4},{16,8},{20,12},{24,16},{28,20},{32,56},... | collective-permute-start | bytes 393224 | tf_op jit(solution)/shard_map/ppermute | solution.py:502
  70.2 8.3 %collective-permute-start.21 = (f32[256,128]{1,0:T(8,128)S(1)}, f32[256,128]{1,0:T(8,128)S(1)}, u32[]{:S(2)}, u32[]{:S(2)}) collective-permute-start(f32[256,128]{1,0:T(8,128)S(1)} %line.3), channel_id=1, source_target_pairs={{0,32},{4,36},{8,40},{12,44},{16,48},{20,52},{24,56},{28,60},{32,6... | collective-permute-start | bytes 393224 | tf_op jit(solution)/shard_map/ppermute | solution.py:513
  70.4 8.0 %collective-permute-start.20 = (f32[256,128]{1,0:T(8,128)S(1)}, f32[256,128]{1,0:T(8,128)S(1)}, u32[]{:S(2)}, u32[]{:S(2)}) collective-permute-start(f32[256,128]{1,0:T(8,128)S(1)} %line.3), channel_id=1, source_target_pairs={{0,64},{4,68},{8,72},{12,76},{16,80},{20,84},{24,88},{28,92},{32,9... | collective-permute-start | bytes 393224 | tf_op jit(solution)/shard_map/ppermute | solution.py:513
  72.9 5.6 %collective-permute-start.19 = (f32[256,128]{1,0:T(8,128)S(1)}, f32[256,128]{1,0:T(8,128)S(1)}, u32[]{:S(2)}, u32[]{:S(2)}) collective-permute-start(f32[256,128]{1,0:T(8,128)S(1)} %line.3), channel_id=1, source_target_pairs={{0,96},{4,100},{8,104},{12,108},{16,112},{20,116},{24,120},{28,124... | collective-permute-start | bytes 393224 | tf_op jit(solution)/shard_map/ppermute | solution.py:513
  78.6 10.3 %collective-permute-start.22 = (f32[256,128]{1,0:T(8,128)S(1)}, f32[256,128]{1,0:T(8,128)S(1)}, u32[]{:S(2)}, u32[]{:S(2)}) collective-permute-start(f32[256,128]{1,0:T(8,128)S(1)} %get-tuple-element.136), channel_id=1, source_target_pairs={{0,8},{4,12},{8,16},{12,20},{16,24},{20,28},{24,0},{28,4},{32,40},... | collective-permute-start | bytes 393224 | tf_op jit(solution)/shard_map/ppermute | solution.py:502
  79.1 9.8 %collective-permute-start.23 = (f32[256,128]{1,0:T(8,128)S(1)}, f32[256,128]{1,0:T(8,128)S(1)}, u32[]{:S(2)}, u32[]{:S(2)}) collective-permute-start(f32[256,128]{1,0:T(8,128)S(1)} %get-tuple-element.138), channel_id=1, source_target_pairs={{0,16},{4,20},{8,24},{12,28},{16,0},{20,4},{24,8},{28,12},{32,48},... | collective-permute-start | bytes 393224 | tf_op jit(solution)/shard_map/ppermute | solution.py:502
  83.6 5.3 %collective-permute-start.24 = (f32[256,128]{1,0:T(8,128)S(1)}, f32[256,128]{1,0:T(8,128)S(1)}, u32[]{:S(2)}, u32[]{:S(2)}) collective-permute-start(f32[256,128]{1,0:T(8,128)S(1)} %get-tuple-element.139), channel_id=1, source_target_pairs={{0,24},{4,28},{8,0},{12,4},{16,8},{20,12},{24,16},{28,20},{32,56},... | collective-permute-start | bytes 393224 | tf_op jit(solution)/shard_map/ppermute | solution.py:502
  83.6 8.2 %collective-permute-start.26 = (f32[1024,128]{1,0:T(8,128)S(1)}, f32[1024,128]{1,0:T(8,128)S(1)}, u32[]{:S(2)}, u32[]{:S(2)}) collective-permute-start(f32[1024,128]{1,0:T(8,128)S(1)} %get-tuple-element.140.own), channel_id=1, source_target_pairs={{0,4},{4,0},{8,12},{12,8},{16,20},{20,16},{24,28},{28,24},{32,36},... | collective-permute-start | bytes 1572872 | tf_op jit(solution)/shard_map/ppermute | solution.py:518
  89.0 3.6 %collective-permute-start.25 = (f32[1024,128]{1,0:T(8,128)S(1)}, f32[1024,128]{1,0:T(8,128)S(1)}, u32[]{:S(2)}, u32[]{:S(2)}) collective-permute-start(f32[1024,128]{1,0:T(8,128)S(1)} %join.3.base), channel_id=1, source_target_pairs={{0,4},{4,0},{8,12},{12,8},{16,20},{20,16},{24,28},{28,24},{32,36},... | collective-permute-start | bytes 1572872 | tf_op jit(solution)/shard_map/ppermute | solution.py:518

commit v5 on v4

--- a/solution.py
+++ b/solution.py
@@ -244,14 +244,13 @@
     )(core, queries, out_grad, k, v, *begun)
 
 
-def output_body(side, core, q, o, intra, gain, base, near, *refs):
+def output_body(side, core, q, o, intra, gain, base, *refs):
     if side == 0:
         output, prefix_half, squares, products = refs
     else:
         squares_in, products_in, output, prefix_half, stats = refs
-    weight = core[0].astype(F32)
     gains = gain[:, pl.ds(side_start(core, side), SIDE)]
-    prefix_half[...] = (base[...] + weight * near[...]).astype(BF16)
+    prefix_half[...] = base[...].astype(BF16)
     parts = (TOP, BOTTOM)
     if side == 0:
         square_sums = [jnp.zeros((HALF, DH), F32) for rows in parts]
@@ -278,16 +277,16 @@
             stats[1:2, rows] = jnp.sum(product_sums[part].T, axis=0, keepdims=True)
 
 
-def whole_output(side, core, q, o, intra, gain, base, near, sums=()):
+def whole_output(side, core, q, o, intra, gain, base, sums=()):
     return call(
         f"output{side}",
         functools.partial(output_body, side),
-        [SMEM] + [VMEM] * (6 + len(sums)),
+        [SMEM] + [VMEM] * (5 + len(sums)),
         [VMEM] * (4 if side == 0 else 3),
         [SIDE_F32, STATE_HALF] + ([LANES, LANES] if side == 0 else [STATS]),
         2 * BLOCK * SIDE * DH,
         MIB,
-    )(core, q, o, intra, gain, base, near, *sums)
+    )(core, q, o, intra, gain, base, *sums)
 
 
 def grad_body(side, core, q, output, o, gain, s0, s1, s2, s3, grad_out, states):
@@ -378,48 +377,37 @@
     return query_grad, {job: parts[2 * i : 2 * i + 2] for i, job in enumerate(jobs)}
 
 
-def last_body(side, core, k, v, base, near, *refs):
+def last_body(side, core, k, v, base, *refs):
     parts = refs[: 2 * PAIRS_SIDE]
-    if side == 0:
-        key_half, value_half = refs[2 * PAIRS_SIDE :]
-    else:
-        key_own, value_own, key_grad, value_grad, key_half, value_half, sems = refs[2 * PAIRS_SIDE :]
-        own = pl.ds(side_start(core, 0), SIDE)
-        results = copies_of(
-            [(key_own, key_grad.at[:, own]), (value_own, value_grad.at[:, own])],
-            sems.at[pl.ds(2 * PAIRS_SIDE, 2)],
-        )
-    weight = 1.0 - core[0].astype(F32)
-    later = (base[...] + weight * near[...]).astype(BF16)
+    key_grad, value_grad, key_half, value_half, sems = refs[-5:]
+    later = base[...].astype(BF16)
+    results = []
     for pair in PAIRS:
         cols = pair_columns(pair)
         states = diagonal(later, pair)
         key_half[:, cols] = (parts[2 * pair][...] + dot_nt(v[:, cols], states)).astype(BF16)
         value_half[:, cols] = (parts[2 * pair + 1][...] + dot(k[:, cols], states)).astype(BF16)
-        if side == 1:
-            window = pair_window(core, side, pair)
-            results += copies_of(
-                [(key_half.at[:, cols], key_grad.at[:, window]), (value_half.at[:, cols], value_grad.at[:, window])],
-                sems.at[pl.ds(2 * pair, 2)],
-            )
-    if side == 1:
-        wait(results)
-
-
-def last_gradients(side, core, k, v, base, near, parts, own=()):
-    inputs = [k, v, base, near] + [array for pair in PAIRS for array in parts[side, pair]] + list(own)
+        window = pair_window(core, side, pair)
+        results += copies_of(
+            [(key_half.at[:, cols], key_grad.at[:, window]), (value_half.at[:, cols], value_grad.at[:, window])],
+            sems.at[pl.ds(2 * pair, 2)],
+        )
+    wait(results)
+
+
+def last_gradients(side, core, k, v, base, parts, results=()):
+    inputs = [k, v, base] + [array for pair in PAIRS for array in parts[side, pair]]
     return call(
         f"last{side}",
         functools.partial(last_body, side),
-        [SMEM] + [VMEM] * len(inputs),
-        [VMEM, VMEM] if side == 0 else [HBM, HBM],
-        [SIDE_BF16, SIDE_BF16] if side == 0 else [WHOLE, WHOLE],
+        [SMEM] + [VMEM] * len(inputs) + [HBM] * len(results),
+        [HBM, HBM],
+        [WHOLE, WHOLE],
         4 * BLOCK * SIDE * DH,
         2 * MIB,
-        []
-        if side == 0
-        else [BUFFER_BF16, BUFFER_BF16, pltpu.SemaphoreType.DMA((2 * PAIRS_SIDE + 2,))],
-    )(core, *inputs)
+        [BUFFER_BF16, BUFFER_BF16, pltpu.SemaphoreType.DMA((2 * PAIRS_SIDE,))],
+        {1 + len(inputs) + i: i for i in range(len(results))},
+    )(core, *inputs, *results)
 
 
 def quarter(place):
@@ -475,13 +463,28 @@
     )(*chip, *pieces, *sums)
 
 
-def join_body(x, a, b, c, d, out):
+def join_body(reverse, x, core, a, b, c, d, own, near, here, there):
+    first = core[0].astype(F32)
+    second = 1.0 - first
+    if reverse:
+        first, second = second, first
     for hop, piece in enumerate((a, b, c, d)):
-        out[quarter(lax.rem(x[0] + LINE - hop, LINE)), :] = piece[...]
-
-
-def join(chip, pieces):
-    return call("join", join_body, [SMEM] + [VMEM] * LINE, VMEM, STATE, MIB, MIB)(chip[0], *pieces)
+        rows = quarter(lax.rem(x[0] + LINE - hop, LINE))
+        here[rows, :] = piece[...] + first * near[rows, :]
+        there[rows, :] = piece[...] + second * own[rows, :]
+
+
+def join(chip, core, pieces, own, near, reverse):
+    here, there = call(
+        f"join{int(reverse)}",
+        functools.partial(join_body, reverse),
+        [SMEM] * 2 + [VMEM] * (LINE + 2),
+        [VMEM] * 2,
+        [STATE, STATE],
+        MIB,
+        MIB,
+    )(chip[0], core, *pieces, own, near)
+    return here, swap(there)
 
 
 def device_index(y, x, core):
@@ -529,9 +532,9 @@
 
 def local(query_rows, key_rows, value_rows, out_grad, norm_gain):
     place = lax.axis_index("ctx").astype(jnp.int32)
-    core = (place % 2).reshape(1)
-    chip = ((place // 2 % LINE).reshape(1), (place // (2 * LINE)).reshape(1))
-    return device(core, chip, query_rows, key_rows, value_rows, out_grad, norm_gain)
+    core, x, y = place % 2, place // 2 % LINE, place // (2 * LINE)
+    core, x, y = lax.optimization_barrier((core.reshape(1), x.reshape(1), y.reshape(1)))
+    return device(core, (x, y), query_rows, key_rows, value_rows, out_grad, norm_gain)
 
 
 def device(core, chip, query_rows, key_rows, value_rows, out_grad, norm_gain):
@@ -547,13 +550,11 @@
     begun = intra_output(1, 1, PAIRS[:2], core, query_rows, out_grad, k1, v1)
     sums[0] = after(sums[0], begun[2])
     pieces = along_x(entering(chip, pieces, sums, False))
-    near1 = swap(after(state0, sums[0]))
     q1, o1, intra1, *turned1 = intra_output(2, 1, PAIRS[2:], core, query_rows, out_grad, k1, v1, begun)
     pieces[1] = after(pieces[1], intra1)
-    base0 = join(chip, pieces)
-    base1 = swap(base0)
-    output0, prefix0, *lanes = whole_output(0, core, q0, o0, intra0, gain, base0, near0)
-    output1, prefix1, stats = whole_output(1, core, q1, o1, intra1, gain, base1, near1, lanes)
+    base0, base1 = join(chip, core, pieces, state0, near0, False)
+    output0, prefix0, *lanes = whole_output(0, core, q0, o0, intra0, gain, base0)
+    output1, prefix1, stats = whole_output(1, core, q1, o1, intra1, gain, base1, lanes)
     stats = [stats] + along_heads(stats)
 
     g1, state1 = local_grad(1, core, q1, output1, o1, gain, stats)
@@ -568,14 +569,12 @@
     parts.update(more)
     sums[0] = after(sums[0], query_grad)
     pieces = along_x(entering(chip, pieces, sums, True))
-    near1 = swap(after(state0, sums[0]))
     query_grad, more = middle_gradients(2, ((1, 2), (1, 3)), core, arrays, (query_grad,))
     parts.update(more)
     pieces[1] = after(pieces[1], query_grad)
-    base0 = join(chip, pieces)
-    base1 = swap(base0)
-    results = last_gradients(0, core, k0, v0, base0, near0, parts)
-    key_grad, value_grad = last_gradients(1, core, k1, v1, base1, near1, parts, results)
+    base0, base1 = join(chip, core, pieces, state0, near0, True)
+    results = last_gradients(0, core, k0, v0, base0, parts)
+    key_grad, value_grad = last_gradients(1, core, k1, v1, base1, parts, results)
     return query_grad, key_grad, value_grad
 
 

time: 95.1 us -> 85.8 us (0.902)
  local copies, waits for them, and re-layouts: 7 us -> 0.01 us
  Pallas kernels: 34.5 us -> 32.5 us
  starting transfers between devices: 40.6 us -> 39.3 us
  waiting for transfers between devices: 11.6 us -> 12.7 us
    unnamed x38 -> x2, local copies, waits for them, and re-layouts: 7 us -> 0.01 us
    ppermute x6 -> x4, starting transfers between devices: 12.7 us -> 8.99 us  [swap(): return lax.ppermute(part, 'ctx', PARTNERS)]
    ppermute x12, starting transfers between devices: 16.2 us -> 18.5 us  [along_x(): got[hop] = lax.ppermute(pieces[hop], 'ctx', pairs)]
    ppermute x12, waiting for transfers between devices: 2.02 us -> 4.09 us  [along_x(): got[hop] = lax.ppermute(pieces[hop], 'ctx', pairs)]
    pallas_call x22, Pallas kernels: 34.5 us -> 32.5 us  [run(): kernel(*(pltpu.with_memory_space_constraint(array, pltpu.HBM) if spec is...]
    ppermute x6 -> x4, waiting for transfers between devices: 2.06 us -> 1.4 us  [swap(): return lax.ppermute(part, 'ctx', PARTNERS)]
  transfers between devices with their start and end apart: 27 -> 25, of which waited for: 9 -> 11; matrix products, arithmetic and copies ran while one was open for 0% -> 0% of each run, Pallas kernels for 27% -> 31%
where the time goes in v5:
time: 85.8 us; the launch traced here: 85.6 us
  starting transfers between devices  39.3 us (46%)
  Pallas kernels  32.5 us (38%)
  waiting for transfers between devices  12.7 us (15%)
  between operations  1.06 us (1%)
    pallas_call x22, Pallas kernels, run(): kernel(*(pltpu.with_memory_space_constraint(array, pltpu.HBM) if spec is...  32.5 us
    ppermute x12, starting transfers between devices, along_x(): got[hop] = lax.ppermute(pieces[hop], 'ctx', pairs)  18.5 us
    ppermute x4, starting transfers between devices, swap(): return lax.ppermute(part, 'ctx', PARTNERS)  8.99 us
    ppermute x6, starting transfers between devices, along_y(): got[hop] = lax.ppermute(part, 'ctx', pairs)  7.33 us
    ppermute x3, starting transfers between devices, along_heads(): lax.ppermute(stats, 'head', [(i, (i + hop) % 4) for i in range(4)])  4.53 us
    ppermute x12, waiting for transfers between devices, along_x(): got[hop] = lax.ppermute(pieces[hop], 'ctx', pairs)  4.09 us
    ppermute x6, waiting for transfers between devices, along_y(): got[hop] = lax.ppermute(part, 'ctx', pairs)  3.95 us
    ppermute x3, waiting for transfers between devices, along_heads(): lax.ppermute(stats, 'head', [(i, (i + hop) % 4) for i in range(4)])  3.24 us
  transfers between devices with their start and end apart: 25, of which 11 were waited for; matrix products, arithmetic and copies ran while one was open for 0% of the time, Pallas kernels for 31%

profile of v5, /device:TPU:1, one launch (start us, length us, event | category | flops | bytes accessed | tf_op | source)
XLA Modules:
  0.0 85.6 jit_solution(10634134945993626631)
XLA Ops:
  0.7 1.9 %state1.1 = (bf16[512,1024]{1,0:T(8,128)(2,1)S(1)}, bf16[512,1024]{1,0:T(8,128)(2,1)S(1)}, f32[1024,128]{1,0:T(8,128)S(1)}) custom-call(s32[1]{0:T(128)} %bitcast.core, bf16[512,2048]{1,0:T(8,128)(2,1)} %k_all.3, bf16[512,2048]{1,0:T(8,128)(2,1)} %v_all.3), custom_call_target="tpu_custom_call" | custom-call | flops 134217728 | bytes 2097152 | tf_op jit(solution)/shard_map/state1/pallas_call | solution.py:79
  2.6 1.5 %collective-permute-start = (f32[1024,128]{1,0:T(8,128)S(1)}, f32[1024,128]{1,0:T(8,128)S(1)}, u32[]{:S(2)}, u32[]{:S(2)}) collective-permute-start(f32[1024,128]{1,0:T(8,128)S(1)} %get-tuple-element.101), channel_id=1, source_target_pairs={{0,4},{4,0},{8,12},{12,8},{16,20},{20,16},{24,28},{28,24},{32,36},... | collective-permute-start | bytes 1572872 | tf_op jit(solution)/shard_map/ppermute | solution.py:521
  4.1 1.9 %state0.1 = (bf16[512,1024]{1,0:T(8,128)(2,1)S(1)}, bf16[512,1024]{1,0:T(8,128)(2,1)S(1)}, f32[1024,128]{1,0:T(8,128)S(1)}) custom-call(s32[1]{0:T(128)} %bitcast.core, bf16[512,2048]{1,0:T(8,128)(2,1)} %k_all.3, bf16[512,2048]{1,0:T(8,128)(2,1)} %v_all.3), custom_call_target="tpu_custom_call" | custom-call | flops 134217728 | bytes 2097152 | tf_op jit(solution)/shard_map/state0/pallas_call | solution.py:79
  6.0 0.0 collective-permute-done.near
  6.0 0.1 split.2
  6.1 1.4 %collective-permute-start.1 = (f32[256,128]{1,0:T(8,128)S(1)}, f32[256,128]{1,0:T(8,128)S(1)}, u32[]{:S(2)}, u32[]{:S(2)}) collective-permute-start(f32[256,128]{1,0:T(8,128)S(1)} %get-tuple-element.103), channel_id=1, source_target_pairs={{0,8},{4,12},{8,16},{12,20},{16,24},{20,28},{24,0},{28,4},{32,40},... | collective-permute-start | bytes 393224 | tf_op jit(solution)/shard_map/ppermute | solution.py:505
  7.5 2.4 %collective-permute-start.2 = (f32[256,128]{1,0:T(8,128)S(1)}, f32[256,128]{1,0:T(8,128)S(1)}, u32[]{:S(2)}, u32[]{:S(2)}) collective-permute-start(f32[256,128]{1,0:T(8,128)S(1)} %get-tuple-element.108), channel_id=1, source_target_pairs={{0,16},{4,20},{8,24},{12,28},{16,0},{20,4},{24,8},{28,12},{32,48},... | collective-permute-start | bytes 393224 | tf_op jit(solution)/shard_map/ppermute | solution.py:505
  9.9 1.2 %collective-permute-start.3 = (f32[256,128]{1,0:T(8,128)S(1)}, f32[256,128]{1,0:T(8,128)S(1)}, u32[]{:S(2)}, u32[]{:S(2)}) collective-permute-start(f32[256,128]{1,0:T(8,128)S(1)} %get-tuple-element.109), channel_id=1, source_target_pairs={{0,24},{4,28},{8,0},{12,4},{16,8},{20,12},{24,16},{28,20},{32,56},... | collective-permute-start | bytes 393224 | tf_op jit(solution)/shard_map/ppermute | solution.py:505
  11.1 4.2 %intra0.1 = (bf16[512,1024]{1,0:T(8,128)(2,1)S(1)}, bf16[512,1024]{1,0:T(8,128)(2,1)S(1)}, f32[512,1024]{1,0:T(8,128)S(1)}, bf16[2048,256]{1,0:T(8,128)(2,1)S(1)}, bf16[4096,256]{1,0:T(8,128)(2,1)S(1)}) custom-call(s32[1]{0:T(128)} %bitcast.core, bf16[512,2048]{1,0:T(8,128)(2,1)} %q_all.5, bf16[512,2048]{1,0:T(8,128)(2,1)} %o_all.5, ...), custom_call_target="tpu_custom_call" | custom-call | flops 1342177280 | bytes 8388608 | tf_op jit(solution)/shard_map/intra0/pallas_call | solution.py:79
  15.3 0.0 collective-permute-done.1.b.refs_1_
  15.3 1.1 %collective-permute-done.2.c.refs_2_ = f32[256,128]{1,0:T(8,128)S(1)} collective-permute-done((f32[256,128]{1,0:T(8,128)S(1)}, f32[256,128]{1,0:T(8,128)S(1)}, u32[]{:S(2)}, u32[]{:S(2)}) %collective-permute-start.2) | collective-permute-done | bytes 131104 | tf_op jit(solution)/shard_map/ppermute | solution.py:505
  16.4 0.0 collective-permute-done.3.d.refs_3_
  16.4 1.4 %collective-permute-start.4 = (f32[256,128]{1,0:T(8,128)S(1)}, f32[256,128]{1,0:T(8,128)S(1)}, u32[]{:S(2)}, u32[]{:S(2)}) collective-permute-start(f32[256,128]{1,0:T(8,128)S(1)} %line.2), channel_id=1, source_target_pairs={{0,32},{4,36},{8,40},{12,44},{16,48},{20,52},{24,56},{28,60},{32,6... | collective-permute-start | bytes 393224 | tf_op jit(solution)/shard_map/ppermute | solution.py:516
  17.8 1.5 %collective-permute-start.6 = (f32[256,128]{1,0:T(8,128)S(1)}, f32[256,128]{1,0:T(8,128)S(1)}, u32[]{:S(2)}, u32[]{:S(2)}) collective-permute-start(f32[256,128]{1,0:T(8,128)S(1)} %line.2), channel_id=1, source_target_pairs={{0,96},{4,100},{8,104},{12,108},{16,112},{20,116},{24,120},{28,124... | collective-permute-start | bytes 393224 | tf_op jit(solution)/shard_map/ppermute | solution.py:516
  19.3 1.6 %collective-permute-start.5 = (f32[256,128]{1,0:T(8,128)S(1)}, f32[256,128]{1,0:T(8,128)S(1)}, u32[]{:S(2)}, u32[]{:S(2)}) collective-permute-start(f32[256,128]{1,0:T(8,128)S(1)} %line.2), channel_id=1, source_target_pairs={{0,64},{4,68},{8,72},{12,76},{16,80},{20,84},{24,88},{28,92},{32,9... | collective-permute-start | bytes 393224 | tf_op jit(solution)/shard_map/ppermute | solution.py:516
  20.9 2.6 %intra1.1 = (bf16[512,1024]{1,0:T(8,128)(2,1)S(1)}, bf16[512,1024]{1,0:T(8,128)(2,1)S(1)}, f32[512,1024]{1,0:T(8,128)S(1)}, bf16[2048,256]{1,0:T(8,128)(2,1)S(1)}, bf16[4096,256]{1,0:T(8,128)(2,1)S(1)}) custom-call(s32[1]{0:T(128)} %bitcast.core, bf16[512,2048]{1,0:T(8,128)(2,1)} %q_all.5, bf16[512,2048]{1,0:T(8,128)(2,1)} %o_all.5, ...), custom_call_target="tpu_custom_call" | custom-call | flops 671088640 | bytes 4194304 | tf_op jit(solution)/shard_map/intra1/pallas_call | solution.py:79
  23.5 0.0 collective-permute-done.6.refs_6_
  23.5 2.8 %collective-permute-done.5.refs_5_ = f32[256,128]{1,0:T(8,128)S(1)} collective-permute-done((f32[256,128]{1,0:T(8,128)S(1)}, f32[256,128]{1,0:T(8,128)S(1)}, u32[]{:S(2)}, u32[]{:S(2)}) %collective-permute-start.5) | collective-permute-done | bytes 131104 | tf_op jit(solution)/shard_map/ppermute | solution.py:516
  26.3 0.2 enter0.1
  26.5 0.8 collective-permute-start.7
  27.3 2.4 %collective-permute-start.8 = (f32[256,128]{1,0:T(8,128)S(1)}, f32[256,128]{1,0:T(8,128)S(1)}, u32[]{:S(2)}, u32[]{:S(2)}) collective-permute-start(f32[256,128]{1,0:T(8,128)S(1)} %get-tuple-element.114), channel_id=1, source_target_pairs={{0,16},{4,20},{8,24},{12,28},{16,0},{20,4},{24,8},{28,12},{32,48},... | collective-permute-start | bytes 393224 | tf_op jit(solution)/shard_map/ppermute | solution.py:505
  29.7 1.0 %collective-permute-start.9 = (f32[256,128]{1,0:T(8,128)S(1)}, f32[256,128]{1,0:T(8,128)S(1)}, u32[]{:S(2)}, u32[]{:S(2)}) collective-permute-start(f32[256,128]{1,0:T(8,128)S(1)} %get-tuple-element.115), channel_id=1, source_target_pairs={{0,24},{4,28},{8,0},{12,4},{16,8},{20,12},{24,16},{28,20},{32,56},... | collective-permute-start | bytes 393224 | tf_op jit(solution)/shard_map/ppermute | solution.py:505
  30.7 2.6 %intra2.1 = (bf16[512,1024]{1,0:T(8,128)(2,1)S(1)}, bf16[512,1024]{1,0:T(8,128)(2,1)S(1)}, f32[512,1024]{1,0:T(8,128)S(1)}, bf16[2048,256]{1,0:T(8,128)(2,1)S(1)}, bf16[4096,256]{1,0:T(8,128)(2,1)S(1)}) custom-call(s32[1]{0:T(128)} %bitcast.core, ...), custom_call_target="tpu_custom_call", output_to_operand_aliasing={{0}: (5, {}), {1}: (6, {}), {2}: (7, {}), {3}: (8, {}), {4}... | custom-call | flops 671088640 | bytes 4194304 | tf_op jit(solution)/shard_map/intra2/pallas_call | solution.py:79
  33.3 1.0 %collective-permute-done.8.c = f32[256,128]{1,0:T(8,128)S(1)} collective-permute-done((f32[256,128]{1,0:T(8,128)S(1)}, f32[256,128]{1,0:T(8,128)S(1)}, u32[]{:S(2)}, u32[]{:S(2)}) %collective-permute-start.8) | collective-permute-done | bytes 131104 | tf_op jit(solution)/shard_map/ppermute | solution.py:505
  34.3 0.1 collective-permute-done.9.d
  34.5 0.1 join0.1
  34.6 2.9 %collective-permute-start.10 = (f32[1024,128]{1,0:T(8,128)S(1)}, f32[1024,128]{1,0:T(8,128)S(1)}, u32[]{:S(2)}, u32[]{:S(2)}) collective-permute-start(f32[1024,128]{1,0:T(8,128)S(1)} %get-tuple-element.116), channel_id=1, source_target_pairs={{0,4},{4,0},{8,12},{12,8},{16,20},{20,16},{24,28},{28,24},{32,36},... | collective-permute-start | bytes 1572872 | tf_op jit(solution)/shard_map/ppermute | solution.py:521
  37.4 0.7 output0.1
  38.1 0.8 collective-permute-done.10.base
  39.0 0.9 %output1.1 = (f32[512,1024]{1,0:T(8,128)S(1)}, bf16[1024,128]{1,0:T(8,128)(2,1)S(1)}, f32[2,512]{1,0:T(2,128)S(1)}) custom-call(s32[1]{0:T(128)} %bitcast.core, bf16[512,1024]{1,0:T(8,128)(2,1)S(1)} %get-tuple-element.95.q.refs_7_.refs_0_, bf16[512,1024]{1,0:T(8,128)(2,1)S(1)} %get-tuple-element.96.o, f32[512,1024]{1,0:T(8,128)S(1)} %get-tuple-element.97.intra, ...), custom_call_target="tpu_custom_call" | custom-call | flops 134217728 | bytes 1048576 | tf_op jit(solution)/shard_map/output1/pallas_call | solution.py:79
  39.9 3.8 %collective-permute-start.13 = (f32[2,512]{1,0:T(2,128)S(1)}, f32[2,512]{1,0:T(2,128)S(1)}, u32[]{:S(2)}, u32[]{:S(2)}) collective-permute-start(f32[2,512]{1,0:T(2,128)S(1)} %get-tuple-element.123.s0), channel_id=1, source_target_pairs={{0,3},{1,0},{2,1},{3,2},{4,7},{5,4},{6,5},{7,6},{8,11},{9,8},{10,9... | collective-permute-start | bytes 12296 | tf_op jit(solution)/shard_map/ppermute | solution.py:526
  43.7 0.0 collective-permute-start.12
  43.7 0.7 collective-permute-start.11
  44.4 0.0 collective-permute-done.13.s3
  44.4 3.2 %collective-permute-done.12.s2 = f32[2,512]{1,0:T(2,128)S(1)} collective-permute-done((f32[2,512]{1,0:T(2,128)S(1)}, f32[2,512]{1,0:T(2,128)S(1)}, u32[]{:S(2)}, u32[]{:S(2)}) %collective-permute-start.12) | collective-permute-done | bytes 4128 | tf_op jit(solution)/shard_map/ppermute | solution.py:526
  47.6 1.0 %grad1.1 = (bf16[512,1024]{1,0:T(8,128)(2,1)S(1)}, f32[1024,128]{1,0:T(8,128)S(1)}) custom-call(s32[1]{0:T(128)} %bitcast.core, bf16[512,1024]{1,0:T(8,128)(2,1)S(1)} %get-tuple-element.95.q.refs_7_.refs_0_, f32[512,1024]{1,0:T(8,128)S(1)} %get-tuple-element.122.output, bf16[512,1024]{1,0:T(8,128)(2,1)S(1)} %get-tuple-element.96.o, f32[1,2048]{1,0:T(1,128)S(1)} %bitcast.6, ...), custom_call_target="tpu_custom_call" | custom-call | flops 134217728 | bytes 1048576 | tf_op jit(solution)/shard_map/grad1/pallas_call | solution.py:79
  48.6 1.9 %collective-permute-start.14 = (f32[1024,128]{1,0:T(8,128)S(1)}, f32[1024,128]{1,0:T(8,128)S(1)}, u32[]{:S(2)}, u32[]{:S(2)}) collective-permute-start(f32[1024,128]{1,0:T(8,128)S(1)} %get-tuple-element.137), channel_id=1, source_target_pairs={{0,4},{4,0},{8,12},{12,8},{16,20},{20,16},{24,28},{28,24},{32,36},... | collective-permute-start | bytes 1572872 | tf_op jit(solution)/shard_map/ppermute | solution.py:521
  50.5 1.0 %grad0.1 = (bf16[512,1024]{1,0:T(8,128)(2,1)S(1)}, f32[1024,128]{1,0:T(8,128)S(1)}) custom-call(s32[1]{0:T(128)} %bitcast.core, bf16[512,1024]{1,0:T(8,128)(2,1)S(1)} %get-tuple-element.117.q.refs_0_, f32[512,1024]{1,0:T(8,128)S(1)} %get-tuple-element.128.output, bf16[512,1024]{1,0:T(8,128)(2,1)S(1)} %get-tuple-element.118.o, f32[1,2048]{1,0:T(1,128)S(1)} %bitcast.7, ...), custom_call_target="tpu_custom_call" | custom-call | flops 134217728 | bytes 1048576 | tf_op jit(solution)/shard_map/grad0/pallas_call | solution.py:79
  51.5 0.5 collective-permute-done.14.near
  52.0 0.1 split.3
  52.1 1.5 %collective-permute-start.15 = (f32[256,128]{1,0:T(8,128)S(1)}, f32[256,128]{1,0:T(8,128)S(1)}, u32[]{:S(2)}, u32[]{:S(2)}) collective-permute-start(f32[256,128]{1,0:T(8,128)S(1)} %get-tuple-element.139), channel_id=1, source_target_pairs={{0,8},{4,12},{8,16},{12,20},{16,24},{20,28},{24,0},{28,4},{32,40},... | collective-permute-start | bytes 393224 | tf_op jit(solution)/shard_map/ppermute | solution.py:505
  53.7 2.1 %collective-permute-start.16 = (f32[256,128]{1,0:T(8,128)S(1)}, f32[256,128]{1,0:T(8,128)S(1)}, u32[]{:S(2)}, u32[]{:S(2)}) collective-permute-start(f32[256,128]{1,0:T(8,128)S(1)} %get-tuple-element.141), channel_id=1, source_target_pairs={{0,16},{4,20},{8,24},{12,28},{16,0},{20,4},{24,8},{28,12},{32,48},... | collective-permute-start | bytes 393224 | tf_op jit(solution)/shard_map/ppermute | solution.py:505
  55.8 0.7 collective-permute-start.17
  56.4 4.2 %middle0.1 = (bf16[512,2048]{1,0:T(8,128)(2,1)}, f32[512,256]{1,0:T(8,128)S(1)}, f32[512,256]{1,0:T(8,128)S(1)}, f32[512,256]{1,0:T(8,128)S(1)}, f32[512,256]{1,...) custom-call(s32[1]{0:T(128)} %bitcast.core, bf16[512,1024]{1,0:T(8,128)(2,1)S(1)} %get-tuple-element.117.q.refs_0_, ...), custom_call_target="tpu_custom_call" | custom-call | flops 1610612736 | bytes 3145728 | tf_op jit(solution)/shard_map/middle0/pallas_call | solution.py:79
  60.7 1.1 %collective-permute-done.16.c.refs_2_ = f32[256,128]{1,0:T(8,128)S(1)} collective-permute-done((f32[256,128]{1,0:T(8,128)S(1)}, f32[256,128]{1,0:T(8,128)S(1)}, u32[]{:S(2)}, u32[]{:S(2)}) %collective-permute-start.16) | collective-permute-done | bytes 131104 | tf_op jit(solution)/shard_map/ppermute | solution.py:505
  61.8 0.0 collective-permute-done.17.d.refs_3_
  61.9 0.3 collective-permute-start.20
  62.2 2.3 %collective-permute-start.19 = (f32[256,128]{1,0:T(8,128)S(1)}, f32[256,128]{1,0:T(8,128)S(1)}, u32[]{:S(2)}, u32[]{:S(2)}) collective-permute-start(f32[256,128]{1,0:T(8,128)S(1)} %line.3), channel_id=1, source_target_pairs={{0,64},{4,68},{8,72},{12,76},{16,80},{20,84},{24,88},{28,92},{32,9... | collective-permute-start | bytes 393224 | tf_op jit(solution)/shard_map/ppermute | solution.py:516
  64.5 0.3 collective-permute-start.18
  64.7 4.2 %middle1.1 = (bf16[512,2048]{1,0:T(8,128)(2,1)}, f32[512,256]{1,0:T(8,128)S(1)}, f32[512,256]{1,0:T(8,128)S(1)}, f32[512,256]{1,0:T(8,128)S(1)}, f32[512,256]{1,...) custom-call(s32[1]{0:T(128)} %bitcast.core, ...), custom_call_target="tpu_custom_call", output_to_operand_aliasing={{0}: (15, {})} | custom-call | flops 1610612736 | bytes 3145728 | tf_op jit(solution)/shard_map/middle1/pallas_call | solution.py:79
  69.0 1.1 %collective-permute-done.18.refs_4_ = f32[256,128]{1,0:T(8,128)S(1)} collective-permute-done((f32[256,128]{1,0:T(8,128)S(1)}, f32[256,128]{1,0:T(8,128)S(1)}, u32[]{:S(2)}, u32[]{:S(2)}) %collective-permute-start.18) | collective-permute-done | bytes 131104 | tf_op jit(solution)/shard_map/ppermute | solution.py:516
  70.1 0.0 collective-permute-done.19.refs_5_
  70.1 0.2 enter1.1
  70.3 2.4 %collective-permute-start.21 = (f32[256,128]{1,0:T(8,128)S(1)}, f32[256,128]{1,0:T(8,128)S(1)}, u32[]{:S(2)}, u32[]{:S(2)}) collective-permute-start(f32[256,128]{1,0:T(8,128)S(1)} %get-tuple-element.145), channel_id=1, source_target_pairs={{0,8},{4,12},{8,16},{12,20},{16,24},{20,28},{24,0},{28,4},{32,40},... | collective-permute-start | bytes 393224 | tf_op jit(solution)/shard_map/ppermute | solution.py:505
  72.7 1.7 %collective-permute-start.22 = (f32[256,128]{1,0:T(8,128)S(1)}, f32[256,128]{1,0:T(8,128)S(1)}, u32[]{:S(2)}, u32[]{:S(2)}) collective-permute-start(f32[256,128]{1,0:T(8,128)S(1)} %get-tuple-element.147), channel_id=1, source_target_pairs={{0,16},{4,20},{8,24},{12,28},{16,0},{20,4},{24,8},{28,12},{32,48},... | collective-permute-start | bytes 393224 | tf_op jit(solution)/shard_map/ppermute | solution.py:505
  74.4 0.8 collective-permute-start.23
  75.2 3.1 %middle2.1 = (bf16[512,2048]{1,0:T(8,128)(2,1)}, f32[512,256]{1,0:T(8,128)S(1)}, f32[512,256]{1,0:T(8,128)S(1)}, f32[512,256]{1,0:T(8,128)S(1)}, f32[512,256]{1,0:T(8,128)S(1)}) custom-call(s32[1]{0:T(128)} %bitcast.core, bf16[512,1024]{1,0:T(8,128)(2,1)S(1)} %get-tuple-element.95.q.refs_7_.refs_0_, ...), custom_call_target="tpu_custom_call", output_to_operand_aliasing={{0}: (8, {})} | custom-call | flops 1073741824 | bytes 2097152 | tf_op jit(solution)/shard_map/middle2/pallas_call | solution.py:79
  78.3 0.3 collective-permute-done.22.c
  78.6 0.5 collective-permute-done.23.d
  79.1 0.1 join1.1
  79.2 2.8 %collective-permute-start.24 = (f32[1024,128]{1,0:T(8,128)S(1)}, f32[1024,128]{1,0:T(8,128)S(1)}, u32[]{:S(2)}, u32[]{:S(2)}) collective-permute-start(f32[1024,128]{1,0:T(8,128)S(1)} %get-tuple-element.149), channel_id=1, source_target_pairs={{0,4},{4,0},{8,12},{12,8},{16,20},{20,16},{24,28},{28,24},{32,36},... | collective-permute-start | bytes 1572872 | tf_op jit(solution)/shard_map/ppermute | solution.py:521
  81.9 1.7 %last0.1 = (bf16[512,2048]{1,0:T(8,128)(2,1)}, bf16[512,2048]{1,0:T(8,128)(2,1)}) custom-call(s32[1]{0:T(128)} %bitcast.core, bf16[512,1024]{1,0:T(8,128)(2,1)S(1)} %get-tuple-element.104.k.refs_1_, bf16[512,1024]{1,0:T(8,128)(2,1)S(1)} %get-tuple-element.105.v.refs_2_, f32[1024,128]{1,0:T(8,128)S(1)} %get-tuple-element.158.base, ...), custom_call_target="tpu_custom_call" | custom-call | flops 268435456 | bytes 2097152 | tf_op jit(solution)/shard_map/last0/pallas_call | solution.py:79
  83.7 0.0 collective-permute-done.24.base
  83.7 1.7 %last1.1 = (bf16[512,2048]{1,0:T(8,128)(2,1)}, bf16[512,2048]{1,0:T(8,128)(2,1)}) custom-call(s32[1]{0:T(128)} %bitcast.core, bf16[512,1024]{1,0:T(8,128)(2,1)S(1)} %get-tuple-element.88.k.refs_8_.refs_1_, bf16[512,1024]{1,0:T(8,128)(2,1)S(1)} %get-tuple-element.89.v.refs_9_.refs_2_, ...), custom_call_target="tpu_custom_call", output_to_operand_aliasing={{0}: (12, {}), {1}: (13, {})} | custom-call | flops 268435456 | bytes 2097152 | tf_op jit(solution)/shard_map/last1/pallas_call | solution.py:79
  (10 shorter events, 0.1 us)
Async XLA Ops:
  2.6 3.4 %collective-permute-start = (f32[1024,128]{1,0:T(8,128)S(1)}, f32[1024,128]{1,0:T(8,128)S(1)}, u32[]{:S(2)}, u32[]{:S(2)}) collective-permute-start(f32[1024,128]{1,0:T(8,128)S(1)} %get-tuple-element.101), channel_id=1, source_target_pairs={{0,4},{4,0},{8,12},{12,8},{16,20},{20,16},{24,28},{28,24},{32,36},... | collective-permute-start | bytes 1572872 | tf_op jit(solution)/shard_map/ppermute | solution.py:521
  6.1 9.2 %collective-permute-start.1 = (f32[256,128]{1,0:T(8,128)S(1)}, f32[256,128]{1,0:T(8,128)S(1)}, u32[]{:S(2)}, u32[]{:S(2)}) collective-permute-start(f32[256,128]{1,0:T(8,128)S(1)} %get-tuple-element.103), channel_id=1, source_target_pairs={{0,8},{4,12},{8,16},{12,20},{16,24},{20,28},{24,0},{28,4},{32,40},... | collective-permute-start | bytes 393224 | tf_op jit(solution)/shard_map/ppermute | solution.py:505
  7.5 8.9 %collective-permute-start.2 = (f32[256,128]{1,0:T(8,128)S(1)}, f32[256,128]{1,0:T(8,128)S(1)}, u32[]{:S(2)}, u32[]{:S(2)}) collective-permute-start(f32[256,128]{1,0:T(8,128)S(1)} %get-tuple-element.108), channel_id=1, source_target_pairs={{0,16},{4,20},{8,24},{12,28},{16,0},{20,4},{24,8},{28,12},{32,48},... | collective-permute-start | bytes 393224 | tf_op jit(solution)/shard_map/ppermute | solution.py:505
  9.9 6.5 %collective-permute-start.3 = (f32[256,128]{1,0:T(8,128)S(1)}, f32[256,128]{1,0:T(8,128)S(1)}, u32[]{:S(2)}, u32[]{:S(2)}) collective-permute-start(f32[256,128]{1,0:T(8,128)S(1)} %get-tuple-element.109), channel_id=1, source_target_pairs={{0,24},{4,28},{8,0},{12,4},{16,8},{20,12},{24,16},{28,20},{32,56},... | collective-permute-start | bytes 393224 | tf_op jit(solution)/shard_map/ppermute | solution.py:505
  16.4 7.0 %collective-permute-start.4 = (f32[256,128]{1,0:T(8,128)S(1)}, f32[256,128]{1,0:T(8,128)S(1)}, u32[]{:S(2)}, u32[]{:S(2)}) collective-permute-start(f32[256,128]{1,0:T(8,128)S(1)} %line.2), channel_id=1, source_target_pairs={{0,32},{4,36},{8,40},{12,44},{16,48},{20,52},{24,56},{28,60},{32,6... | collective-permute-start | bytes 393224 | tf_op jit(solution)/shard_map/ppermute | solution.py:516
  17.8 5.7 %collective-permute-start.6 = (f32[256,128]{1,0:T(8,128)S(1)}, f32[256,128]{1,0:T(8,128)S(1)}, u32[]{:S(2)}, u32[]{:S(2)}) collective-permute-start(f32[256,128]{1,0:T(8,128)S(1)} %line.2), channel_id=1, source_target_pairs={{0,96},{4,100},{8,104},{12,108},{16,112},{20,116},{24,120},{28,124... | collective-permute-start | bytes 393224 | tf_op jit(solution)/shard_map/ppermute | solution.py:516
  19.3 7.0 %collective-permute-start.5 = (f32[256,128]{1,0:T(8,128)S(1)}, f32[256,128]{1,0:T(8,128)S(1)}, u32[]{:S(2)}, u32[]{:S(2)}) collective-permute-start(f32[256,128]{1,0:T(8,128)S(1)} %line.2), channel_id=1, source_target_pairs={{0,64},{4,68},{8,72},{12,76},{16,80},{20,84},{24,88},{28,92},{32,9... | collective-permute-start | bytes 393224 | tf_op jit(solution)/shard_map/ppermute | solution.py:516
  26.5 6.9 %collective-permute-start.7 = (f32[256,128]{1,0:T(8,128)S(1)}, f32[256,128]{1,0:T(8,128)S(1)}, u32[]{:S(2)}, u32[]{:S(2)}) collective-permute-start(f32[256,128]{1,0:T(8,128)S(1)} %get-tuple-element.112), channel_id=1, source_target_pairs={{0,8},{4,12},{8,16},{12,20},{16,24},{20,28},{24,0},{28,4},{32,40},... | collective-permute-start | bytes 393224 | tf_op jit(solution)/shard_map/ppermute | solution.py:505
  27.3 7.1 %collective-permute-start.8 = (f32[256,128]{1,0:T(8,128)S(1)}, f32[256,128]{1,0:T(8,128)S(1)}, u32[]{:S(2)}, u32[]{:S(2)}) collective-permute-start(f32[256,128]{1,0:T(8,128)S(1)} %get-tuple-element.114), channel_id=1, source_target_pairs={{0,16},{4,20},{8,24},{12,28},{16,0},{20,4},{24,8},{28,12},{32,48},... | collective-permute-start | bytes 393224 | tf_op jit(solution)/shard_map/ppermute | solution.py:505
  29.7 4.8 %collective-permute-start.9 = (f32[256,128]{1,0:T(8,128)S(1)}, f32[256,128]{1,0:T(8,128)S(1)}, u32[]{:S(2)}, u32[]{:S(2)}) collective-permute-start(f32[256,128]{1,0:T(8,128)S(1)} %get-tuple-element.115), channel_id=1, source_target_pairs={{0,24},{4,28},{8,0},{12,4},{16,8},{20,12},{24,16},{28,20},{32,56},... | collective-permute-start | bytes 393224 | tf_op jit(solution)/shard_map/ppermute | solution.py:505
  30.7 6.7 %copy-start = (f32[2048]{0:T(1024)S(1)}, f32[2048]{0:T(1024)}, u32[]{:S(2)}) copy-start(f32[2048]{0:T(1024)} %param.9) | copy-start | bytes 24580
  34.6 4.4 %collective-permute-start.10 = (f32[1024,128]{1,0:T(8,128)S(1)}, f32[1024,128]{1,0:T(8,128)S(1)}, u32[]{:S(2)}, u32[]{:S(2)}) collective-permute-start(f32[1024,128]{1,0:T(8,128)S(1)} %get-tuple-element.116), channel_id=1, source_target_pairs={{0,4},{4,0},{8,12},{12,8},{16,20},{20,16},{24,28},{28,24},{32,36},... | collective-permute-start | bytes 1572872 | tf_op jit(solution)/shard_map/ppermute | solution.py:521
  39.9 4.6 %collective-permute-start.13 = (f32[2,512]{1,0:T(2,128)S(1)}, f32[2,512]{1,0:T(2,128)S(1)}, u32[]{:S(2)}, u32[]{:S(2)}) collective-permute-start(f32[2,512]{1,0:T(2,128)S(1)} %get-tuple-element.123.s0), channel_id=1, source_target_pairs={{0,3},{1,0},{2,1},{3,2},{4,7},{5,4},{6,5},{7,6},{8,11},{9,8},{10,9... | collective-permute-start | bytes 12296 | tf_op jit(solution)/shard_map/ppermute | solution.py:526
  43.7 4.0 %collective-permute-start.12 = (f32[2,512]{1,0:T(2,128)S(1)}, f32[2,512]{1,0:T(2,128)S(1)}, u32[]{:S(2)}, u32[]{:S(2)}) collective-permute-start(f32[2,512]{1,0:T(2,128)S(1)} %get-tuple-element.123.s0), channel_id=1, source_target_pairs={{0,2},{1,3},{2,0},{3,1},{4,6},{5,7},{6,4},{7,5},{8,10},{9,11},{10,... | collective-permute-start | bytes 12296 | tf_op jit(solution)/shard_map/ppermute | solution.py:526
  43.7 4.0 %collective-permute-start.11 = (f32[2,512]{1,0:T(2,128)S(1)}, f32[2,512]{1,0:T(2,128)S(1)}, u32[]{:S(2)}, u32[]{:S(2)}) collective-permute-start(f32[2,512]{1,0:T(2,128)S(1)} %get-tuple-element.123.s0), channel_id=1, source_target_pairs={{0,1},{1,2},{2,3},{3,0},{4,5},{5,6},{6,7},{7,4},{8,9},{9,10},{10,1... | collective-permute-start | bytes 12296 | tf_op jit(solution)/shard_map/ppermute | solution.py:526
  48.6 3.4 %collective-permute-start.14 = (f32[1024,128]{1,0:T(8,128)S(1)}, f32[1024,128]{1,0:T(8,128)S(1)}, u32[]{:S(2)}, u32[]{:S(2)}) collective-permute-start(f32[1024,128]{1,0:T(8,128)S(1)} %get-tuple-element.137), channel_id=1, source_target_pairs={{0,4},{4,0},{8,12},{12,8},{16,20},{20,16},{24,28},{28,24},{32,36},... | collective-permute-start | bytes 1572872 | tf_op jit(solution)/shard_map/ppermute | solution.py:521
  52.1 8.6 %collective-permute-start.15 = (f32[256,128]{1,0:T(8,128)S(1)}, f32[256,128]{1,0:T(8,128)S(1)}, u32[]{:S(2)}, u32[]{:S(2)}) collective-permute-start(f32[256,128]{1,0:T(8,128)S(1)} %get-tuple-element.139), channel_id=1, source_target_pairs={{0,8},{4,12},{8,16},{12,20},{16,24},{20,28},{24,0},{28,4},{32,40},... | collective-permute-start | bytes 393224 | tf_op jit(solution)/shard_map/ppermute | solution.py:505
  53.7 8.2 %collective-permute-start.16 = (f32[256,128]{1,0:T(8,128)S(1)}, f32[256,128]{1,0:T(8,128)S(1)}, u32[]{:S(2)}, u32[]{:S(2)}) collective-permute-start(f32[256,128]{1,0:T(8,128)S(1)} %get-tuple-element.141), channel_id=1, source_target_pairs={{0,16},{4,20},{8,24},{12,28},{16,0},{20,4},{24,8},{28,12},{32,48},... | collective-permute-start | bytes 393224 | tf_op jit(solution)/shard_map/ppermute | solution.py:505
  55.8 6.1 %collective-permute-start.17 = (f32[256,128]{1,0:T(8,128)S(1)}, f32[256,128]{1,0:T(8,128)S(1)}, u32[]{:S(2)}, u32[]{:S(2)}) collective-permute-start(f32[256,128]{1,0:T(8,128)S(1)} %get-tuple-element.142), channel_id=1, source_target_pairs={{0,24},{4,28},{8,0},{12,4},{16,8},{20,12},{24,16},{28,20},{32,56},... | collective-permute-start | bytes 393224 | tf_op jit(solution)/shard_map/ppermute | solution.py:505
  61.9 8.3 %collective-permute-start.20 = (f32[256,128]{1,0:T(8,128)S(1)}, f32[256,128]{1,0:T(8,128)S(1)}, u32[]{:S(2)}, u32[]{:S(2)}) collective-permute-start(f32[256,128]{1,0:T(8,128)S(1)} %line.3), channel_id=1, source_target_pairs={{0,32},{4,36},{8,40},{12,44},{16,48},{20,52},{24,56},{28,60},{32,6... | collective-permute-start | bytes 393224 | tf_op jit(solution)/shard_map/ppermute | solution.py:516
  62.2 8.0 %collective-permute-start.19 = (f32[256,128]{1,0:T(8,128)S(1)}, f32[256,128]{1,0:T(8,128)S(1)}, u32[]{:S(2)}, u32[]{:S(2)}) collective-permute-start(f32[256,128]{1,0:T(8,128)S(1)} %line.3), channel_id=1, source_target_pairs={{0,64},{4,68},{8,72},{12,76},{16,80},{20,84},{24,88},{28,92},{32,9... | collective-permute-start | bytes 393224 | tf_op jit(solution)/shard_map/ppermute | solution.py:516
  64.5 5.6 %collective-permute-start.18 = (f32[256,128]{1,0:T(8,128)S(1)}, f32[256,128]{1,0:T(8,128)S(1)}, u32[]{:S(2)}, u32[]{:S(2)}) collective-permute-start(f32[256,128]{1,0:T(8,128)S(1)} %line.3), channel_id=1, source_target_pairs={{0,96},{4,100},{8,104},{12,108},{16,112},{20,116},{24,120},{28,124... | collective-permute-start | bytes 393224 | tf_op jit(solution)/shard_map/ppermute | solution.py:516
  70.3 8.0 %collective-permute-start.21 = (f32[256,128]{1,0:T(8,128)S(1)}, f32[256,128]{1,0:T(8,128)S(1)}, u32[]{:S(2)}, u32[]{:S(2)}) collective-permute-start(f32[256,128]{1,0:T(8,128)S(1)} %get-tuple-element.145), channel_id=1, source_target_pairs={{0,8},{4,12},{8,16},{12,20},{16,24},{20,28},{24,0},{28,4},{32,40},... | collective-permute-start | bytes 393224 | tf_op jit(solution)/shard_map/ppermute | solution.py:505
  72.7 5.9 %collective-permute-start.22 = (f32[256,128]{1,0:T(8,128)S(1)}, f32[256,128]{1,0:T(8,128)S(1)}, u32[]{:S(2)}, u32[]{:S(2)}) collective-permute-start(f32[256,128]{1,0:T(8,128)S(1)} %get-tuple-element.147), channel_id=1, source_target_pairs={{0,16},{4,20},{8,24},{12,28},{16,0},{20,4},{24,8},{28,12},{32,48},... | collective-permute-start | bytes 393224 | tf_op jit(solution)/shard_map/ppermute | solution.py:505
  74.4 4.7 %collective-permute-start.23 = (f32[256,128]{1,0:T(8,128)S(1)}, f32[256,128]{1,0:T(8,128)S(1)}, u32[]{:S(2)}, u32[]{:S(2)}) collective-permute-start(f32[256,128]{1,0:T(8,128)S(1)} %get-tuple-element.148), channel_id=1, source_target_pairs={{0,24},{4,28},{8,0},{12,4},{16,8},{20,12},{24,16},{28,20},{32,56},... | collective-permute-start | bytes 393224 | tf_op jit(solution)/shard_map/ppermute | solution.py:505
  79.2 4.5 %collective-permute-start.24 = (f32[1024,128]{1,0:T(8,128)S(1)}, f32[1024,128]{1,0:T(8,128)S(1)}, u32[]{:S(2)}, u32[]{:S(2)}) collective-permute-start(f32[1024,128]{1,0:T(8,128)S(1)} %get-tuple-element.149), channel_id=1, source_target_pairs={{0,4},{4,0},{8,12},{12,8},{16,20},{20,16},{24,28},{28,24},{32,36},... | collective-permute-start | bytes 1572872 | tf_op jit(solution)/shard_map/ppermute | solution.py:521

commit v6 on v5

--- a/solution.py
+++ b/solution.py
@@ -37,6 +37,8 @@
 SIDE_F32 = jax.ShapeDtypeStruct((BLOCK, SIDE), F32)
 SIDE_BF16 = jax.ShapeDtypeStruct((BLOCK, SIDE), BF16)
 STATE = jax.ShapeDtypeStruct((ROWS, DH), F32)
+HALF_STATE = jax.ShapeDtypeStruct((ROWS // 2, DH), F32)
+TURNED = jax.ShapeDtypeStruct((SIDE, BLOCK), BF16)
 STATE_HALF = jax.ShapeDtypeStruct((ROWS, DH), BF16)
 LANES = jax.ShapeDtypeStruct((BLOCK, DH), F32)
 STATS = jax.ShapeDtypeStruct((2, BLOCK), F32)
@@ -113,12 +115,6 @@
     return jnp.concatenate(
         [jnp.concatenate([first, zero], axis=1), jnp.concatenate([zero, second], axis=1)], axis=0
     )
-
-
-def store_states(out, pair, a, b):
-    both = dot_tn(a, b)
-    out[2 * pair * DH : (2 * pair + 1) * DH, :] = both[:DH, :DH]
-    out[(2 * pair + 1) * DH : (2 * pair + 2) * DH, :] = both[DH:, DH:]
 
 
 def seen_keys():
@@ -204,8 +200,9 @@
     )(core, keys, values)
 
 
-def intra_body(side, pairs, core, q_all, o_all, k, v, *refs):
-    q, o, out, first, last, sems = refs[-6:]
+def intra_body(side, pairs, core, q_all, o_all, gain, k, v, *refs):
+    q, turned, scaled, out, first, last, o, sems = refs[-8:]
+    gains = gain[:, pl.ds(side_start(core, side), SIDE)]
     before, behind = seen_keys(), seen_queries()
     copies = copies_of(
         [
@@ -227,49 +224,55 @@
             total = dot(scores0, values[TOP])
             out[TOP, cols] = total[TOP]
             out[BOTTOM, cols] = total[BOTTOM] + dot(scores1, values[BOTTOM])
+        turned[pair_columns(pair), :] = q[:, pair_columns(pair)].T
     wait(copies[len(pairs) :])
-
-
-def intra_output(number, side, pairs, core, queries, out_grad, k, v, begun=()):
+    for pair in pairs:
+        cols = pair_columns(pair)
+        scaled[:, cols] = o[:, cols].astype(F32) * gains[:, cols]
+
+
+def intra_output(number, side, pairs, core, queries, out_grad, gain, k, v, begun=()):
     return call(
         f"intra{number}",
         functools.partial(intra_body, side, pairs),
-        [SMEM, HBM, HBM, VMEM, VMEM] + [VMEM] * len(begun),
-        [VMEM] * 5,
-        [SIDE_BF16, SIDE_BF16, SIDE_F32, FIRST_SCORES, LAST_SCORES],
+        [SMEM, HBM, HBM, VMEM, VMEM, VMEM] + [VMEM] * len(begun),
+        [VMEM] * 6,
+        [SIDE_BF16, TURNED, SIDE_F32, SIDE_F32, FIRST_SCORES, LAST_SCORES],
         5 * BLOCK * BLOCK * SIDE * len(pairs) // 4,
         2 * MIB * len(pairs),
-        [pltpu.SemaphoreType.DMA((2 * len(pairs),))],
-        {5 + i: i for i in range(len(begun))},
-    )(core, queries, out_grad, k, v, *begun)
-
-
-def output_body(side, core, q, o, intra, gain, base, *refs):
-    if side == 0:
-        output, prefix_half, squares, products = refs
+        [BUFFER_BF16, pltpu.SemaphoreType.DMA((2 * len(pairs),))],
+        {6 + i: i for i in range(len(begun))},
+    )(core, queries, out_grad, gain, k, v, *begun)
+
+
+def output_body(number, q, scaled, intra, base, *refs):
+    pairs = (PAIRS, PAIRS[:2], PAIRS[2:])[number]
+    sums_in = refs[:2] if number > 0 else ()
+    if number < 2:
+        output, prefix_half, squares, products = refs[-4:]
     else:
-        squares_in, products_in, output, prefix_half, stats = refs
-    gains = gain[:, pl.ds(side_start(core, side), SIDE)]
-    prefix_half[...] = base[...].astype(BF16)
+        output, prefix_half, stats = refs[-3:]
+    first = head_columns(2 * pairs[0]).start
+    prefix_half[first : first + len(pairs) * 2 * DH, :] = base[...].astype(BF16)
     parts = (TOP, BOTTOM)
-    if side == 0:
+    if number == 0:
         square_sums = [jnp.zeros((HALF, DH), F32) for rows in parts]
         product_sums = [jnp.zeros((HALF, DH), F32) for rows in parts]
     else:
-        square_sums = [squares_in[rows, :] for rows in parts]
-        product_sums = [products_in[rows, :] for rows in parts]
-    for pair in PAIRS:
+        square_sums = [sums_in[0][rows, :] for rows in parts]
+        product_sums = [sums_in[1][rows, :] for rows in parts]
+    for pair in pairs:
         cols = pair_columns(pair)
         states = diagonal(prefix_half, pair)
         for part, rows in enumerate(parts):
             value = intra[rows, cols] + dot(q[rows, cols], states)
             output[rows, cols] = value
-            terms = o[rows, cols].astype(F32) * gains[:, cols] * value
+            terms = scaled[rows, cols] * value
             value = value * value
             square_sums[part] = square_sums[part] + (value[:, :DH] + value[:, DH:])
             product_sums[part] = product_sums[part] + (terms[:, :DH] + terms[:, DH:])
     for part, rows in enumerate(parts):
-        if side == 0:
+        if number < 2:
             squares[rows, :] = square_sums[part]
             products[rows, :] = product_sums[part]
         else:
@@ -277,45 +280,48 @@
             stats[1:2, rows] = jnp.sum(product_sums[part].T, axis=0, keepdims=True)
 
 
-def whole_output(side, core, q, o, intra, gain, base, sums=()):
+def whole_output(number, q, scaled, intra, base, sums=(), begun=()):
+    last = [STATS] if number == 2 else [LANES, LANES]
+    inputs = [q, scaled, intra, base, *sums, *begun]
     return call(
-        f"output{side}",
-        functools.partial(output_body, side),
-        [SMEM] + [VMEM] * (5 + len(sums)),
-        [VMEM] * (4 if side == 0 else 3),
-        [SIDE_F32, STATE_HALF] + ([LANES, LANES] if side == 0 else [STATS]),
+        f"output{number}",
+        functools.partial(output_body, number),
+        [VMEM] * len(inputs),
+        [VMEM] * (2 + len(last)),
+        [SIDE_F32, STATE_HALF] + last,
         2 * BLOCK * SIDE * DH,
         MIB,
-    )(core, q, o, intra, gain, base, *sums)
-
-
-def grad_body(side, core, q, output, o, gain, s0, s1, s2, s3, grad_out, states):
+        (),
+        {len(inputs) - len(begun) + i: i for i in range(len(begun))},
+    )(*inputs)
+
+
+def grad_body(turned, output, scaled, s0, s1, s2, s3, grad_out, states):
     total = (s0[...] + s1[...]) + (s2[...] + s3[...])
     mean_square = total[0:1, :] / WIDTH_ALL + epsilon
     radius = jnp.sqrt(mean_square)
     scale = total[1:2, :] / (WIDTH_ALL * radius * radius)
     inverse = jnp.broadcast_to(1.0 / radius, (DH, BLOCK)).T
     coeff = jnp.broadcast_to(scale, (DH, BLOCK)).T
-    gains = gain[:, pl.ds(side_start(core, side), SIDE)]
     for pair in PAIRS:
         for head in (2 * pair, 2 * pair + 1):
             cols = head_columns(head)
-            scaled = o[:, cols].astype(F32) * gains[:, cols]
-            grad_out[:, cols] = ((scaled - output[:, cols] * coeff) * inverse).astype(BF16)
-        cols = pair_columns(pair)
-        store_states(states, pair, q[:, cols], grad_out[:, cols])
-
-
-def local_grad(side, core, q, output, o, gain, stats):
+            grad_out[:, cols] = ((scaled[:, cols] - output[:, cols] * coeff) * inverse).astype(BF16)
+        both = dot(turned[pair_columns(pair), :], grad_out[:, pair_columns(pair)])
+        for h in range(2):
+            states[head_columns(2 * pair + h), :] = both[head_columns(h), head_columns(h)]
+
+
+def local_grad(side, turned, output, scaled, stats):
     return call(
         f"grad{side}",
-        functools.partial(grad_body, side),
-        [SMEM] + [VMEM] * 8,
+        grad_body,
+        [VMEM] * 7,
         [VMEM] * 2,
         [SIDE_BF16, STATE],
         2 * BLOCK * SIDE * DH,
         MIB,
-    )(core, q, output, o, gain, *stats)
+    )(turned, output, scaled, *stats)
 
 
 SIDE_ARRAYS = 7
@@ -463,7 +469,8 @@
     )(*chip, *pieces, *sums)
 
 
-def join_body(reverse, x, core, a, b, c, d, own, near, here, there):
+def join_body(reverse, x, core, a, b, c, d, own, near, here, *theirs):
+    whole = theirs[-1]
     first = core[0].astype(F32)
     second = 1.0 - first
     if reverse:
@@ -471,20 +478,24 @@
     for hop, piece in enumerate((a, b, c, d)):
         rows = quarter(lax.rem(x[0] + LINE - hop, LINE))
         here[rows, :] = piece[...] + first * near[rows, :]
-        there[rows, :] = piece[...] + second * own[rows, :]
+        whole[rows, :] = piece[...] + second * own[rows, :]
+    if not reverse:
+        theirs[0][...] = whole[: ROWS // 2, :]
+        theirs[1][...] = whole[ROWS // 2 :, :]
 
 
 def join(chip, core, pieces, own, near, reverse):
-    here, there = call(
+    here, *theirs = call(
         f"join{int(reverse)}",
         functools.partial(join_body, reverse),
         [SMEM] * 2 + [VMEM] * (LINE + 2),
-        [VMEM] * 2,
-        [STATE, STATE],
+        [VMEM] * (2 if reverse else 3),
+        [STATE, STATE] if reverse else [STATE, HALF_STATE, HALF_STATE],
         MIB,
         MIB,
+        [] if reverse else [pltpu.VMEM((ROWS, DH), F32)],
     )(chip[0], core, *pieces, own, near)
-    return here, swap(there)
+    return (here, *map(swap, theirs))
 
 
 def device_index(y, x, core):
@@ -544,22 +555,29 @@
     near0 = swap(state1)
     k0, v0, state0 = local_state(0, core, key_rows, value_rows)
     pieces = along_x(split(chip, state0, near0))
-    q0, o0, intra0, *turned0 = intra_output(0, 0, PAIRS, core, query_rows, out_grad, k0, v0)
+    q0, t0, scaled0, intra0, *turned0 = intra_output(
+        0, 0, PAIRS, core, query_rows, out_grad, gain, k0, v0
+    )
     pieces[1] = after(pieces[1], intra0)
     sums = along_y(line_sum(pieces), False)
-    begun = intra_output(1, 1, PAIRS[:2], core, query_rows, out_grad, k1, v1)
-    sums[0] = after(sums[0], begun[2])
+    begun = intra_output(1, 1, PAIRS[:2], core, query_rows, out_grad, gain, k1, v1)
+    sums[0] = after(sums[0], begun[3])
     pieces = along_x(entering(chip, pieces, sums, False))
-    q1, o1, intra1, *turned1 = intra_output(2, 1, PAIRS[2:], core, query_rows, out_grad, k1, v1, begun)
+    q1, t1, scaled1, intra1, *turned1 = intra_output(
+        2, 1, PAIRS[2:], core, query_rows, out_grad, gain, k1, v1, begun
+    )
     pieces[1] = after(pieces[1], intra1)
-    base0, base1 = join(chip, core, pieces, state0, near0, False)
-    output0, prefix0, *lanes = whole_output(0, core, q0, o0, intra0, gain, base0)
-    output1, prefix1, stats = whole_output(1, core, q1, o1, intra1, gain, base1, lanes)
+    base0, base1, base2 = join(chip, core, pieces, state0, near0, False)
+    output0, prefix0, *lanes = whole_output(0, q0, scaled0, intra0, base0)
+    *begun, squares, products = whole_output(1, q1, scaled1, intra1, base1, lanes)
+    output1, prefix1, stats = whole_output(
+        2, q1, scaled1, intra1, base2, (squares, products), begun
+    )
     stats = [stats] + along_heads(stats)
 
-    g1, state1 = local_grad(1, core, q1, output1, o1, gain, stats)
+    g1, state1 = local_grad(1, t1, output1, scaled1, stats)
     near0 = swap(state1)
-    g0, state0 = local_grad(0, core, q0, output0, o0, gain, stats)
+    g0, state0 = local_grad(0, t0, output0, scaled0, stats)
     arrays = ((q0, k0, v0, g0, prefix0, *turned0), (q1, k1, v1, g1, prefix1, *turned1))
     pieces = along_x(split(chip, state0, near0))
     query_grad, parts = middle_gradients(0, ((0, 0), (0, 1), (0, 2)), core, arrays)

time: 85.8 us -> 85.3 us (level)
    pallas_call x22 -> x23, Pallas kernels: 32.5 us -> 32.7 us  [run(): kernel(*(pltpu.with_memory_space_constraint(array, pltpu.HBM) if spec is...]
    ppermute x4 -> x5, starting transfers between devices: 8.99 us -> 8.99 us  [swap(): return lax.ppermute(part, 'ctx', PARTNERS)]
  transfers between devices with their start and end apart: 25 -> 26, of which waited for: 11 -> 12; matrix products, arithmetic and copies ran while one was open for 0% -> 0% of each run, Pallas kernels for 31% -> 32%
where the time goes in v6:
time: 85.3 us; the launch traced here: 85 us
  starting transfers between devices  39.3 us (46%)
  Pallas kernels  32.7 us (38%)
  waiting for transfers between devices  12 us (14%)
  between operations  1.08 us (1%)
    pallas_call x23, Pallas kernels, run(): kernel(*(pltpu.with_memory_space_constraint(array, pltpu.HBM) if spec is...  32.7 us
    ppermute x12, starting transfers between devices, along_x(): got[hop] = lax.ppermute(pieces[hop], 'ctx', pairs)  18.5 us
    ppermute x5, starting transfers between devices, swap(): return lax.ppermute(part, 'ctx', PARTNERS)  8.99 us
    ppermute x6, starting transfers between devices, along_y(): got[hop] = lax.ppermute(part, 'ctx', pairs)  7.29 us
    ppermute x3, starting transfers between devices, along_heads(): lax.ppermute(stats, 'head', [(i, (i + hop) % 4) for i in range(4)])  4.51 us
    ppermute x12, waiting for transfers between devices, along_x(): got[hop] = lax.ppermute(pieces[hop], 'ctx', pairs)  3.91 us
    ppermute x6, waiting for transfers between devices, along_y(): got[hop] = lax.ppermute(part, 'ctx', pairs)  3.88 us
    ppermute x3, waiting for transfers between devices, along_heads(): lax.ppermute(stats, 'head', [(i, (i + hop) % 4) for i in range(4)])  3.28 us
  transfers between devices with their start and end apart: 26, of which 12 were waited for; matrix products, arithmetic and copies ran while one was open for 0% of the time, Pallas kernels for 32%

profile of v6, /device:TPU:1, one launch (start us, length us, event | category | flops | bytes accessed | tf_op | source)
XLA Modules:
  0.0 85.0 jit_solution(14152740661667898671)
XLA Ops:
  0.7 1.9 %state1.1 = (bf16[512,1024]{1,0:T(8,128)(2,1)S(1)}, bf16[512,1024]{1,0:T(8,128)(2,1)S(1)}, f32[1024,128]{1,0:T(8,128)S(1)}) custom-call(s32[1]{0:T(128)} %bitcast.core, bf16[512,2048]{1,0:T(8,128)(2,1)} %k_all.3, bf16[512,2048]{1,0:T(8,128)(2,1)} %v_all.3), custom_call_target="tpu_custom_call" | custom-call | flops 134217728 | bytes 2097152 | tf_op jit(solution)/shard_map/state1/pallas_call | solution.py:81
  2.6 0.0 copy-start
  2.6 1.5 %collective-permute-start = (f32[1024,128]{1,0:T(8,128)S(1)}, f32[1024,128]{1,0:T(8,128)S(1)}, u32[]{:S(2)}, u32[]{:S(2)}) collective-permute-start(f32[1024,128]{1,0:T(8,128)S(1)} %get-tuple-element.111), channel_id=1, source_target_pairs={{0,4},{4,0},{8,12},{12,8},{16,20},{20,16},{24,28},{28,24},{32,36},... | collective-permute-start | bytes 1572872 | tf_op jit(solution)/shard_map/ppermute | solution.py:532
  4.1 1.9 %state0.1 = (bf16[512,1024]{1,0:T(8,128)(2,1)S(1)}, bf16[512,1024]{1,0:T(8,128)(2,1)S(1)}, f32[1024,128]{1,0:T(8,128)S(1)}) custom-call(s32[1]{0:T(128)} %bitcast.core, bf16[512,2048]{1,0:T(8,128)(2,1)} %k_all.3, bf16[512,2048]{1,0:T(8,128)(2,1)} %v_all.3), custom_call_target="tpu_custom_call" | custom-call | flops 134217728 | bytes 2097152 | tf_op jit(solution)/shard_map/state0/pallas_call | solution.py:81
  6.0 0.0 collective-permute-done.near
  6.1 0.1 split.2
  6.1 1.4 %collective-permute-start.1 = (f32[256,128]{1,0:T(8,128)S(1)}, f32[256,128]{1,0:T(8,128)S(1)}, u32[]{:S(2)}, u32[]{:S(2)}) collective-permute-start(f32[256,128]{1,0:T(8,128)S(1)} %get-tuple-element.113), channel_id=1, source_target_pairs={{0,8},{4,12},{8,16},{12,20},{16,24},{20,28},{24,0},{28,4},{32,40},... | collective-permute-start | bytes 393224 | tf_op jit(solution)/shard_map/ppermute | solution.py:516
  7.5 2.5 %collective-permute-start.2 = (f32[256,128]{1,0:T(8,128)S(1)}, f32[256,128]{1,0:T(8,128)S(1)}, u32[]{:S(2)}, u32[]{:S(2)}) collective-permute-start(f32[256,128]{1,0:T(8,128)S(1)} %get-tuple-element.118), channel_id=1, source_target_pairs={{0,16},{4,20},{8,24},{12,28},{16,0},{20,4},{24,8},{28,12},{32,48},... | collective-permute-start | bytes 393224 | tf_op jit(solution)/shard_map/ppermute | solution.py:516
  10.0 1.1 %collective-permute-start.3 = (f32[256,128]{1,0:T(8,128)S(1)}, f32[256,128]{1,0:T(8,128)S(1)}, u32[]{:S(2)}, u32[]{:S(2)}) collective-permute-start(f32[256,128]{1,0:T(8,128)S(1)} %get-tuple-element.119), channel_id=1, source_target_pairs={{0,24},{4,28},{8,0},{12,4},{16,8},{20,12},{24,16},{28,20},{32,56},... | collective-permute-start | bytes 393224 | tf_op jit(solution)/shard_map/ppermute | solution.py:516
  11.1 4.4 %intra0.1 = (bf16[512,1024]{1,0:T(8,128)(2,1)S(1)}, bf16[1024,512]{1,0:T(8,128)(2,1)S(1)}, f32[512,1024]{1,0:T(8,128)S(1)}, f32[512,1024]{1,0:T(8,128)S(1)}, bf1...) custom-call(s32[1]{0:T(128)} %bitcast.core, bf16[512,2048]{1,0:T(8,128)(2,1)} %q_all.5, ...), custom_call_target="tpu_custom_call" | custom-call | flops 1342177280 | bytes 8388608 | tf_op jit(solution)/shard_map/intra0/pallas_call | solution.py:81
  15.5 0.0 collective-permute-done.1.b.refs_1_
  15.5 0.9 %collective-permute-done.2.c.refs_2_ = f32[256,128]{1,0:T(8,128)S(1)} collective-permute-done((f32[256,128]{1,0:T(8,128)S(1)}, f32[256,128]{1,0:T(8,128)S(1)}, u32[]{:S(2)}, u32[]{:S(2)}) %collective-permute-start.2) | collective-permute-done | bytes 131104 | tf_op jit(solution)/shard_map/ppermute | solution.py:516
  16.5 1.4 %collective-permute-start.4 = (f32[256,128]{1,0:T(8,128)S(1)}, f32[256,128]{1,0:T(8,128)S(1)}, u32[]{:S(2)}, u32[]{:S(2)}) collective-permute-start(f32[256,128]{1,0:T(8,128)S(1)} %line.2), channel_id=1, source_target_pairs={{0,32},{4,36},{8,40},{12,44},{16,48},{20,52},{24,56},{28,60},{32,6... | collective-permute-start | bytes 393224 | tf_op jit(solution)/shard_map/ppermute | solution.py:527
  17.8 1.5 %collective-permute-start.6 = (f32[256,128]{1,0:T(8,128)S(1)}, f32[256,128]{1,0:T(8,128)S(1)}, u32[]{:S(2)}, u32[]{:S(2)}) collective-permute-start(f32[256,128]{1,0:T(8,128)S(1)} %line.2), channel_id=1, source_target_pairs={{0,96},{4,100},{8,104},{12,108},{16,112},{20,116},{24,120},{28,124... | collective-permute-start | bytes 393224 | tf_op jit(solution)/shard_map/ppermute | solution.py:527
  19.3 1.6 %collective-permute-start.5 = (f32[256,128]{1,0:T(8,128)S(1)}, f32[256,128]{1,0:T(8,128)S(1)}, u32[]{:S(2)}, u32[]{:S(2)}) collective-permute-start(f32[256,128]{1,0:T(8,128)S(1)} %line.2), channel_id=1, source_target_pairs={{0,64},{4,68},{8,72},{12,76},{16,80},{20,84},{24,88},{28,92},{32,9... | collective-permute-start | bytes 393224 | tf_op jit(solution)/shard_map/ppermute | solution.py:527
  20.9 2.7 %intra1.1 = (bf16[512,1024]{1,0:T(8,128)(2,1)S(1)}, bf16[1024,512]{1,0:T(8,128)(2,1)S(1)}, f32[512,1024]{1,0:T(8,128)S(1)}, f32[512,1024]{1,0:T(8,128)S(1)}, bf1...) custom-call(s32[1]{0:T(128)} %bitcast.core, bf16[512,2048]{1,0:T(8,128)(2,1)} %q_all.5, ...), custom_call_target="tpu_custom_call" | custom-call | flops 671088640 | bytes 4194304 | tf_op jit(solution)/shard_map/intra1/pallas_call | solution.py:81
  23.6 0.0 collective-permute-done.4.refs_4_
  23.6 2.7 %collective-permute-done.5.refs_5_ = f32[256,128]{1,0:T(8,128)S(1)} collective-permute-done((f32[256,128]{1,0:T(8,128)S(1)}, f32[256,128]{1,0:T(8,128)S(1)}, u32[]{:S(2)}, u32[]{:S(2)}) %collective-permute-start.5) | collective-permute-done | bytes 131104 | tf_op jit(solution)/shard_map/ppermute | solution.py:527
  26.3 0.2 enter0.1
  26.5 0.8 collective-permute-start.7
  27.3 2.4 %collective-permute-start.8 = (f32[256,128]{1,0:T(8,128)S(1)}, f32[256,128]{1,0:T(8,128)S(1)}, u32[]{:S(2)}, u32[]{:S(2)}) collective-permute-start(f32[256,128]{1,0:T(8,128)S(1)} %get-tuple-element.124), channel_id=1, source_target_pairs={{0,16},{4,20},{8,24},{12,28},{16,0},{20,4},{24,8},{28,12},{32,48},... | collective-permute-start | bytes 393224 | tf_op jit(solution)/shard_map/ppermute | solution.py:516
  29.7 1.0 %collective-permute-start.9 = (f32[256,128]{1,0:T(8,128)S(1)}, f32[256,128]{1,0:T(8,128)S(1)}, u32[]{:S(2)}, u32[]{:S(2)}) collective-permute-start(f32[256,128]{1,0:T(8,128)S(1)} %get-tuple-element.125), channel_id=1, source_target_pairs={{0,24},{4,28},{8,0},{12,4},{16,8},{20,12},{24,16},{28,20},{32,56},... | collective-permute-start | bytes 393224 | tf_op jit(solution)/shard_map/ppermute | solution.py:516
  30.8 2.7 %intra2.1 = (bf16[512,1024]{1,0:T(8,128)(2,1)S(1)}, bf16[1024,512]{1,0:T(8,128)(2,1)S(1)}, f32[512,1024]{1,0:T(8,128)S(1)}, f32[512,1024]{1,0:T(8,128)S(1)}, bf1...) custom-call(s32[1]{0:T(128)} %bitcast.core, ...), custom_call_target="tpu_custom_call", output_to_operand_aliasing={{0}: (6, {}), {1}: (7, {}), {2}: (8, {}), {3}: (9, {}), {4}... | custom-call | flops 671088640 | bytes 4194304 | tf_op jit(solution)/shard_map/intra2/pallas_call | solution.py:81
  33.4 0.9 %collective-permute-done.8.c = f32[256,128]{1,0:T(8,128)S(1)} collective-permute-done((f32[256,128]{1,0:T(8,128)S(1)}, f32[256,128]{1,0:T(8,128)S(1)}, u32[]{:S(2)}, u32[]{:S(2)}) %collective-permute-start.8) | collective-permute-done | bytes 131104 | tf_op jit(solution)/shard_map/ppermute | solution.py:516
  34.4 0.1 collective-permute-done.9.d
  34.5 0.1 join0.1
  34.6 2.7 %collective-permute-start.11 = (f32[512,128]{1,0:T(8,128)S(1)}, f32[512,128]{1,0:T(8,128)S(1)}, u32[]{:S(2)}, u32[]{:S(2)}) collective-permute-start(f32[512,128]{1,0:T(8,128)S(1)} %get-tuple-element.127), channel_id=1, source_target_pairs={{0,4},{4,0},{8,12},{12,8},{16,20},{20,16},{24,28},{28,24},{32,36},... | collective-permute-start | bytes 786440 | tf_op jit(solution)/shard_map/ppermute | solution.py:532
  37.3 0.3 collective-permute-start.10
  37.6 0.7 output0.1
  38.3 0.2 collective-permute-done.11.base
  38.5 0.4 output1.1
  38.9 0.6 output2.1
  39.5 3.8 %collective-permute-start.14 = (f32[2,512]{1,0:T(2,128)S(1)}, f32[2,512]{1,0:T(2,128)S(1)}, u32[]{:S(2)}, u32[]{:S(2)}) collective-permute-start(f32[2,512]{1,0:T(2,128)S(1)} %get-tuple-element.138.s0), channel_id=1, source_target_pairs={{0,3},{1,0},{2,1},{3,2},{4,7},{5,4},{6,5},{7,6},{8,11},{9,8},{10,9... | collective-permute-start | bytes 12296 | tf_op jit(solution)/shard_map/ppermute | solution.py:537
  43.3 0.0 collective-permute-start.13
  43.3 0.7 collective-permute-start.12
  44.0 0.1 collective-permute-done.14.s3
  44.0 3.2 %collective-permute-done.13.s2 = f32[2,512]{1,0:T(2,128)S(1)} collective-permute-done((f32[2,512]{1,0:T(2,128)S(1)}, f32[2,512]{1,0:T(2,128)S(1)}, u32[]{:S(2)}, u32[]{:S(2)}) %collective-permute-start.13) | collective-permute-done | bytes 4128 | tf_op jit(solution)/shard_map/ppermute | solution.py:537
  47.2 0.8 grad1.1
  48.1 1.9 %collective-permute-start.15 = (f32[1024,128]{1,0:T(8,128)S(1)}, f32[1024,128]{1,0:T(8,128)S(1)}, u32[]{:S(2)}, u32[]{:S(2)}) collective-permute-start(f32[1024,128]{1,0:T(8,128)S(1)} %get-tuple-element.153), channel_id=1, source_target_pairs={{0,4},{4,0},{8,12},{12,8},{16,20},{20,16},{24,28},{28,24},{32,36},... | collective-permute-start | bytes 1572872 | tf_op jit(solution)/shard_map/ppermute | solution.py:532
  50.0 0.8 grad0.1
  50.8 0.7 collective-permute-done.15.near
  51.5 0.1 split.3
  51.6 1.5 %collective-permute-start.16 = (f32[256,128]{1,0:T(8,128)S(1)}, f32[256,128]{1,0:T(8,128)S(1)}, u32[]{:S(2)}, u32[]{:S(2)}) collective-permute-start(f32[256,128]{1,0:T(8,128)S(1)} %get-tuple-element.155), channel_id=1, source_target_pairs={{0,8},{4,12},{8,16},{12,20},{16,24},{20,28},{24,0},{28,4},{32,40},... | collective-permute-start | bytes 393224 | tf_op jit(solution)/shard_map/ppermute | solution.py:516
  53.1 2.1 %collective-permute-start.17 = (f32[256,128]{1,0:T(8,128)S(1)}, f32[256,128]{1,0:T(8,128)S(1)}, u32[]{:S(2)}, u32[]{:S(2)}) collective-permute-start(f32[256,128]{1,0:T(8,128)S(1)} %get-tuple-element.157), channel_id=1, source_target_pairs={{0,16},{4,20},{8,24},{12,28},{16,0},{20,4},{24,8},{28,12},{32,48},... | collective-permute-start | bytes 393224 | tf_op jit(solution)/shard_map/ppermute | solution.py:516
  55.2 0.6 collective-permute-start.18
  55.8 4.2 %middle0.1 = (bf16[512,2048]{1,0:T(8,128)(2,1)}, f32[512,256]{1,0:T(8,128)S(1)}, f32[512,256]{1,0:T(8,128)S(1)}, f32[512,256]{1,0:T(8,128)S(1)}, f32[512,256]{1,...) custom-call(s32[1]{0:T(128)} %bitcast.core, bf16[512,1024]{1,0:T(8,128)(2,1)S(1)} %get-tuple-element.128.q.refs_0_, ...), custom_call_target="tpu_custom_call" | custom-call | flops 1610612736 | bytes 3145728 | tf_op jit(solution)/shard_map/middle0/pallas_call | solution.py:81
  60.1 1.2 %collective-permute-done.17.c.refs_2_ = f32[256,128]{1,0:T(8,128)S(1)} collective-permute-done((f32[256,128]{1,0:T(8,128)S(1)}, f32[256,128]{1,0:T(8,128)S(1)}, u32[]{:S(2)}, u32[]{:S(2)}) %collective-permute-start.17) | collective-permute-done | bytes 131104 | tf_op jit(solution)/shard_map/ppermute | solution.py:516
  61.3 0.3 collective-permute-start.21
  61.6 2.3 %collective-permute-start.20 = (f32[256,128]{1,0:T(8,128)S(1)}, f32[256,128]{1,0:T(8,128)S(1)}, u32[]{:S(2)}, u32[]{:S(2)}) collective-permute-start(f32[256,128]{1,0:T(8,128)S(1)} %line.3), channel_id=1, source_target_pairs={{0,64},{4,68},{8,72},{12,76},{16,80},{20,84},{24,88},{28,92},{32,9... | collective-permute-start | bytes 393224 | tf_op jit(solution)/shard_map/ppermute | solution.py:527
  63.9 0.2 collective-permute-start.19
  64.1 4.2 %middle1.1 = (bf16[512,2048]{1,0:T(8,128)(2,1)}, f32[512,256]{1,0:T(8,128)S(1)}, f32[512,256]{1,0:T(8,128)S(1)}, f32[512,256]{1,0:T(8,128)S(1)}, f32[512,256]{1,...) custom-call(s32[1]{0:T(128)} %bitcast.core, ...), custom_call_target="tpu_custom_call", output_to_operand_aliasing={{0}: (15, {})} | custom-call | flops 1610612736 | bytes 3145728 | tf_op jit(solution)/shard_map/middle1/pallas_call | solution.py:81
  68.4 1.2 %collective-permute-done.19.refs_4_ = f32[256,128]{1,0:T(8,128)S(1)} collective-permute-done((f32[256,128]{1,0:T(8,128)S(1)}, f32[256,128]{1,0:T(8,128)S(1)}, u32[]{:S(2)}, u32[]{:S(2)}) %collective-permute-start.19) | collective-permute-done | bytes 131104 | tf_op jit(solution)/shard_map/ppermute | solution.py:527
  69.6 0.2 enter1.1
  69.8 2.5 %collective-permute-start.22 = (f32[256,128]{1,0:T(8,128)S(1)}, f32[256,128]{1,0:T(8,128)S(1)}, u32[]{:S(2)}, u32[]{:S(2)}) collective-permute-start(f32[256,128]{1,0:T(8,128)S(1)} %get-tuple-element.161), channel_id=1, source_target_pairs={{0,8},{4,12},{8,16},{12,20},{16,24},{20,28},{24,0},{28,4},{32,40},... | collective-permute-start | bytes 393224 | tf_op jit(solution)/shard_map/ppermute | solution.py:516
  72.3 1.6 %collective-permute-start.23 = (f32[256,128]{1,0:T(8,128)S(1)}, f32[256,128]{1,0:T(8,128)S(1)}, u32[]{:S(2)}, u32[]{:S(2)}) collective-permute-start(f32[256,128]{1,0:T(8,128)S(1)} %get-tuple-element.163), channel_id=1, source_target_pairs={{0,16},{4,20},{8,24},{12,28},{16,0},{20,4},{24,8},{28,12},{32,48},... | collective-permute-start | bytes 393224 | tf_op jit(solution)/shard_map/ppermute | solution.py:516
  73.9 0.8 collective-permute-start.24
  74.8 3.1 %middle2.1 = (bf16[512,2048]{1,0:T(8,128)(2,1)}, f32[512,256]{1,0:T(8,128)S(1)}, f32[512,256]{1,0:T(8,128)S(1)}, f32[512,256]{1,0:T(8,128)S(1)}, f32[512,256]{1,0:T(8,128)S(1)}) custom-call(s32[1]{0:T(128)} %bitcast.core, bf16[512,1024]{1,0:T(8,128)(2,1)S(1)} %get-tuple-element.104.q.refs_7_.refs_0_, ...), custom_call_target="tpu_custom_call", output_to_operand_aliasing={{0}: (8, {})} | custom-call | flops 1073741824 | bytes 2097152 | tf_op jit(solution)/shard_map/middle2/pallas_call | solution.py:81
  77.9 0.0 collective-permute-done.22.b
  77.9 0.3 collective-permute-done.23.c
  78.2 0.5 collective-permute-done.24.d
  78.6 0.1 join1.1
  78.7 2.7 %collective-permute-start.25 = (f32[1024,128]{1,0:T(8,128)S(1)}, f32[1024,128]{1,0:T(8,128)S(1)}, u32[]{:S(2)}, u32[]{:S(2)}) collective-permute-start(f32[1024,128]{1,0:T(8,128)S(1)} %get-tuple-element.165), channel_id=1, source_target_pairs={{0,4},{4,0},{8,12},{12,8},{16,20},{20,16},{24,28},{28,24},{32,36},... | collective-permute-start | bytes 1572872 | tf_op jit(solution)/shard_map/ppermute | solution.py:532
  81.4 1.7 %last0.1 = (bf16[512,2048]{1,0:T(8,128)(2,1)}, bf16[512,2048]{1,0:T(8,128)(2,1)}) custom-call(s32[1]{0:T(128)} %bitcast.core, bf16[512,1024]{1,0:T(8,128)(2,1)S(1)} %get-tuple-element.114.k.refs_1_, bf16[512,1024]{1,0:T(8,128)(2,1)S(1)} %get-tuple-element.115.v.refs_2_, f32[1024,128]{1,0:T(8,128)S(1)} %get-tuple-element.174.base, ...), custom_call_target="tpu_custom_call" | custom-call | flops 268435456 | bytes 2097152 | tf_op jit(solution)/shard_map/last0/pallas_call | solution.py:81
  83.1 1.7 %last1.1 = (bf16[512,2048]{1,0:T(8,128)(2,1)}, bf16[512,2048]{1,0:T(8,128)(2,1)}) custom-call(s32[1]{0:T(128)} %bitcast.core, bf16[512,1024]{1,0:T(8,128)(2,1)S(1)} %get-tuple-element.96.k.refs_8_.refs_1_, bf16[512,1024]{1,0:T(8,128)(2,1)S(1)} %get-tuple-element.97.v.refs_9_.refs_2_, ...), custom_call_target="tpu_custom_call", output_to_operand_aliasing={{0}: (12, {}), {1}: (13, {})} | custom-call | flops 268435456 | bytes 2097152 | tf_op jit(solution)/shard_map/last1/pallas_call | solution.py:81
  (13 shorter events, 0.1 us)
Async XLA Ops:
  2.6 8.5 %copy-start = (f32[2048]{0:T(1024)S(1)}, f32[2048]{0:T(1024)}, u32[]{:S(2)}) copy-start(f32[2048]{0:T(1024)} %param.9) | copy-start | bytes 24580
  2.6 3.4 %collective-permute-start = (f32[1024,128]{1,0:T(8,128)S(1)}, f32[1024,128]{1,0:T(8,128)S(1)}, u32[]{:S(2)}, u32[]{:S(2)}) collective-permute-start(f32[1024,128]{1,0:T(8,128)S(1)} %get-tuple-element.111), channel_id=1, source_target_pairs={{0,4},{4,0},{8,12},{12,8},{16,20},{20,16},{24,28},{28,24},{32,36},... | collective-permute-start | bytes 1572872 | tf_op jit(solution)/shard_map/ppermute | solution.py:532
  6.1 9.4 %collective-permute-start.1 = (f32[256,128]{1,0:T(8,128)S(1)}, f32[256,128]{1,0:T(8,128)S(1)}, u32[]{:S(2)}, u32[]{:S(2)}) collective-permute-start(f32[256,128]{1,0:T(8,128)S(1)} %get-tuple-element.113), channel_id=1, source_target_pairs={{0,8},{4,12},{8,16},{12,20},{16,24},{20,28},{24,0},{28,4},{32,40},... | collective-permute-start | bytes 393224 | tf_op jit(solution)/shard_map/ppermute | solution.py:516
  7.5 8.9 %collective-permute-start.2 = (f32[256,128]{1,0:T(8,128)S(1)}, f32[256,128]{1,0:T(8,128)S(1)}, u32[]{:S(2)}, u32[]{:S(2)}) collective-permute-start(f32[256,128]{1,0:T(8,128)S(1)} %get-tuple-element.118), channel_id=1, source_target_pairs={{0,16},{4,20},{8,24},{12,28},{16,0},{20,4},{24,8},{28,12},{32,48},... | collective-permute-start | bytes 393224 | tf_op jit(solution)/shard_map/ppermute | solution.py:516
  10.0 6.5 %collective-permute-start.3 = (f32[256,128]{1,0:T(8,128)S(1)}, f32[256,128]{1,0:T(8,128)S(1)}, u32[]{:S(2)}, u32[]{:S(2)}) collective-permute-start(f32[256,128]{1,0:T(8,128)S(1)} %get-tuple-element.119), channel_id=1, source_target_pairs={{0,24},{4,28},{8,0},{12,4},{16,8},{20,12},{24,16},{28,20},{32,56},... | collective-permute-start | bytes 393224 | tf_op jit(solution)/shard_map/ppermute | solution.py:516
  16.5 7.1 %collective-permute-start.4 = (f32[256,128]{1,0:T(8,128)S(1)}, f32[256,128]{1,0:T(8,128)S(1)}, u32[]{:S(2)}, u32[]{:S(2)}) collective-permute-start(f32[256,128]{1,0:T(8,128)S(1)} %line.2), channel_id=1, source_target_pairs={{0,32},{4,36},{8,40},{12,44},{16,48},{20,52},{24,56},{28,60},{32,6... | collective-permute-start | bytes 393224 | tf_op jit(solution)/shard_map/ppermute | solution.py:527
  17.8 5.8 %collective-permute-start.6 = (f32[256,128]{1,0:T(8,128)S(1)}, f32[256,128]{1,0:T(8,128)S(1)}, u32[]{:S(2)}, u32[]{:S(2)}) collective-permute-start(f32[256,128]{1,0:T(8,128)S(1)} %line.2), channel_id=1, source_target_pairs={{0,96},{4,100},{8,104},{12,108},{16,112},{20,116},{24,120},{28,124... | collective-permute-start | bytes 393224 | tf_op jit(solution)/shard_map/ppermute | solution.py:527
  19.3 7.0 %collective-permute-start.5 = (f32[256,128]{1,0:T(8,128)S(1)}, f32[256,128]{1,0:T(8,128)S(1)}, u32[]{:S(2)}, u32[]{:S(2)}) collective-permute-start(f32[256,128]{1,0:T(8,128)S(1)} %line.2), channel_id=1, source_target_pairs={{0,64},{4,68},{8,72},{12,76},{16,80},{20,84},{24,88},{28,92},{32,9... | collective-permute-start | bytes 393224 | tf_op jit(solution)/shard_map/ppermute | solution.py:527
  26.5 6.9 %collective-permute-start.7 = (f32[256,128]{1,0:T(8,128)S(1)}, f32[256,128]{1,0:T(8,128)S(1)}, u32[]{:S(2)}, u32[]{:S(2)}) collective-permute-start(f32[256,128]{1,0:T(8,128)S(1)} %get-tuple-element.122), channel_id=1, source_target_pairs={{0,8},{4,12},{8,16},{12,20},{16,24},{20,28},{24,0},{28,4},{32,40},... | collective-permute-start | bytes 393224 | tf_op jit(solution)/shard_map/ppermute | solution.py:516
  27.3 7.1 %collective-permute-start.8 = (f32[256,128]{1,0:T(8,128)S(1)}, f32[256,128]{1,0:T(8,128)S(1)}, u32[]{:S(2)}, u32[]{:S(2)}) collective-permute-start(f32[256,128]{1,0:T(8,128)S(1)} %get-tuple-element.124), channel_id=1, source_target_pairs={{0,16},{4,20},{8,24},{12,28},{16,0},{20,4},{24,8},{28,12},{32,48},... | collective-permute-start | bytes 393224 | tf_op jit(solution)/shard_map/ppermute | solution.py:516
  29.7 4.8 %collective-permute-start.9 = (f32[256,128]{1,0:T(8,128)S(1)}, f32[256,128]{1,0:T(8,128)S(1)}, u32[]{:S(2)}, u32[]{:S(2)}) collective-permute-start(f32[256,128]{1,0:T(8,128)S(1)} %get-tuple-element.125), channel_id=1, source_target_pairs={{0,24},{4,28},{8,0},{12,4},{16,8},{20,12},{24,16},{28,20},{32,56},... | collective-permute-start | bytes 393224 | tf_op jit(solution)/shard_map/ppermute | solution.py:516
  34.6 3.8 %collective-permute-start.11 = (f32[512,128]{1,0:T(8,128)S(1)}, f32[512,128]{1,0:T(8,128)S(1)}, u32[]{:S(2)}, u32[]{:S(2)}) collective-permute-start(f32[512,128]{1,0:T(8,128)S(1)} %get-tuple-element.127), channel_id=1, source_target_pairs={{0,4},{4,0},{8,12},{12,8},{16,20},{20,16},{24,28},{28,24},{32,36},... | collective-permute-start | bytes 786440 | tf_op jit(solution)/shard_map/ppermute | solution.py:532
  37.3 1.6 %collective-permute-start.10 = (f32[512,128]{1,0:T(8,128)S(1)}, f32[512,128]{1,0:T(8,128)S(1)}, u32[]{:S(2)}, u32[]{:S(2)}) collective-permute-start(f32[512,128]{1,0:T(8,128)S(1)} %get-tuple-element.126), channel_id=1, source_target_pairs={{0,4},{4,0},{8,12},{12,8},{16,20},{20,16},{24,28},{28,24},{32,36},... | collective-permute-start | bytes 786440 | tf_op jit(solution)/shard_map/ppermute | solution.py:532
  39.5 4.6 %collective-permute-start.14 = (f32[2,512]{1,0:T(2,128)S(1)}, f32[2,512]{1,0:T(2,128)S(1)}, u32[]{:S(2)}, u32[]{:S(2)}) collective-permute-start(f32[2,512]{1,0:T(2,128)S(1)} %get-tuple-element.138.s0), channel_id=1, source_target_pairs={{0,3},{1,0},{2,1},{3,2},{4,7},{5,4},{6,5},{7,6},{8,11},{9,8},{10,9... | collective-permute-start | bytes 12296 | tf_op jit(solution)/shard_map/ppermute | solution.py:537
  43.3 4.0 %collective-permute-start.13 = (f32[2,512]{1,0:T(2,128)S(1)}, f32[2,512]{1,0:T(2,128)S(1)}, u32[]{:S(2)}, u32[]{:S(2)}) collective-permute-start(f32[2,512]{1,0:T(2,128)S(1)} %get-tuple-element.138.s0), channel_id=1, source_target_pairs={{0,2},{1,3},{2,0},{3,1},{4,6},{5,7},{6,4},{7,5},{8,10},{9,11},{10,... | collective-permute-start | bytes 12296 | tf_op jit(solution)/shard_map/ppermute | solution.py:537
  43.3 4.0 %collective-permute-start.12 = (f32[2,512]{1,0:T(2,128)S(1)}, f32[2,512]{1,0:T(2,128)S(1)}, u32[]{:S(2)}, u32[]{:S(2)}) collective-permute-start(f32[2,512]{1,0:T(2,128)S(1)} %get-tuple-element.138.s0), channel_id=1, source_target_pairs={{0,1},{1,2},{2,3},{3,0},{4,5},{5,6},{6,7},{7,4},{8,9},{9,10},{10,1... | collective-permute-start | bytes 12296 | tf_op jit(solution)/shard_map/ppermute | solution.py:537
  48.1 3.4 %collective-permute-start.15 = (f32[1024,128]{1,0:T(8,128)S(1)}, f32[1024,128]{1,0:T(8,128)S(1)}, u32[]{:S(2)}, u32[]{:S(2)}) collective-permute-start(f32[1024,128]{1,0:T(8,128)S(1)} %get-tuple-element.153), channel_id=1, source_target_pairs={{0,4},{4,0},{8,12},{12,8},{16,20},{20,16},{24,28},{28,24},{32,36},... | collective-permute-start | bytes 1572872 | tf_op jit(solution)/shard_map/ppermute | solution.py:532
  51.6 8.5 %collective-permute-start.16 = (f32[256,128]{1,0:T(8,128)S(1)}, f32[256,128]{1,0:T(8,128)S(1)}, u32[]{:S(2)}, u32[]{:S(2)}) collective-permute-start(f32[256,128]{1,0:T(8,128)S(1)} %get-tuple-element.155), channel_id=1, source_target_pairs={{0,8},{4,12},{8,16},{12,20},{16,24},{20,28},{24,0},{28,4},{32,40},... | collective-permute-start | bytes 393224 | tf_op jit(solution)/shard_map/ppermute | solution.py:516
  53.1 8.2 %collective-permute-start.17 = (f32[256,128]{1,0:T(8,128)S(1)}, f32[256,128]{1,0:T(8,128)S(1)}, u32[]{:S(2)}, u32[]{:S(2)}) collective-permute-start(f32[256,128]{1,0:T(8,128)S(1)} %get-tuple-element.157), channel_id=1, source_target_pairs={{0,16},{4,20},{8,24},{12,28},{16,0},{20,4},{24,8},{28,12},{32,48},... | collective-permute-start | bytes 393224 | tf_op jit(solution)/shard_map/ppermute | solution.py:516
  55.2 6.1 %collective-permute-start.18 = (f32[256,128]{1,0:T(8,128)S(1)}, f32[256,128]{1,0:T(8,128)S(1)}, u32[]{:S(2)}, u32[]{:S(2)}) collective-permute-start(f32[256,128]{1,0:T(8,128)S(1)} %get-tuple-element.158), channel_id=1, source_target_pairs={{0,24},{4,28},{8,0},{12,4},{16,8},{20,12},{24,16},{28,20},{32,56},... | collective-permute-start | bytes 393224 | tf_op jit(solution)/shard_map/ppermute | solution.py:516
  61.3 8.3 %collective-permute-start.21 = (f32[256,128]{1,0:T(8,128)S(1)}, f32[256,128]{1,0:T(8,128)S(1)}, u32[]{:S(2)}, u32[]{:S(2)}) collective-permute-start(f32[256,128]{1,0:T(8,128)S(1)} %line.3), channel_id=1, source_target_pairs={{0,32},{4,36},{8,40},{12,44},{16,48},{20,52},{24,56},{28,60},{32,6... | collective-permute-start | bytes 393224 | tf_op jit(solution)/shard_map/ppermute | solution.py:527
  61.6 8.0 %collective-permute-start.20 = (f32[256,128]{1,0:T(8,128)S(1)}, f32[256,128]{1,0:T(8,128)S(1)}, u32[]{:S(2)}, u32[]{:S(2)}) collective-permute-start(f32[256,128]{1,0:T(8,128)S(1)} %line.3), channel_id=1, source_target_pairs={{0,64},{4,68},{8,72},{12,76},{16,80},{20,84},{24,88},{28,92},{32,9... | collective-permute-start | bytes 393224 | tf_op jit(solution)/shard_map/ppermute | solution.py:527
  63.9 5.7 %collective-permute-start.19 = (f32[256,128]{1,0:T(8,128)S(1)}, f32[256,128]{1,0:T(8,128)S(1)}, u32[]{:S(2)}, u32[]{:S(2)}) collective-permute-start(f32[256,128]{1,0:T(8,128)S(1)} %line.3), channel_id=1, source_target_pairs={{0,96},{4,100},{8,104},{12,108},{16,112},{20,116},{24,120},{28,124... | collective-permute-start | bytes 393224 | tf_op jit(solution)/shard_map/ppermute | solution.py:527
  69.8 8.1 %collective-permute-start.22 = (f32[256,128]{1,0:T(8,128)S(1)}, f32[256,128]{1,0:T(8,128)S(1)}, u32[]{:S(2)}, u32[]{:S(2)}) collective-permute-start(f32[256,128]{1,0:T(8,128)S(1)} %get-tuple-element.161), channel_id=1, source_target_pairs={{0,8},{4,12},{8,16},{12,20},{16,24},{20,28},{24,0},{28,4},{32,40},... | collective-permute-start | bytes 393224 | tf_op jit(solution)/shard_map/ppermute | solution.py:516
  72.3 5.9 %collective-permute-start.23 = (f32[256,128]{1,0:T(8,128)S(1)}, f32[256,128]{1,0:T(8,128)S(1)}, u32[]{:S(2)}, u32[]{:S(2)}) collective-permute-start(f32[256,128]{1,0:T(8,128)S(1)} %get-tuple-element.163), channel_id=1, source_target_pairs={{0,16},{4,20},{8,24},{12,28},{16,0},{20,4},{24,8},{28,12},{32,48},... | collective-permute-start | bytes 393224 | tf_op jit(solution)/shard_map/ppermute | solution.py:516
  73.9 4.7 %collective-permute-start.24 = (f32[256,128]{1,0:T(8,128)S(1)}, f32[256,128]{1,0:T(8,128)S(1)}, u32[]{:S(2)}, u32[]{:S(2)}) collective-permute-start(f32[256,128]{1,0:T(8,128)S(1)} %get-tuple-element.164), channel_id=1, source_target_pairs={{0,24},{4,28},{8,0},{12,4},{16,8},{20,12},{24,16},{28,20},{32,56},... | collective-permute-start | bytes 393224 | tf_op jit(solution)/shard_map/ppermute | solution.py:516
  78.7 4.4 %collective-permute-start.25 = (f32[1024,128]{1,0:T(8,128)S(1)}, f32[1024,128]{1,0:T(8,128)S(1)}, u32[]{:S(2)}, u32[]{:S(2)}) collective-permute-start(f32[1024,128]{1,0:T(8,128)S(1)} %get-tuple-element.165), channel_id=1, source_target_pairs={{0,4},{4,0},{8,12},{12,8},{16,20},{20,16},{24,28},{28,24},{32,36},... | collective-permute-start | bytes 1572872 | tf_op jit(solution)/shard_map/ppermute | solution.py:532

commit v7 on v6

--- a/solution.py
+++ b/solution.py
@@ -580,14 +580,14 @@
     g0, state0 = local_grad(0, t0, output0, scaled0, stats)
     arrays = ((q0, k0, v0, g0, prefix0, *turned0), (q1, k1, v1, g1, prefix1, *turned1))
     pieces = along_x(split(chip, state0, near0))
-    query_grad, parts = middle_gradients(0, ((0, 0), (0, 1), (0, 2)), core, arrays)
+    query_grad, parts = middle_gradients(0, ((0, 0), (0, 1)), core, arrays)
     pieces[1] = after(pieces[1], query_grad)
     sums = along_y(line_sum(pieces), True)
-    query_grad, more = middle_gradients(1, ((0, 3), (1, 0), (1, 1)), core, arrays, (query_grad,))
+    query_grad, more = middle_gradients(1, ((0, 2), (0, 3), (1, 0)), core, arrays, (query_grad,))
     parts.update(more)
     sums[0] = after(sums[0], query_grad)
     pieces = along_x(entering(chip, pieces, sums, True))
-    query_grad, more = middle_gradients(2, ((1, 2), (1, 3)), core, arrays, (query_grad,))
+    query_grad, more = middle_gradients(2, ((1, 1), (1, 2), (1, 3)), core, arrays, (query_grad,))
     parts.update(more)
     pieces[1] = after(pieces[1], query_grad)
     base0, base1 = join(chip, core, pieces, state0, near0, True)

time: 85.3 us -> 85.3 us (level)
  transfers between devices with their start and end apart: 26 -> 26, of which waited for: 12 -> 10; matrix products, arithmetic and copies ran while one was open for 0% -> 0% of each run, Pallas kernels for 32% -> 32%
where the time goes in v7:
time: 85.3 us; the launch traced here: 85.1 us
  starting transfers between devices  39 us (46%)
  Pallas kernels  32.7 us (38%)
  waiting for transfers between devices  12.3 us (14%)
  between operations  1.1 us (1%)
    pallas_call x23, Pallas kernels, run(): kernel(*(pltpu.with_memory_space_constraint(array, pltpu.HBM) if spec is...  32.7 us
    ppermute x12, starting transfers between devices, along_x(): got[hop] = lax.ppermute(pieces[hop], 'ctx', pairs)  18.5 us
    ppermute x5, starting transfers between devices, swap(): return lax.ppermute(part, 'ctx', PARTNERS)  8.67 us
    ppermute x6, starting transfers between devices, along_y(): got[hop] = lax.ppermute(part, 'ctx', pairs)  7.29 us
    ppermute x3, starting transfers between devices, along_heads(): lax.ppermute(stats, 'head', [(i, (i + hop) % 4) for i in range(4)])  4.51 us
    ppermute x12, waiting for transfers between devices, along_x(): got[hop] = lax.ppermute(pieces[hop], 'ctx', pairs)  4.28 us
    ppermute x6, waiting for transfers between devices, along_y(): got[hop] = lax.ppermute(part, 'ctx', pairs)  3.89 us
    ppermute x3, waiting for transfers between devices, along_heads(): lax.ppermute(stats, 'head', [(i, (i + hop) % 4) for i in range(4)])  3.28 us
  transfers between devices with their start and end apart: 26, of which 10 were waited for; matrix products, arithmetic and copies ran while one was open for 0% of the time, Pallas kernels for 32%

profile of v7, /device:TPU:1, one launch (start us, length us, event | category | flops | bytes accessed | tf_op | source)
XLA Modules:
  0.0 85.1 jit_solution(10118318075129477261)
XLA Ops:
  0.7 1.9 %state1.1 = (bf16[512,1024]{1,0:T(8,128)(2,1)S(1)}, bf16[512,1024]{1,0:T(8,128)(2,1)S(1)}, f32[1024,128]{1,0:T(8,128)S(1)}) custom-call(s32[1]{0:T(128)} %bitcast.core, bf16[512,2048]{1,0:T(8,128)(2,1)} %k_all.3, bf16[512,2048]{1,0:T(8,128)(2,1)} %v_all.3), custom_call_target="tpu_custom_call" | custom-call | flops 134217728 | bytes 2097152 | tf_op jit(solution)/shard_map/state1/pallas_call | solution.py:81
  2.6 0.0 copy-start
  2.6 1.5 %collective-permute-start = (f32[1024,128]{1,0:T(8,128)S(1)}, f32[1024,128]{1,0:T(8,128)S(1)}, u32[]{:S(2)}, u32[]{:S(2)}) collective-permute-start(f32[1024,128]{1,0:T(8,128)S(1)} %get-tuple-element.111), channel_id=1, source_target_pairs={{0,4},{4,0},{8,12},{12,8},{16,20},{20,16},{24,28},{28,24},{32,36},... | collective-permute-start | bytes 1572872 | tf_op jit(solution)/shard_map/ppermute | solution.py:532
  4.1 1.9 %state0.1 = (bf16[512,1024]{1,0:T(8,128)(2,1)S(1)}, bf16[512,1024]{1,0:T(8,128)(2,1)S(1)}, f32[1024,128]{1,0:T(8,128)S(1)}) custom-call(s32[1]{0:T(128)} %bitcast.core, bf16[512,2048]{1,0:T(8,128)(2,1)} %k_all.3, bf16[512,2048]{1,0:T(8,128)(2,1)} %v_all.3), custom_call_target="tpu_custom_call" | custom-call | flops 134217728 | bytes 2097152 | tf_op jit(solution)/shard_map/state0/pallas_call | solution.py:81
  6.1 0.1 split.2
  6.1 1.4 %collective-permute-start.1 = (f32[256,128]{1,0:T(8,128)S(1)}, f32[256,128]{1,0:T(8,128)S(1)}, u32[]{:S(2)}, u32[]{:S(2)}) collective-permute-start(f32[256,128]{1,0:T(8,128)S(1)} %get-tuple-element.113), channel_id=1, source_target_pairs={{0,8},{4,12},{8,16},{12,20},{16,24},{20,28},{24,0},{28,4},{32,40},... | collective-permute-start | bytes 393224 | tf_op jit(solution)/shard_map/ppermute | solution.py:516
  7.5 2.5 %collective-permute-start.2 = (f32[256,128]{1,0:T(8,128)S(1)}, f32[256,128]{1,0:T(8,128)S(1)}, u32[]{:S(2)}, u32[]{:S(2)}) collective-permute-start(f32[256,128]{1,0:T(8,128)S(1)} %get-tuple-element.118), channel_id=1, source_target_pairs={{0,16},{4,20},{8,24},{12,28},{16,0},{20,4},{24,8},{28,12},{32,48},... | collective-permute-start | bytes 393224 | tf_op jit(solution)/shard_map/ppermute | solution.py:516
  10.0 1.1 %collective-permute-start.3 = (f32[256,128]{1,0:T(8,128)S(1)}, f32[256,128]{1,0:T(8,128)S(1)}, u32[]{:S(2)}, u32[]{:S(2)}) collective-permute-start(f32[256,128]{1,0:T(8,128)S(1)} %get-tuple-element.119), channel_id=1, source_target_pairs={{0,24},{4,28},{8,0},{12,4},{16,8},{20,12},{24,16},{28,20},{32,56},... | collective-permute-start | bytes 393224 | tf_op jit(solution)/shard_map/ppermute | solution.py:516
  11.1 4.4 %intra0.1 = (bf16[512,1024]{1,0:T(8,128)(2,1)S(1)}, bf16[1024,512]{1,0:T(8,128)(2,1)S(1)}, f32[512,1024]{1,0:T(8,128)S(1)}, f32[512,1024]{1,0:T(8,128)S(1)}, bf1...) custom-call(s32[1]{0:T(128)} %bitcast.core, bf16[512,2048]{1,0:T(8,128)(2,1)} %q_all.5, ...), custom_call_target="tpu_custom_call" | custom-call | flops 1342177280 | bytes 8388608 | tf_op jit(solution)/shard_map/intra0/pallas_call | solution.py:81
  15.5 0.9 %collective-permute-done.2.c.refs_2_ = f32[256,128]{1,0:T(8,128)S(1)} collective-permute-done((f32[256,128]{1,0:T(8,128)S(1)}, f32[256,128]{1,0:T(8,128)S(1)}, u32[]{:S(2)}, u32[]{:S(2)}) %collective-permute-start.2) | collective-permute-done | bytes 131104 | tf_op jit(solution)/shard_map/ppermute | solution.py:516
  16.4 0.0 collective-permute-done.3.d.refs_3_
  16.5 1.4 %collective-permute-start.4 = (f32[256,128]{1,0:T(8,128)S(1)}, f32[256,128]{1,0:T(8,128)S(1)}, u32[]{:S(2)}, u32[]{:S(2)}) collective-permute-start(f32[256,128]{1,0:T(8,128)S(1)} %line.2), channel_id=1, source_target_pairs={{0,32},{4,36},{8,40},{12,44},{16,48},{20,52},{24,56},{28,60},{32,6... | collective-permute-start | bytes 393224 | tf_op jit(solution)/shard_map/ppermute | solution.py:527
  17.8 1.5 %collective-permute-start.6 = (f32[256,128]{1,0:T(8,128)S(1)}, f32[256,128]{1,0:T(8,128)S(1)}, u32[]{:S(2)}, u32[]{:S(2)}) collective-permute-start(f32[256,128]{1,0:T(8,128)S(1)} %line.2), channel_id=1, source_target_pairs={{0,96},{4,100},{8,104},{12,108},{16,112},{20,116},{24,120},{28,124... | collective-permute-start | bytes 393224 | tf_op jit(solution)/shard_map/ppermute | solution.py:527
  19.3 1.6 %collective-permute-start.5 = (f32[256,128]{1,0:T(8,128)S(1)}, f32[256,128]{1,0:T(8,128)S(1)}, u32[]{:S(2)}, u32[]{:S(2)}) collective-permute-start(f32[256,128]{1,0:T(8,128)S(1)} %line.2), channel_id=1, source_target_pairs={{0,64},{4,68},{8,72},{12,76},{16,80},{20,84},{24,88},{28,92},{32,9... | collective-permute-start | bytes 393224 | tf_op jit(solution)/shard_map/ppermute | solution.py:527
  20.9 2.7 %intra1.1 = (bf16[512,1024]{1,0:T(8,128)(2,1)S(1)}, bf16[1024,512]{1,0:T(8,128)(2,1)S(1)}, f32[512,1024]{1,0:T(8,128)S(1)}, f32[512,1024]{1,0:T(8,128)S(1)}, bf1...) custom-call(s32[1]{0:T(128)} %bitcast.core, bf16[512,2048]{1,0:T(8,128)(2,1)} %q_all.5, ...), custom_call_target="tpu_custom_call" | custom-call | flops 671088640 | bytes 4194304 | tf_op jit(solution)/shard_map/intra1/pallas_call | solution.py:81
  23.6 2.7 %collective-permute-done.5.refs_5_ = f32[256,128]{1,0:T(8,128)S(1)} collective-permute-done((f32[256,128]{1,0:T(8,128)S(1)}, f32[256,128]{1,0:T(8,128)S(1)}, u32[]{:S(2)}, u32[]{:S(2)}) %collective-permute-start.5) | collective-permute-done | bytes 131104 | tf_op jit(solution)/shard_map/ppermute | solution.py:527
  26.3 0.2 enter0.1
  26.5 0.8 collective-permute-start.7
  27.3 2.4 %collective-permute-start.8 = (f32[256,128]{1,0:T(8,128)S(1)}, f32[256,128]{1,0:T(8,128)S(1)}, u32[]{:S(2)}, u32[]{:S(2)}) collective-permute-start(f32[256,128]{1,0:T(8,128)S(1)} %get-tuple-element.124), channel_id=1, source_target_pairs={{0,16},{4,20},{8,24},{12,28},{16,0},{20,4},{24,8},{28,12},{32,48},... | collective-permute-start | bytes 393224 | tf_op jit(solution)/shard_map/ppermute | solution.py:516
  29.7 1.0 %collective-permute-start.9 = (f32[256,128]{1,0:T(8,128)S(1)}, f32[256,128]{1,0:T(8,128)S(1)}, u32[]{:S(2)}, u32[]{:S(2)}) collective-permute-start(f32[256,128]{1,0:T(8,128)S(1)} %get-tuple-element.125), channel_id=1, source_target_pairs={{0,24},{4,28},{8,0},{12,4},{16,8},{20,12},{24,16},{28,20},{32,56},... | collective-permute-start | bytes 393224 | tf_op jit(solution)/shard_map/ppermute | solution.py:516
  30.8 2.7 %intra2.1 = (bf16[512,1024]{1,0:T(8,128)(2,1)S(1)}, bf16[1024,512]{1,0:T(8,128)(2,1)S(1)}, f32[512,1024]{1,0:T(8,128)S(1)}, f32[512,1024]{1,0:T(8,128)S(1)}, bf1...) custom-call(s32[1]{0:T(128)} %bitcast.core, ...), custom_call_target="tpu_custom_call", output_to_operand_aliasing={{0}: (6, {}), {1}: (7, {}), {2}: (8, {}), {3}: (9, {}), {4}... | custom-call | flops 671088640 | bytes 4194304 | tf_op jit(solution)/shard_map/intra2/pallas_call | solution.py:81
  33.4 0.0 collective-permute-done.7.b
  33.4 0.9 %collective-permute-done.8.c = f32[256,128]{1,0:T(8,128)S(1)} collective-permute-done((f32[256,128]{1,0:T(8,128)S(1)}, f32[256,128]{1,0:T(8,128)S(1)}, u32[]{:S(2)}, u32[]{:S(2)}) %collective-permute-start.8) | collective-permute-done | bytes 131104 | tf_op jit(solution)/shard_map/ppermute | solution.py:516
  34.4 0.1 collective-permute-done.9.d
  34.5 0.1 join0.1
  34.6 2.7 %collective-permute-start.11 = (f32[512,128]{1,0:T(8,128)S(1)}, f32[512,128]{1,0:T(8,128)S(1)}, u32[]{:S(2)}, u32[]{:S(2)}) collective-permute-start(f32[512,128]{1,0:T(8,128)S(1)} %get-tuple-element.127), channel_id=1, source_target_pairs={{0,4},{4,0},{8,12},{12,8},{16,20},{20,16},{24,28},{28,24},{32,36},... | collective-permute-start | bytes 786440 | tf_op jit(solution)/shard_map/ppermute | solution.py:532
  37.3 0.3 collective-permute-start.10
  37.6 0.7 output0.1
  38.3 0.2 collective-permute-done.11.base
  38.5 0.4 output1.1
  38.9 0.0 collective-permute-done.10.base
  38.9 0.6 output2.1
  39.5 3.8 %collective-permute-start.14 = (f32[2,512]{1,0:T(2,128)S(1)}, f32[2,512]{1,0:T(2,128)S(1)}, u32[]{:S(2)}, u32[]{:S(2)}) collective-permute-start(f32[2,512]{1,0:T(2,128)S(1)} %get-tuple-element.138.s0), channel_id=1, source_target_pairs={{0,3},{1,0},{2,1},{3,2},{4,7},{5,4},{6,5},{7,6},{8,11},{9,8},{10,9... | collective-permute-start | bytes 12296 | tf_op jit(solution)/shard_map/ppermute | solution.py:537
  43.3 0.0 collective-permute-start.13
  43.3 0.7 collective-permute-start.12
  44.0 0.1 collective-permute-done.14.s3
  44.0 3.2 %collective-permute-done.13.s2 = f32[2,512]{1,0:T(2,128)S(1)} collective-permute-done((f32[2,512]{1,0:T(2,128)S(1)}, f32[2,512]{1,0:T(2,128)S(1)}, u32[]{:S(2)}, u32[]{:S(2)}) %collective-permute-start.13) | collective-permute-done | bytes 4128 | tf_op jit(solution)/shard_map/ppermute | solution.py:537
  47.2 0.8 grad1.1
  48.1 1.9 %collective-permute-start.15 = (f32[1024,128]{1,0:T(8,128)S(1)}, f32[1024,128]{1,0:T(8,128)S(1)}, u32[]{:S(2)}, u32[]{:S(2)}) collective-permute-start(f32[1024,128]{1,0:T(8,128)S(1)} %get-tuple-element.153), channel_id=1, source_target_pairs={{0,4},{4,0},{8,12},{12,8},{16,20},{20,16},{24,28},{28,24},{32,36},... | collective-permute-start | bytes 1572872 | tf_op jit(solution)/shard_map/ppermute | solution.py:532
  50.0 0.8 grad0.1
  50.8 0.7 collective-permute-done.15.near
  51.5 0.1 split.3
  51.6 1.5 %collective-permute-start.16 = (f32[256,128]{1,0:T(8,128)S(1)}, f32[256,128]{1,0:T(8,128)S(1)}, u32[]{:S(2)}, u32[]{:S(2)}) collective-permute-start(f32[256,128]{1,0:T(8,128)S(1)} %get-tuple-element.155), channel_id=1, source_target_pairs={{0,8},{4,12},{8,16},{12,20},{16,24},{20,28},{24,0},{28,4},{32,40},... | collective-permute-start | bytes 393224 | tf_op jit(solution)/shard_map/ppermute | solution.py:516
  53.1 2.1 %collective-permute-start.17 = (f32[256,128]{1,0:T(8,128)S(1)}, f32[256,128]{1,0:T(8,128)S(1)}, u32[]{:S(2)}, u32[]{:S(2)}) collective-permute-start(f32[256,128]{1,0:T(8,128)S(1)} %get-tuple-element.157), channel_id=1, source_target_pairs={{0,16},{4,20},{8,24},{12,28},{16,0},{20,4},{24,8},{28,12},{32,48},... | collective-permute-start | bytes 393224 | tf_op jit(solution)/shard_map/ppermute | solution.py:516
  55.2 0.6 collective-permute-start.18
  55.8 3.1 %middle0.1 = (bf16[512,2048]{1,0:T(8,128)(2,1)}, f32[512,256]{1,0:T(8,128)S(1)}, f32[512,256]{1,0:T(8,128)S(1)}, f32[512,256]{1,0:T(8,128)S(1)}, f32[512,256]{1,0:T(8,128)S(1)}) custom-call(s32[1]{0:T(128)} %bitcast.core, bf16[512,1024]{1,0:T(8,128)(2,1)S(1)} %get-tuple-element.128.q.refs_0_, bf16[512,1024]{1,0:T(8,128)(2,1)S(1)} %get-tuple-element.114.k.refs_1_, ...), custom_call_target="tpu_custom_call" | custom-call | flops 1073741824 | bytes 2097152 | tf_op jit(solution)/shard_map/middle0/pallas_call | solution.py:81
  58.9 2.3 %collective-permute-done.17.c.refs_2_ = f32[256,128]{1,0:T(8,128)S(1)} collective-permute-done((f32[256,128]{1,0:T(8,128)S(1)}, f32[256,128]{1,0:T(8,128)S(1)}, u32[]{:S(2)}, u32[]{:S(2)}) %collective-permute-start.17) | collective-permute-done | bytes 131104 | tf_op jit(solution)/shard_map/ppermute | solution.py:516
  61.3 0.0 collective-permute-done.18.d.refs_3_
  61.3 0.3 collective-permute-start.21
  61.6 2.3 %collective-permute-start.20 = (f32[256,128]{1,0:T(8,128)S(1)}, f32[256,128]{1,0:T(8,128)S(1)}, u32[]{:S(2)}, u32[]{:S(2)}) collective-permute-start(f32[256,128]{1,0:T(8,128)S(1)} %line.3), channel_id=1, source_target_pairs={{0,64},{4,68},{8,72},{12,76},{16,80},{20,84},{24,88},{28,92},{32,9... | collective-permute-start | bytes 393224 | tf_op jit(solution)/shard_map/ppermute | solution.py:527
  63.9 0.2 collective-permute-start.19
  64.1 4.2 %middle1.1 = (bf16[512,2048]{1,0:T(8,128)(2,1)}, f32[512,256]{1,0:T(8,128)S(1)}, f32[512,256]{1,0:T(8,128)S(1)}, f32[512,256]{1,0:T(8,128)S(1)}, f32[512,256]{1,...) custom-call(s32[1]{0:T(128)} %bitcast.core, ...), custom_call_target="tpu_custom_call", output_to_operand_aliasing={{0}: (15, {})} | custom-call | flops 1610612736 | bytes 3145728 | tf_op jit(solution)/shard_map/middle1/pallas_call | solution.py:81
  68.4 1.2 %collective-permute-done.19.refs_4_ = f32[256,128]{1,0:T(8,128)S(1)} collective-permute-done((f32[256,128]{1,0:T(8,128)S(1)}, f32[256,128]{1,0:T(8,128)S(1)}, u32[]{:S(2)}, u32[]{:S(2)}) %collective-permute-start.19) | collective-permute-done | bytes 131104 | tf_op jit(solution)/shard_map/ppermute | solution.py:527
  69.6 0.0 collective-permute-done.21.refs_6_
  69.6 0.2 enter1.1
  69.8 2.5 %collective-permute-start.22 = (f32[256,128]{1,0:T(8,128)S(1)}, f32[256,128]{1,0:T(8,128)S(1)}, u32[]{:S(2)}, u32[]{:S(2)}) collective-permute-start(f32[256,128]{1,0:T(8,128)S(1)} %get-tuple-element.161), channel_id=1, source_target_pairs={{0,8},{4,12},{8,16},{12,20},{16,24},{20,28},{24,0},{28,4},{32,40},... | collective-permute-start | bytes 393224 | tf_op jit(solution)/shard_map/ppermute | solution.py:516
  72.3 1.6 %collective-permute-start.23 = (f32[256,128]{1,0:T(8,128)S(1)}, f32[256,128]{1,0:T(8,128)S(1)}, u32[]{:S(2)}, u32[]{:S(2)}) collective-permute-start(f32[256,128]{1,0:T(8,128)S(1)} %get-tuple-element.163), channel_id=1, source_target_pairs={{0,16},{4,20},{8,24},{12,28},{16,0},{20,4},{24,8},{28,12},{32,48},... | collective-permute-start | bytes 393224 | tf_op jit(solution)/shard_map/ppermute | solution.py:516
  73.9 0.8 collective-permute-start.24
  74.8 4.2 %middle2.1 = (bf16[512,2048]{1,0:T(8,128)(2,1)}, f32[512,256]{1,0:T(8,128)S(1)}, f32[512,256]{1,0:T(8,128)S(1)}, f32[512,256]{1,0:T(8,128)S(1)}, f32[512,256]{1,...) custom-call(s32[1]{0:T(128)} %bitcast.core, ...), custom_call_target="tpu_custom_call", output_to_operand_aliasing={{0}: (8, {})} | custom-call | flops 1610612736 | bytes 3145728 | tf_op jit(solution)/shard_map/middle2/pallas_call | solution.py:81
  79.0 0.0 collective-permute-done.22.b
  79.0 0.1 join1.1
  79.1 2.3 %collective-permute-start.25 = (f32[1024,128]{1,0:T(8,128)S(1)}, f32[1024,128]{1,0:T(8,128)S(1)}, u32[]{:S(2)}, u32[]{:S(2)}) collective-permute-start(f32[1024,128]{1,0:T(8,128)S(1)} %get-tuple-element.165), channel_id=1, source_target_pairs={{0,4},{4,0},{8,12},{12,8},{16,20},{20,16},{24,28},{28,24},{32,36},... | collective-permute-start | bytes 1572872 | tf_op jit(solution)/shard_map/ppermute | solution.py:532
  81.5 1.7 %last0.1 = (bf16[512,2048]{1,0:T(8,128)(2,1)}, bf16[512,2048]{1,0:T(8,128)(2,1)}) custom-call(s32[1]{0:T(128)} %bitcast.core, bf16[512,1024]{1,0:T(8,128)(2,1)S(1)} %get-tuple-element.114.k.refs_1_, bf16[512,1024]{1,0:T(8,128)(2,1)S(1)} %get-tuple-element.115.v.refs_2_, f32[1024,128]{1,0:T(8,128)S(1)} %get-tuple-element.174.base, ...), custom_call_target="tpu_custom_call" | custom-call | flops 268435456 | bytes 2097152 | tf_op jit(solution)/shard_map/last0/pallas_call | solution.py:81
  83.2 1.7 %last1.1 = (bf16[512,2048]{1,0:T(8,128)(2,1)}, bf16[512,2048]{1,0:T(8,128)(2,1)}) custom-call(s32[1]{0:T(128)} %bitcast.core, bf16[512,1024]{1,0:T(8,128)(2,1)S(1)} %get-tuple-element.96.k.refs_8_.refs_1_, bf16[512,1024]{1,0:T(8,128)(2,1)S(1)} %get-tuple-element.97.v.refs_9_.refs_2_, ...), custom_call_target="tpu_custom_call", output_to_operand_aliasing={{0}: (12, {}), {1}: (13, {})} | custom-call | flops 268435456 | bytes 2097152 | tf_op jit(solution)/shard_map/last1/pallas_call | solution.py:81
  (13 shorter events, 0.1 us)
Async XLA Ops:
  2.6 8.5 %copy-start = (f32[2048]{0:T(1024)S(1)}, f32[2048]{0:T(1024)}, u32[]{:S(2)}) copy-start(f32[2048]{0:T(1024)} %param.9) | copy-start | bytes 24580
  2.6 3.4 %collective-permute-start = (f32[1024,128]{1,0:T(8,128)S(1)}, f32[1024,128]{1,0:T(8,128)S(1)}, u32[]{:S(2)}, u32[]{:S(2)}) collective-permute-start(f32[1024,128]{1,0:T(8,128)S(1)} %get-tuple-element.111), channel_id=1, source_target_pairs={{0,4},{4,0},{8,12},{12,8},{16,20},{20,16},{24,28},{28,24},{32,36},... | collective-permute-start | bytes 1572872 | tf_op jit(solution)/shard_map/ppermute | solution.py:532
  6.1 9.4 %collective-permute-start.1 = (f32[256,128]{1,0:T(8,128)S(1)}, f32[256,128]{1,0:T(8,128)S(1)}, u32[]{:S(2)}, u32[]{:S(2)}) collective-permute-start(f32[256,128]{1,0:T(8,128)S(1)} %get-tuple-element.113), channel_id=1, source_target_pairs={{0,8},{4,12},{8,16},{12,20},{16,24},{20,28},{24,0},{28,4},{32,40},... | collective-permute-start | bytes 393224 | tf_op jit(solution)/shard_map/ppermute | solution.py:516
  7.5 8.9 %collective-permute-start.2 = (f32[256,128]{1,0:T(8,128)S(1)}, f32[256,128]{1,0:T(8,128)S(1)}, u32[]{:S(2)}, u32[]{:S(2)}) collective-permute-start(f32[256,128]{1,0:T(8,128)S(1)} %get-tuple-element.118), channel_id=1, source_target_pairs={{0,16},{4,20},{8,24},{12,28},{16,0},{20,4},{24,8},{28,12},{32,48},... | collective-permute-start | bytes 393224 | tf_op jit(solution)/shard_map/ppermute | solution.py:516
  10.0 6.5 %collective-permute-start.3 = (f32[256,128]{1,0:T(8,128)S(1)}, f32[256,128]{1,0:T(8,128)S(1)}, u32[]{:S(2)}, u32[]{:S(2)}) collective-permute-start(f32[256,128]{1,0:T(8,128)S(1)} %get-tuple-element.119), channel_id=1, source_target_pairs={{0,24},{4,28},{8,0},{12,4},{16,8},{20,12},{24,16},{28,20},{32,56},... | collective-permute-start | bytes 393224 | tf_op jit(solution)/shard_map/ppermute | solution.py:516
  16.5 7.1 %collective-permute-start.4 = (f32[256,128]{1,0:T(8,128)S(1)}, f32[256,128]{1,0:T(8,128)S(1)}, u32[]{:S(2)}, u32[]{:S(2)}) collective-permute-start(f32[256,128]{1,0:T(8,128)S(1)} %line.2), channel_id=1, source_target_pairs={{0,32},{4,36},{8,40},{12,44},{16,48},{20,52},{24,56},{28,60},{32,6... | collective-permute-start | bytes 393224 | tf_op jit(solution)/shard_map/ppermute | solution.py:527
  17.8 5.8 %collective-permute-start.6 = (f32[256,128]{1,0:T(8,128)S(1)}, f32[256,128]{1,0:T(8,128)S(1)}, u32[]{:S(2)}, u32[]{:S(2)}) collective-permute-start(f32[256,128]{1,0:T(8,128)S(1)} %line.2), channel_id=1, source_target_pairs={{0,96},{4,100},{8,104},{12,108},{16,112},{20,116},{24,120},{28,124... | collective-permute-start | bytes 393224 | tf_op jit(solution)/shard_map/ppermute | solution.py:527
  19.3 7.0 %collective-permute-start.5 = (f32[256,128]{1,0:T(8,128)S(1)}, f32[256,128]{1,0:T(8,128)S(1)}, u32[]{:S(2)}, u32[]{:S(2)}) collective-permute-start(f32[256,128]{1,0:T(8,128)S(1)} %line.2), channel_id=1, source_target_pairs={{0,64},{4,68},{8,72},{12,76},{16,80},{20,84},{24,88},{28,92},{32,9... | collective-permute-start | bytes 393224 | tf_op jit(solution)/shard_map/ppermute | solution.py:527
  26.5 6.9 %collective-permute-start.7 = (f32[256,128]{1,0:T(8,128)S(1)}, f32[256,128]{1,0:T(8,128)S(1)}, u32[]{:S(2)}, u32[]{:S(2)}) collective-permute-start(f32[256,128]{1,0:T(8,128)S(1)} %get-tuple-element.122), channel_id=1, source_target_pairs={{0,8},{4,12},{8,16},{12,20},{16,24},{20,28},{24,0},{28,4},{32,40},... | collective-permute-start | bytes 393224 | tf_op jit(solution)/shard_map/ppermute | solution.py:516
  27.3 7.1 %collective-permute-start.8 = (f32[256,128]{1,0:T(8,128)S(1)}, f32[256,128]{1,0:T(8,128)S(1)}, u32[]{:S(2)}, u32[]{:S(2)}) collective-permute-start(f32[256,128]{1,0:T(8,128)S(1)} %get-tuple-element.124), channel_id=1, source_target_pairs={{0,16},{4,20},{8,24},{12,28},{16,0},{20,4},{24,8},{28,12},{32,48},... | collective-permute-start | bytes 393224 | tf_op jit(solution)/shard_map/ppermute | solution.py:516
  29.7 4.8 %collective-permute-start.9 = (f32[256,128]{1,0:T(8,128)S(1)}, f32[256,128]{1,0:T(8,128)S(1)}, u32[]{:S(2)}, u32[]{:S(2)}) collective-permute-start(f32[256,128]{1,0:T(8,128)S(1)} %get-tuple-element.125), channel_id=1, source_target_pairs={{0,24},{4,28},{8,0},{12,4},{16,8},{20,12},{24,16},{28,20},{32,56},... | collective-permute-start | bytes 393224 | tf_op jit(solution)/shard_map/ppermute | solution.py:516
  34.6 3.8 %collective-permute-start.11 = (f32[512,128]{1,0:T(8,128)S(1)}, f32[512,128]{1,0:T(8,128)S(1)}, u32[]{:S(2)}, u32[]{:S(2)}) collective-permute-start(f32[512,128]{1,0:T(8,128)S(1)} %get-tuple-element.127), channel_id=1, source_target_pairs={{0,4},{4,0},{8,12},{12,8},{16,20},{20,16},{24,28},{28,24},{32,36},... | collective-permute-start | bytes 786440 | tf_op jit(solution)/shard_map/ppermute | solution.py:532
  37.3 1.6 %collective-permute-start.10 = (f32[512,128]{1,0:T(8,128)S(1)}, f32[512,128]{1,0:T(8,128)S(1)}, u32[]{:S(2)}, u32[]{:S(2)}) collective-permute-start(f32[512,128]{1,0:T(8,128)S(1)} %get-tuple-element.126), channel_id=1, source_target_pairs={{0,4},{4,0},{8,12},{12,8},{16,20},{20,16},{24,28},{28,24},{32,36},... | collective-permute-start | bytes 786440 | tf_op jit(solution)/shard_map/ppermute | solution.py:532
  39.5 4.6 %collective-permute-start.14 = (f32[2,512]{1,0:T(2,128)S(1)}, f32[2,512]{1,0:T(2,128)S(1)}, u32[]{:S(2)}, u32[]{:S(2)}) collective-permute-start(f32[2,512]{1,0:T(2,128)S(1)} %get-tuple-element.138.s0), channel_id=1, source_target_pairs={{0,3},{1,0},{2,1},{3,2},{4,7},{5,4},{6,5},{7,6},{8,11},{9,8},{10,9... | collective-permute-start | bytes 12296 | tf_op jit(solution)/shard_map/ppermute | solution.py:537
  43.3 4.0 %collective-permute-start.13 = (f32[2,512]{1,0:T(2,128)S(1)}, f32[2,512]{1,0:T(2,128)S(1)}, u32[]{:S(2)}, u32[]{:S(2)}) collective-permute-start(f32[2,512]{1,0:T(2,128)S(1)} %get-tuple-element.138.s0), channel_id=1, source_target_pairs={{0,2},{1,3},{2,0},{3,1},{4,6},{5,7},{6,4},{7,5},{8,10},{9,11},{10,... | collective-permute-start | bytes 12296 | tf_op jit(solution)/shard_map/ppermute | solution.py:537
  43.3 4.0 %collective-permute-start.12 = (f32[2,512]{1,0:T(2,128)S(1)}, f32[2,512]{1,0:T(2,128)S(1)}, u32[]{:S(2)}, u32[]{:S(2)}) collective-permute-start(f32[2,512]{1,0:T(2,128)S(1)} %get-tuple-element.138.s0), channel_id=1, source_target_pairs={{0,1},{1,2},{2,3},{3,0},{4,5},{5,6},{6,7},{7,4},{8,9},{9,10},{10,1... | collective-permute-start | bytes 12296 | tf_op jit(solution)/shard_map/ppermute | solution.py:537
  48.1 3.4 %collective-permute-start.15 = (f32[1024,128]{1,0:T(8,128)S(1)}, f32[1024,128]{1,0:T(8,128)S(1)}, u32[]{:S(2)}, u32[]{:S(2)}) collective-permute-start(f32[1024,128]{1,0:T(8,128)S(1)} %get-tuple-element.153), channel_id=1, source_target_pairs={{0,4},{4,0},{8,12},{12,8},{16,20},{20,16},{24,28},{28,24},{32,36},... | collective-permute-start | bytes 1572872 | tf_op jit(solution)/shard_map/ppermute | solution.py:532
  51.6 7.4 %collective-permute-start.16 = (f32[256,128]{1,0:T(8,128)S(1)}, f32[256,128]{1,0:T(8,128)S(1)}, u32[]{:S(2)}, u32[]{:S(2)}) collective-permute-start(f32[256,128]{1,0:T(8,128)S(1)} %get-tuple-element.155), channel_id=1, source_target_pairs={{0,8},{4,12},{8,16},{12,20},{16,24},{20,28},{24,0},{28,4},{32,40},... | collective-permute-start | bytes 393224 | tf_op jit(solution)/shard_map/ppermute | solution.py:516
  53.1 8.2 %collective-permute-start.17 = (f32[256,128]{1,0:T(8,128)S(1)}, f32[256,128]{1,0:T(8,128)S(1)}, u32[]{:S(2)}, u32[]{:S(2)}) collective-permute-start(f32[256,128]{1,0:T(8,128)S(1)} %get-tuple-element.157), channel_id=1, source_target_pairs={{0,16},{4,20},{8,24},{12,28},{16,0},{20,4},{24,8},{28,12},{32,48},... | collective-permute-start | bytes 393224 | tf_op jit(solution)/shard_map/ppermute | solution.py:516
  55.2 6.1 %collective-permute-start.18 = (f32[256,128]{1,0:T(8,128)S(1)}, f32[256,128]{1,0:T(8,128)S(1)}, u32[]{:S(2)}, u32[]{:S(2)}) collective-permute-start(f32[256,128]{1,0:T(8,128)S(1)} %get-tuple-element.158), channel_id=1, source_target_pairs={{0,24},{4,28},{8,0},{12,4},{16,8},{20,12},{24,16},{28,20},{32,56},... | collective-permute-start | bytes 393224 | tf_op jit(solution)/shard_map/ppermute | solution.py:516
  61.3 8.3 %collective-permute-start.21 = (f32[256,128]{1,0:T(8,128)S(1)}, f32[256,128]{1,0:T(8,128)S(1)}, u32[]{:S(2)}, u32[]{:S(2)}) collective-permute-start(f32[256,128]{1,0:T(8,128)S(1)} %line.3), channel_id=1, source_target_pairs={{0,32},{4,36},{8,40},{12,44},{16,48},{20,52},{24,56},{28,60},{32,6... | collective-permute-start | bytes 393224 | tf_op jit(solution)/shard_map/ppermute | solution.py:527
  61.6 8.0 %collective-permute-start.20 = (f32[256,128]{1,0:T(8,128)S(1)}, f32[256,128]{1,0:T(8,128)S(1)}, u32[]{:S(2)}, u32[]{:S(2)}) collective-permute-start(f32[256,128]{1,0:T(8,128)S(1)} %line.3), channel_id=1, source_target_pairs={{0,64},{4,68},{8,72},{12,76},{16,80},{20,84},{24,88},{28,92},{32,9... | collective-permute-start | bytes 393224 | tf_op jit(solution)/shard_map/ppermute | solution.py:527
  63.9 5.7 %collective-permute-start.19 = (f32[256,128]{1,0:T(8,128)S(1)}, f32[256,128]{1,0:T(8,128)S(1)}, u32[]{:S(2)}, u32[]{:S(2)}) collective-permute-start(f32[256,128]{1,0:T(8,128)S(1)} %line.3), channel_id=1, source_target_pairs={{0,96},{4,100},{8,104},{12,108},{16,112},{20,116},{24,120},{28,124... | collective-permute-start | bytes 393224 | tf_op jit(solution)/shard_map/ppermute | solution.py:527
  69.8 9.2 %collective-permute-start.22 = (f32[256,128]{1,0:T(8,128)S(1)}, f32[256,128]{1,0:T(8,128)S(1)}, u32[]{:S(2)}, u32[]{:S(2)}) collective-permute-start(f32[256,128]{1,0:T(8,128)S(1)} %get-tuple-element.161), channel_id=1, source_target_pairs={{0,8},{4,12},{8,16},{12,20},{16,24},{20,28},{24,0},{28,4},{32,40},... | collective-permute-start | bytes 393224 | tf_op jit(solution)/shard_map/ppermute | solution.py:516
  72.3 6.7 %collective-permute-start.23 = (f32[256,128]{1,0:T(8,128)S(1)}, f32[256,128]{1,0:T(8,128)S(1)}, u32[]{:S(2)}, u32[]{:S(2)}) collective-permute-start(f32[256,128]{1,0:T(8,128)S(1)} %get-tuple-element.163), channel_id=1, source_target_pairs={{0,16},{4,20},{8,24},{12,28},{16,0},{20,4},{24,8},{28,12},{32,48},... | collective-permute-start | bytes 393224 | tf_op jit(solution)/shard_map/ppermute | solution.py:516
  73.9 5.1 %collective-permute-start.24 = (f32[256,128]{1,0:T(8,128)S(1)}, f32[256,128]{1,0:T(8,128)S(1)}, u32[]{:S(2)}, u32[]{:S(2)}) collective-permute-start(f32[256,128]{1,0:T(8,128)S(1)} %get-tuple-element.164), channel_id=1, source_target_pairs={{0,24},{4,28},{8,0},{12,4},{16,8},{20,12},{24,16},{28,20},{32,56},... | collective-permute-start | bytes 393224 | tf_op jit(solution)/shard_map/ppermute | solution.py:516
  79.1 4.1 %collective-permute-start.25 = (f32[1024,128]{1,0:T(8,128)S(1)}, f32[1024,128]{1,0:T(8,128)S(1)}, u32[]{:S(2)}, u32[]{:S(2)}) collective-permute-start(f32[1024,128]{1,0:T(8,128)S(1)} %get-tuple-element.165), channel_id=1, source_target_pairs={{0,4},{4,0},{8,12},{12,8},{16,20},{20,16},{24,28},{28,24},{32,36},... | collective-permute-start | bytes 1572872 | tf_op jit(solution)/shard_map/ppermute | solution.py:532
